TPU v7x, 512 devices: a whole 4x8x8 slice. The times are simulated.
512 devices in a mesh: dp: 32 (over x_hi, z, core), mp: 16 (over x_lo, y).
Axes of the slice: x: 4 (x_hi: 2, x_lo: 2; x = x_hi * 2 + x_lo), y: 8, z: 8, core: 2. Of those that a mesh axis runs over, the one named last changes fastest.
Arguments:
- activations: bfloat16 [16384, 3072], P('dp'), may hold values from -48 to 48
- output_grad: bfloat16 [16384, 12288], P('dp', 'mp'), may hold values from -48 to 48
- weight_grad: bfloat16 [3072, 12288], P('dp', 'mp'), may hold values from -4 to 4
- input_basis: bfloat16 [3072, 3072], P(None, 'dp'), may hold values from -0.109375 to 0.109375
- input_eigen: float32 [3072], P('dp'), may hold values from 0.1 to 3
- output_basis: bfloat16 [16, 768, 768], P('mp', 'dp'), may hold values from -0.21875 to 0.21875
- output_eigen: float32 [16, 768], P('mp'), may hold values from 0.1 to 3
- input_factor: float32 [3072, 3072], P('mp', 'dp'), may hold values from -0.06 to 5
- output_factor: float32 [16, 768, 768], P('mp', 'dp'), may hold values from -0.06 to 5
Outputs:
- new_input_factor: float32 [3072, 3072], P('mp', 'dp')
- new_output_factor: float32 [16, 768, 768], P('mp', 'dp')
- preconditioned: bfloat16 [3072, 12288], P('dp', 'mp')
All inputs are finite; a program needn't handle non-finite values.
Results may differ from a plain program's by a relative error of at most 0.025.
Values may be sent and summed in bfloat16 or wider, within the bound.
No kernel may reach another device: no remote copies, remote signals or barrier semaphores. Data moves between devices by JAX's collectives and lax.ppermute only.
A program may use at most 64 MiB of HBM per device.

v0:
```python
import jax
import jax.numpy as jnp
from jax import lax
from jax.sharding import PartitionSpec as P

keep_rate = 0.95
damping = 0.03


def per_device(
    activations,
    output_grad,
    weight_grad,
    input_basis,
    input_eigen,
    output_basis,
    output_eigen,
    input_factor,
    output_factor,
):
    data_count = lax.axis_size("dp")
    model_count = lax.axis_size("mp")
    data_index = lax.axis_index("dp")
    model_index = lax.axis_index("mp")
    feature_count = activations.shape[1]
    hidden_count = output_grad.shape[1]
    block_width = feature_count // model_count
    column_width = feature_count // data_count
    token_total = activations.shape[0] * data_count
    selected = lax.dynamic_slice_in_dim(activations, model_index * block_width, block_width, 1)
    input_term = lax.dot_general(
        selected, activations, (((0,), (0,)), ((), ())), preferred_element_type=jnp.float32
    )
    output_term = lax.dot_general(
        output_grad, output_grad, (((0,), (0,)), ((), ())), preferred_element_type=jnp.float32
    )[None]
    input_whole, output_whole = (
        lax.psum(input_term.astype(jnp.bfloat16), "dp").astype(jnp.float32),
        lax.psum(output_term.astype(jnp.bfloat16), "dp").astype(jnp.float32),
    )
    input_sum = lax.dynamic_slice_in_dim(input_whole, data_index * column_width, column_width, 1)
    share_rows = hidden_count // data_count
    output_sum = lax.dynamic_slice_in_dim(output_whole, data_index * share_rows, share_rows, 1)
    new_input = keep_rate * input_factor + (1.0 - keep_rate) * (input_sum / token_total)
    new_output = keep_rate * output_factor + (1.0 - keep_rate) * (output_sum / token_total)
    columns = input_basis
    left_part = lax.dot_general(
        columns,
        lax.all_gather(weight_grad, "dp", axis=0, tiled=True),
        (((0,), (0,)), ((), ())),
        preferred_element_type=jnp.float32,
    ).astype(jnp.bfloat16)
    block_full = lax.all_gather(output_basis, "dp", axis=1, tiled=True)[0]
    rotated = jnp.dot(left_part, block_full, preferred_element_type=jnp.float32)
    denominator = input_eigen[:, None] * output_eigen[0][None, :] + damping
    scaled = (rotated / denominator).astype(jnp.bfloat16)
    back_part = lax.dot_general(
        scaled, block_full, (((1,), (1,)), ((), ())), preferred_element_type=jnp.float32
    ).astype(jnp.bfloat16)
    basis_slab = lax.all_to_all(input_basis, "dp", split_axis=0, concat_axis=1, tiled=True)
    columns = basis_slab
    result = jnp.dot(
        columns,
        lax.all_gather(back_part, "dp", axis=0, tiled=True),
        preferred_element_type=jnp.float32,
    ).astype(jnp.bfloat16)
    return (new_input, new_output, result)


def solution(mesh):
    placed = (
        P("dp", None),
        P("dp", "mp"),
        P("dp", "mp"),
        P(None, "dp"),
        P("dp"),
        P("mp", "dp", None),
        P("mp", None),
        P("mp", "dp"),
        P("mp", "dp", None),
    )
    return jax.shard_map(
        per_device,
        mesh=mesh,
        in_specs=placed,
        out_specs=(P("mp", "dp"), P("mp", "dp", None), P("dp", "mp")),
        check_vma=False,
    )
```

profile of v0, /device:TPU:1, one launch (start us, length us, event | category | flops | bytes accessed | tf_op | source)
XLA Modules:
  0.0 586.9 jit_solution(13267550326581278079)
XLA Ops:
  7.2 0.0 all-gather.4.cloned.1.call-start
  7.2 0.7 all-gather.4.cloned.1.call-update
  7.9 0.0 all-gather.6.cloned.1.call-start
  8.0 0.7 all-gather.6.cloned.1.call-update
  8.7 0.0 all-reduce.3.cloned.1.call-start
  8.7 3.4 fusion
  12.1 1.9 convolution_convert_fusion
  14.1 0.0 all-reduce.3.cloned.1.call-update
  14.1 0.0 all-gather.8.cloned.1.call-start
  14.2 98.1 %all-gather.4.cloned.1.call-done = bf16[3072,768]{1,0:T(8,128)(2,1)} async-done(((bf16[96,768]{1,0:T(8,128)(2,1)}), bf16[3072,768]{1,0:T(8,128)(2,1)}) %all-gather.4.cloned.1.call-update) | async-done | bytes 4718608 | tf_op jit(solution)/shard_map/all_gather | solution.py:49
  112.3 3.4 convolution_convert_fusion.3
  115.7 80.1 %all-gather.6.cloned.1.call-done = bf16[1,768,768]{2,1,0:T(8,128)(2,1)} async-done(((bf16[1,24,768]{2,1,0:T(8,128)(2,1)}), bf16[1,768,768]{2,1,0:T(8,128)(2,1)}) %all-gather.6.cloned.1.call-update) | async-done | bytes 1179664 | tf_op jit(solution)/shard_map/all_gather | solution.py:53
  195.8 3.1 fusion.8
  198.8 0.0 all-gather.8.cloned.1.call-update
  198.8 2.2 copy.13
  201.1 5.4 all-to-all-start
  206.5 25.9 %all-to-all-done = bf16[32,96,96]{2,1,0:T(8,128)(2,1)} async-done(((bf16[32,96,96]{2,1,0:T(8,128)(2,1)}), bf16[32,96,96]{2,1,0:T(8,128)(2,1)}, u32[]{:S(2)}, u32[]{:S(2)}) %all-to-all-start) | async-done | bytes 589856 | tf_op jit(solution)/shard_map/all_to_all | solution.py:60
  232.4 2.3 copy.14
  234.7 2.8 all_to_all.17
  237.6 241.3 %all-reduce.3.cloned.1.call-done = (bf16[192,3072]{1,0:T(8,128)(2,1)}, bf16[1,768,768]{2,1,0:T(8,128)(2,1)}) async-done(((bf16[192,3072]{1,0:T(8,128)(2,1)}, bf16[1,768,768]{2,1,0:T(8,128)(2,1)}), (bf16[192,3072]{1,0:T(8,128)(2,1)}, bf16[1,768,768]{2,1,0:T(8,128)(2,1)})) %all-reduce.3.cloned.1.call-update) | async-done | bytes 2359312 | tf_op jit(solution)/shard_map/psum | solution.py:38
  478.9 1.4 multiply_add_fusion.1
  480.3 1.6 multiply_add_fusion
  481.9 94.4 %all-gather.8.cloned.1.call-done = bf16[3072,768]{1,0:T(8,128)(2,1)} async-done(((bf16[96,768]{1,0:T(8,128)(2,1)}), bf16[3072,768]{1,0:T(8,128)(2,1)}) %all-gather.8.cloned.1.call-update) | async-done | bytes 4718608 | tf_op jit(solution)/shard_map/all_gather | solution.py:64
  576.3 4.1 fusion.16
  (11 shorter events, 0.0 us)
Async XLA Ops:
  7.2 5.0 copy-start
  7.2 105.1 %all-gather.4.cloned.1.call-start = ((), (), s32[]{:S(2)}) async-start(), calls=%async_computation.1 | async-start | bytes 4866048 | tf_op jit(solution)/shard_map/all_gather | solution.py:49
  7.9 187.9 %all-gather.6.cloned.1.call-start = ((), (), s32[]{:S(2)}) async-start(), calls=%async_computation.2 | async-start | bytes 1216512 | tf_op jit(solution)/shard_map/all_gather | solution.py:53
  8.7 470.2 %all-reduce.3.cloned.1.call-start = ((), (), s32[]{:S(2)}) async-start(), calls=%async_computation.4 | async-start | bytes 4718592 | tf_op jit(solution)/shard_map/psum | solution.py:38
  12.1 2.0 copy-start.3
  14.1 562.2 %all-gather.8.cloned.1.call-start = ((), (), s32[]{:S(2)}) async-start(), calls=%async_computation.3 | async-start | bytes 4866048 | tf_op jit(solution)/shard_map/all_gather | solution.py:64
  14.2 181.6 %copy-start.4 = (f32[96]{0:T(128)S(1)}, f32[96]{0:T(128)}, u32[]{:S(2)}) copy-start(f32[96]{0:T(128)} %param.13) | copy-start | bytes 1156
  201.1 277.8 %copy-start.2 = (f32[1,24,768]{2,1,0:T(8,128)S(1)}, f32[1,24,768]{2,1,0:T(8,128)}, u32[]{:S(2)}) copy-start(f32[1,24,768]{2,1,0:T(8,128)} %param.17) | copy-start | bytes 221188
  201.1 279.2 %copy-start.1 = (f32[192,96]{1,0:T(8,128)S(1)}, f32[192,96]{1,0:T(8,128)}, u32[]{:S(2)}) copy-start(f32[192,96]{1,0:T(8,128)} %param.16) | copy-start | bytes 221188
  201.1 31.3 %all-to-all-start = ((bf16[32,96,96]{2,1,0:T(8,128)(2,1)}), bf16[32,96,96]{2,1,0:T(8,128)(2,1)}, u32[]{:S(2)}, u32[]{:S(2)}) async-start(bf16[32,96,96]{2,1,0:T(8,128)(2,1)} %bitcast.27), calls=%async_computation | async-start | bytes 1572864 | tf_op jit(solution)/shard_map/all_to_all | solution.py:60
Sparse Core Ops, SparseCore 0:
  11.4 100.8 all-gather.3
  115.6 80.1 all-gather.5
  198.7 280.0 all-reduce.2
  482.7 93.5 all-gather.7
where the time goes:
time: 587 us
  waiting for transfers between devices  541 us (92%)
  matrix products  15.9 us (3%)
  between operations  13.8 us (2%)
  local copies, waits for them, and re-layouts  7.42 us (1%)
    psum x1, waiting for transfers between devices, per_device(): lax.psum(input_term.astype(jnp.bfloat16), 'dp').astype(jnp.float32)  241 us
    all_gather x1, waiting for transfers between devices, per_device(): lax.all_gather(weight_grad, 'dp', axis=0, tiled=True)  98.1 us
    all_gather x1, waiting for transfers between devices, per_device(): lax.all_gather(back_part, 'dp', axis=0, tiled=True)  94.4 us
    all_gather x1, waiting for transfers between devices, per_device(): block_full = lax.all_gather(output_basis, 'dp', axis=1, tiled=True)[0]  80.1 us
    all_to_all x1, waiting for transfers between devices, per_device(): lax.all_to_all(input_basis, 'dp', split_axis=0, concat_axis=1, tiled=True)  25.9 us
  transfers between devices with their start and end apart: 5, of which 5 were waited for; matrix products, arithmetic and copies ran while one was open for 3% of the time, Pallas kernels for 0%

commit v1 on v0

v1 whole, which is shorter than its diff:
```python
import jax
import jax.numpy as jnp
from jax import lax
from jax.sharding import Mesh, PartitionSpec as P

keep_rate = 0.95
damping = 0.03
swap = ((0, 1), (1, 0))
DP = ("xh", "z", "c")
MP = ("xl", "y")


def dot(a, b, da, db):
    return lax.dot_general(a, b, (((da,), (db,)), ((), ())), preferred_element_type=jnp.float32)


def pick(a, index, axis):
    return lax.dynamic_index_in_dim(a, index, axis, keepdims=False)


def per_device(
    activations,
    output_grad,
    weight_grad,
    input_basis,
    input_eigen,
    output_basis,
    output_eigen,
    input_factor,
    output_factor,
):
    bf16, f32 = jnp.bfloat16, jnp.float32
    xh, c = lax.axis_index("xh"), lax.axis_index("c")
    m = lax.axis_index(MP)
    tokens = activations.shape[0] * 32

    halves = weight_grad.reshape(96, 2, 384).transpose(1, 0, 2)
    send = jnp.broadcast_to(halves[None], (8, 2, 96, 384)).reshape(16, 96, 384)
    grad_rows = lax.all_to_all(send, ("z", "c"), 0, 0).reshape(1536, 384)

    basis_out = output_basis[0]
    basis_far = lax.ppermute(basis_out, "xh", swap)
    basis_pair = jnp.where(xh == 0, jnp.stack([basis_out, basis_far]), jnp.stack([basis_far, basis_out]))
    basis_all = lax.all_gather(basis_pair, ("z", "c"), axis=0)
    v_rel = jnp.concatenate([pick(basis_all, c, 1), pick(basis_all, 1 - c, 1)], axis=0).reshape(768, 768)

    ut = input_basis.T
    ut_mine = lax.dynamic_slice_in_dim(ut, xh * 1536, 1536, 1)
    ut_other = lax.dynamic_slice_in_dim(ut, (1 - xh) * 1536, 1536, 1)
    ut_far = lax.ppermute(ut_other, "xh", swap)
    mine = jnp.stack([ut_mine, ut_far])
    theirs = lax.ppermute(mine, "c", swap)
    first = jnp.stack([mine, theirs], axis=1).reshape(384, 1536)

    selected = lax.dynamic_slice_in_dim(activations, m * 192, 192, 1)
    input_term = dot(activations, selected, 0, 0).astype(bf16)
    output_term = dot(output_grad, output_grad, 0, 0).astype(bf16)
    in_parts = input_term.reshape(2, 8, 2, 96, 192).transpose(2, 1, 3, 0, 4).reshape(2, 8, 96, 384)
    out_parts = output_term.reshape(2, 8, 2, 24, 2, 384).transpose(2, 1, 4, 0, 3, 5).reshape(2, 8, 96, 384)
    parts = jnp.concatenate([in_parts, out_parts], axis=2)
    came = lax.ppermute(pick(parts, 1 - c, 0), "c", swap)
    pair = (pick(parts, c, 0).astype(f32) + came.astype(f32)).astype(bf16)
    summed = lax.psum_scatter(pair, "z", scatter_dimension=0, tiled=False)
    in_sum = summed[:96].reshape(96, 2, 192)
    out_sum = summed[96:].reshape(2, 2, 24, 384)
    in_came = lax.ppermute(pick(in_sum, 1 - xh, 1), "xh", swap)
    out_came = lax.ppermute(pick(out_sum, 1 - xh, 1), "xh", swap)
    in_total = pick(in_sum, xh, 1).astype(f32) + in_came.astype(f32)
    out_total = pick(out_sum, xh, 1).astype(f32) + out_came.astype(f32)
    new_input = keep_rate * input_factor + (1.0 - keep_rate) * (in_total.T / tokens)
    new_output = keep_rate * output_factor + (1.0 - keep_rate) * (
        out_total.transpose(1, 0, 2).reshape(1, 24, 768) / tokens
    )

    left_part = dot(first, grad_rows, 1, 0).reshape(2, 2, 96, 384)
    left_came = lax.ppermute(left_part[1].astype(bf16), "xh", swap)
    left_two = (left_part[0] + left_came.astype(f32)).astype(bf16)
    left_far = lax.ppermute(left_two[1], "c", swap)
    left = jnp.concatenate([left_two[0], left_far], axis=1)
    rotated = dot(left, v_rel, 1, 0)
    denominator = input_eigen[:, None] * output_eigen[0][None, :] + damping
    scaled = (rotated / denominator).astype(bf16)
    back = dot(scaled, v_rel, 1, 1).astype(bf16)

    rel = jnp.stack([ut_mine, ut_other], axis=1).reshape(96, 2, 8, 192).transpose(2, 0, 1, 3).reshape(8, 96, 384)
    slab = lax.all_to_all(rel, "z", 0, 0)
    slab_far = lax.ppermute(slab, "c", swap)
    second = jnp.where(
        c == 0, jnp.stack([slab, slab_far], axis=1), jnp.stack([slab_far, slab], axis=1)
    ).reshape(1536, 384)

    near, far = back[:, :384], back[:, 384:]
    back_halves = jnp.where(c == 0, jnp.stack([near, far]), jnp.stack([far, near]))
    send = jnp.broadcast_to(back_halves[None], (8, 2, 96, 384)).reshape(16, 96, 384)
    back_rows = lax.all_to_all(send, ("z", "c"), 0, 0).reshape(1536, 384)
    out_part = dot(second, back_rows, 0, 0).reshape(2, 192, 384)
    out_far = lax.ppermute(out_part[1].astype(bf16), "xh", swap)
    out_two = (out_part[0] + out_far.astype(f32)).astype(bf16).reshape(2, 96, 384)
    result = lax.all_to_all(out_two, "c", 0, 0).transpose(1, 0, 2).reshape(96, 768)
    return (new_input, new_output, result)


def solution(mesh):
    fine = Mesh(mesh.devices.reshape(2, 8, 2, 2, 8), DP + MP)
    placed = (
        P(DP, None),
        P(DP, MP),
        P(DP, MP),
        P(None, DP),
        P(DP),
        P(MP, DP, None),
        P(MP, None),
        P(MP, DP),
        P(MP, DP, None),
    )
    return jax.shard_map(
        per_device,
        mesh=fine,
        in_specs=placed,
        out_specs=(P(MP, DP), P(MP, DP, None), P(DP, MP)),
        check_vma=False,
    )
```

time: 587 us -> 202 us (0.34)
  the two profiles are of different devices: /device:TPU:1 before, /device:TPU:33 now
where the time goes in v1:
time: 202 us; the launch traced here: 201 us
  starting transfers between devices  55.4 us (27%)
  local copies, waits for them, and re-layouts  43.7 us (22%)
  waiting for transfers between devices  42.2 us (21%)
  other arithmetic  20 us (10%)
  between operations  15.9 us (8%)
  matrix products  12.5 us (6%)
  blocking collectives  11 us (5%)
    reduce_scatter x1, waiting for transfers between devices, per_device(): summed = lax.psum_scatter(pair, 'z', scatter_dimension=0, tiled=False)  32.2 us
    reshape x3, local copies, waits for them, and re-layouts, per_device(): input_term.reshape(2, 8, 2, 96, 192).transpose(2, 1, 3, 0, 4)  16.9 us
    dot_general x5, matrix products, dot(): lax.dot_general(a, b, (((da,), (db,)), ((), ())), preferred_element_type=...  12.5 us
    all_to_all x1, starting transfers between devices, per_device(): grad_rows = lax.all_to_all(send, ('z', 'c'), 0, 0).reshape(1536, 384)  11.1 us
    all_to_all x1, blocking collectives, per_device(): lax.all_to_all(out_two, 'c', 0, 0).transpose(1, 0, 2).reshape(96, 768)  11 us
    all_to_all x1, starting transfers between devices, per_device(): back_rows = lax.all_to_all(send, ('z', 'c'), 0, 0).reshape(1536, 384)  7.14 us
    all_to_all x1, starting transfers between devices, per_device(): slab = lax.all_to_all(rel, 'z', 0, 0)  6.74 us
    reshape x2, local copies, waits for them, and re-layouts, per_device(): output_term.reshape(2, 8, 2, 24, 2, 384).transpose(2, 1, 4, 0, 3, 5)  6.04 us
  transfers between devices with their start and end apart: 15, of which 4 were waited for; matrix products, arithmetic and copies ran while one was open for 35% of the time, Pallas kernels for 0%

profile of v1, /device:TPU:33, one launch (start us, length us, event | category | flops | bytes accessed | tf_op | source)
XLA Modules:
  0.0 200.7 jit_solution(7173359144068760835)
XLA Ops:
  10.3 11.1 %all-to-all-start.1 = ((bf16[16,96,384]{2,1,0:T(8,128)(2,1)}), bf16[16,96,384]{2,1,0:T(8,128)(2,1)}, u32[]{:S(2)}, u32[]{:S(2)}) async-start(bf16[16,96,384]{2,1,0:T(8,128)(2,1)} %bitcast.89), calls=%async_computation.2 | async-start | bytes 2359296 | tf_op jit(solution)/shard_map/all_to_all | solution.py:39
  21.5 4.7 %collective-permute-start.8 = (bf16[24,768]{1,0:T(8,128)(2,1)S(1)}, bf16[24,768]{1,0:T(8,128)(2,1)S(1)}, u32[]{:S(2)}, u32[]{:S(2)}) collective-permute-start(bf16[24,768]{1,0:T(8,128)(2,1)S(1)} %bitcast.101), channel_id=1, source_target_pairs={{0,256},{256,0},{1,257},{257,1},{2,258},{258,2},{3,259},{259,3},{4... | collective-permute-start | bytes 110600 | tf_op jit(solution)/shard_map/ppermute | solution.py:42
  32.9 6.2 %reshape.200 = bf16[2,8,2,96,192]{3,2,1,0,4:T(2,128)(2,1)} reshape(bf16[3072,192]{0,1:T(8,128)(2,1)} %fusion) | data formatting | bytes 2359296 | tf_op jit(solution)/shard_map/reshape | solution.py:58
  39.1 6.2 %copy.34 = bf16[2,8,2,96,192]{4,0,3,1,2:T(2,128)(2,1)} copy(bf16[2,8,2,96,192]{3,2,1,0,4:T(2,128)(2,1)} %reshape.200) | data formatting | bytes 2359296 | tf_op jit(solution)/shard_map/reshape | solution.py:58
  45.3 4.5 %reshape.201 = bf16[2,8,96,384]{3,2,1,0:T(8,128)(2,1)} reshape(bf16[2,8,96,2,192]{4,3,2,1,0:T(2,128)(2,1)} %bitcast.88) | data formatting | bytes 2359296 | tf_op jit(solution)/shard_map/reshape | solution.py:58
  49.8 3.2 %convolution_convert_fusion.1 = bf16[768,768]{1,0:T(8,128)(2,1)} fusion(bf16[512,768]{1,0:T(8,128)(2,1)} %param.10), kind=kOutput, calls=%fused_computation.8 | convolution fusion | flops 604569600 | bytes 1966080 | tf_op jit(solution)/shard_map/dot_general | solution.py:14
  53.0 3.6 %reshape.202 = bf16[2,8,2,24,2,384]{5,4,3,2,1,0:T(2,128)(2,1)} reshape(bf16[768,768]{1,0:T(8,128)(2,1)} %convolution_convert_fusion.1) | data formatting | bytes 2359296 | tf_op jit(solution)/shard_map/reshape | solution.py:59
  56.6 2.5 %copy.35 = bf16[2,8,2,24,2,384]{5,3,0,4,1,2:T(8,128)(2,1)} copy(bf16[2,8,2,24,2,384]{5,4,3,2,1,0:T(2,128)(2,1)} %reshape.202) | data formatting | bytes 2359296 | tf_op jit(solution)/shard_map/reshape | solution.py:59
  59.1 2.5 %fusion.3 = bf16[8,192,384]{2,1,0:T(8,128)(2,1)} fusion(s32[]{:T(128)S(6)} %select_n.76, bf16[2,8,96,384]{3,2,1,0:T(8,128)(2,1)} %reshape.201, bf16[2,8,96,384]{3,2,1,0:T(8,128)(2,1)} %bitcast.86), kind=kLoop, calls=%fused_computation.10 | loop fusion | flops 2359296 | bytes 3538948 | tf_op jit(solution)/shard_map/jit(dynamic_index_in_dim)/squeeze | solution.py:18
  61.6 2.6 %collective-permute-start = (bf16[8,192,384]{2,1,0:T(8,128)(2,1)}, bf16[8,192,384]{2,1,0:T(8,128)(2,1)}, u32[]{:S(2)}, u32[]{:S(2)}) collective-permute-start(bf16[8,192,384]{2,1,0:T(8,128)(2,1)} %fusion.3), channel_id=1, source_target_pairs={{0,16},{16,0},{1,17},{17,1},{2,18},{18,2},{3,19},{19,3},{4,20},{20... | collective-permute-start | bytes 3538952 | tf_op jit(solution)/shard_map/ppermute | solution.py:61
  73.6 2.8 %maximum_bitcast_fusion = bf16[8,96,2,192]{3,2,1,0:T(2,128)(2,1)} fusion(bf16[96,1,8,192]{3,1,0,2:T(2,128)(2,1)S(1)} %copy-done.3, bf16[96,1,8,192]{3,1,0,2:T(2,128)(2,1)S(1)} %copy.39), kind=kLoop, calls=%fused_computation.19 | loop fusion | flops 1179648 | bytes 1179648 | tf_op jit(solution)/shard_map/transpose | solution.py:85
  76.4 3.0 %reshape.206 = bf16[8,96,384]{2,1,0:T(8,128)(2,1)} reshape(bf16[8,96,2,192]{3,2,1,0:T(2,128)(2,1)} %maximum_bitcast_fusion) | data formatting | bytes 1179648 | tf_op jit(solution)/shard_map/reshape | solution.py:85
  81.9 6.7 %all-to-all-start = ((bf16[8,96,384]{2,1,0:T(8,128)(2,1)}), bf16[8,96,384]{2,1,0:T(8,128)(2,1)}, u32[]{:S(2)}, u32[]{:S(2)}) async-start(bf16[8,96,384]{2,1,0:T(8,128)(2,1)} %reshape.206), calls=%async_computation.1 | async-start | bytes 1179648 | tf_op jit(solution)/shard_map/all_to_all | solution.py:86
  88.7 2.5 %fusion.31 = f32[384,384]{1,0:T(8,128)S(1)} fusion(bf16[384,1536]{1,0:T(8,128)(2,1)} %bitcast.92, bf16[1536,384]{1,0:T(8,128)(2,1)} %bitcast.27), kind=kOutput, calls=%fused_computation.62 | convolution fusion | flops 452984832 | bytes 2949120 | tf_op jit(solution)/shard_map/dot_general | solution.py:14
  92.8 4.6 %collective-permute-start.6 = (bf16[2,96,384]{2,1,0:T(8,128)(2,1)}, bf16[2,96,384]{2,1,0:T(8,128)(2,1)}, u32[]{:S(2)}, u32[]{:S(2)}) collective-permute-start(bf16[2,96,384]{2,1,0:T(8,128)(2,1)} %bitcast.29), channel_id=1, source_target_pairs={{0,256},{256,0},{1,257},{257,1},{2,258},{258,2},{3,259},{259,3},{4... | collective-permute-start | bytes 442376 | tf_op jit(solution)/shard_map/ppermute | solution.py:76
  97.4 2.6 %fusion.1 = bf16[8,192,384]{2,1,0:T(8,128)(2,1)} fusion(bf16[8,192,384]{2,1,0:T(8,128)(2,1)} %collective-permute-done, s32[]{:T(128)S(6)} %select_n.75, bf16[2,8,96,384]{3,2,1,0:T(8,128)(2,1)S(1)} %copy-done.2, bf16[2,8,96,384]{3,2,1,0:T(8,128)(2,1)S(1)} %bitcast.87), kind=kLoop, calls=%fused_computation.7 | loop fusion | flops 4718592 | bytes 4718596 | tf_op jit(solution)/shard_map/convert_element_type | solution.py:62
  102.5 3.1 %collective-permute-start.7 = (bf16[96,384]{1,0:T(8,128)(2,1)S(1)}, bf16[96,384]{1,0:T(8,128)(2,1)S(1)}, u32[]{:S(2)}, u32[]{:S(2)}) collective-permute-start(bf16[96,384]{1,0:T(8,128)(2,1)S(1)} %get-tuple-element.13), channel_id=1, source_target_pairs={{0,16},{16,0},{1,17},{17,1},{2,18},{18,2},{3,19},{19,3},{4,20},{20... | collective-permute-start | bytes 221192 | tf_op jit(solution)/shard_map/ppermute | solution.py:78
  110.4 7.1 %all-to-all-start.2 = ((bf16[16,96,384]{2,1,0:T(8,128)(2,1)}), bf16[16,96,384]{2,1,0:T(8,128)(2,1)}, u32[]{:S(2)}, u32[]{:S(2)}) async-start(bf16[16,96,384]{2,1,0:T(8,128)(2,1)} %bitcast.90), calls=%async_computation.3 | async-start | bytes 2359296 | tf_op jit(solution)/shard_map/all_to_all | solution.py:95
  124.7 32.2 %reduce-scatter.2.cloned.1.call-done = bf16[1,192,384]{2,1,0:T(8,128)(2,1)} async-done(((bf16[8,192,384]{2,1,0:T(8,128)(2,1)}), bf16[1,192,384]{2,1,0:T(8,128)(2,1)}) %reduce-scatter.2.cloned.1.call-update) | async-done | bytes 147472 | tf_op jit(solution)/shard_map/reduce_scatter | solution.py:63
  157.9 4.6 %collective-permute-start.2 = (bf16[2,24,384]{2,1,0:T(8,128)(2,1)S(1)}, bf16[2,24,384]{2,1,0:T(8,128)(2,1)}, u32[]{:S(2)}, u32[]{:S(2)}) collective-permute-start(bf16[2,24,384]{2,1,0:T(8,128)(2,1)S(1)} %dynamic-slice_bitcast_fusion.5), channel_id=1, source_target_pairs={{0,256},{256,0},{1,257},{257,1},{2,258},{258,2},{3,259},{259,3},{4... | collective-permute-start | bytes 110600 | tf_op jit(solution)/shard_map/ppermute | solution.py:67
  166.8 3.3 %collective-permute-done.1 = bf16[96,192]{0,1:T(8,128)(2,1)S(1)} collective-permute-done((bf16[96,192]{0,1:T(8,128)(2,1)}, bf16[96,192]{0,1:T(8,128)(2,1)S(1)}, u32[]{:S(2)}, u32[]{:S(2)}) %collective-permute-start.1) | collective-permute-done | bytes 36896 | tf_op jit(solution)/shard_map/ppermute | solution.py:66
  171.6 2.4 %fusion.32 = f32[384,384]{1,0:T(8,128)S(1)} fusion(bf16[1536,384]{1,0:T(8,128)(2,1)} %bitcast.91, bf16[1536,384]{1,0:T(8,128)(2,1)} %bitcast.41), kind=kOutput, calls=%fused_computation.63 | convolution fusion | flops 452984832 | bytes 2949120 | tf_op jit(solution)/shard_map/dot_general | solution.py:14
  177.0 4.5 %collective-permute-done.9 = bf16[192,384]{1,0:T(8,128)(2,1)S(1)} collective-permute-done((bf16[192,384]{1,0:T(8,128)(2,1)S(1)}, bf16[192,384]{1,0:T(8,128)(2,1)S(1)}, u32[]{:S(2)}, u32[]{:S(2)}) %collective-permute-start.9) | collective-permute-done | bytes 147488 | tf_op jit(solution)/shard_map/ppermute | solution.py:97
  181.6 11.0 %all_to_all.20 = bf16[2,96,384]{2,1,0:T(8,128)(2,1)S(1)} all-to-all(bf16[2,96,384]{2,1,0:T(8,128)(2,1)S(1)} %bitcast.97), channel_id=1, replica_groups=mesh['xh'=2,'z'=8,'c'=2,'xl'=2,'y'=8] {'c'}, dimensions={0} | all-to-all | bytes 294912 | tf_op jit(solution)/shard_map/all_to_all | solution.py:99
  (79 shorter events, 47.1 us)
Async XLA Ops:
  8.0 23.0 %copy-start = (bf16[512,3072]{1,0:T(8,128)(2,1)S(1)}, bf16[512,3072]{1,0:T(8,128)(2,1)}, u32[]{:S(2)}) copy-start(bf16[512,3072]{1,0:T(8,128)(2,1)} %param.9) | copy-start | bytes 9437188
  10.3 11.2 %copy-start.6 = (bf16[1,24,768]{2,1,0:T(8,128)(2,1)S(1)}, bf16[1,24,768]{2,1,0:T(8,128)(2,1)}, u32[]{:S(2)}) copy-start(bf16[1,24,768]{2,1,0:T(8,128)(2,1)} %param.14) | copy-start | bytes 110596
  10.3 71.6 %all-to-all-start.1 = ((bf16[16,96,384]{2,1,0:T(8,128)(2,1)}), bf16[16,96,384]{2,1,0:T(8,128)(2,1)}, u32[]{:S(2)}, u32[]{:S(2)}) async-start(bf16[16,96,384]{2,1,0:T(8,128)(2,1)} %bitcast.89), calls=%async_computation.2 | async-start | bytes 2359296 | tf_op jit(solution)/shard_map/all_to_all | solution.py:39
  21.5 78.7 %all-gather.2.cloned.1.call-start = ((), (), s32[]{:S(2)}) async-start(), calls=%async_computation.6 | async-start | bytes 1253376 | tf_op jit(solution)/shard_map/all_gather | solution.py:44
  21.5 8.8 %collective-permute-start.8 = (bf16[24,768]{1,0:T(8,128)(2,1)S(1)}, bf16[24,768]{1,0:T(8,128)(2,1)S(1)}, u32[]{:S(2)}, u32[]{:S(2)}) collective-permute-start(bf16[24,768]{1,0:T(8,128)(2,1)S(1)} %bitcast.101), channel_id=1, source_target_pairs={{0,256},{256,0},{1,257},{257,1},{2,258},{258,2},{3,259},{259,3},{4... | collective-permute-start | bytes 110600 | tf_op jit(solution)/shard_map/ppermute | solution.py:42
  28.1 36.1 %collective-permute-start.4 = (bf16[96,1536]{1,0:T(8,128)(2,1)}, bf16[96,1536]{1,0:T(8,128)(2,1)}, u32[]{:S(2)}, u32[]{:S(2)}) collective-permute-start(bf16[96,1536]{1,0:T(8,128)(2,1)} %get-tuple-element.8), channel_id=1, source_target_pairs={{0,256},{256,0},{1,257},{257,1},{2,258},{258,2},{3,259},{259,3},{4... | collective-permute-start | bytes 884744 | tf_op jit(solution)/shard_map/ppermute | solution.py:50
  61.6 35.8 %collective-permute-start = (bf16[8,192,384]{2,1,0:T(8,128)(2,1)}, bf16[8,192,384]{2,1,0:T(8,128)(2,1)}, u32[]{:S(2)}, u32[]{:S(2)}) collective-permute-start(bf16[8,192,384]{2,1,0:T(8,128)(2,1)} %fusion.3), channel_id=1, source_target_pairs={{0,16},{16,0},{1,17},{17,1},{2,18},{18,2},{3,19},{19,3},{4,20},{20... | collective-permute-start | bytes 3538952 | tf_op jit(solution)/shard_map/ppermute | solution.py:61
  66.3 13.2 %collective-permute-start.5 = (bf16[2,96,1536]{2,1,0:T(8,128)(2,1)}, bf16[2,96,1536]{2,1,0:T(8,128)(2,1)}, u32[]{:S(2)}, u32[]{:S(2)}) collective-permute-start(bf16[2,96,1536]{2,1,0:T(8,128)(2,1)} %get-tuple-element.6), channel_id=1, source_target_pairs={{0,16},{16,0},{1,17},{17,1},{2,18},{18,2},{3,19},{19,3},{4,20},{20... | collective-permute-start | bytes 1769480 | tf_op jit(solution)/shard_map/ppermute | solution.py:52
  72.5 1.1 copy-start.3
  76.4 3.0 %copy-start.7 = (f32[1,768]{1,0:T(1,128)S(1)}, f32[1,768]{1,0:T(1,128)}, u32[]{:S(2)}) copy-start(f32[1,768]{1,0:T(1,128)} %param.15) | copy-start | bytes 9220
  81.9 27.3 %all-to-all-start = ((bf16[8,96,384]{2,1,0:T(8,128)(2,1)}), bf16[8,96,384]{2,1,0:T(8,128)(2,1)}, u32[]{:S(2)}, u32[]{:S(2)}) async-start(bf16[8,96,384]{2,1,0:T(8,128)(2,1)} %reshape.206), calls=%async_computation.1 | async-start | bytes 1179648 | tf_op jit(solution)/shard_map/all_to_all | solution.py:86
  88.6 68.3 %reduce-scatter.2.cloned.1.call-start = ((), (), s32[]{:S(2)}) async-start(), calls=%async_computation.5 | async-start | bytes 1327104 | tf_op jit(solution)/shard_map/reduce_scatter | solution.py:63
  88.7 8.7 %copy-start.1 = (bf16[2,8,2,24,2,384]{5,3,0,4,1,2:T(8,128)(2,1)S(1)}, bf16[2,8,2,24,2,384]{5,3,0,4,1,2:T(8,128)(2,1)}, u32[]{:S(2)}) copy-start(bf16[2,8,2,24,2,384]{5,3,0,4,1,2:T(8,128)(2,1)} %copy.35) | copy-start | bytes 3538948
  88.7 8.7 %copy-start.2 = (bf16[2,8,96,384]{3,2,1,0:T(8,128)(2,1)S(1)}, bf16[2,8,96,384]{3,2,1,0:T(8,128)(2,1)}, u32[]{:S(2)}) copy-start(bf16[2,8,96,384]{3,2,1,0:T(8,128)(2,1)} %reshape.201) | copy-start | bytes 3538948
  92.8 8.7 %collective-permute-start.6 = (bf16[2,96,384]{2,1,0:T(8,128)(2,1)}, bf16[2,96,384]{2,1,0:T(8,128)(2,1)}, u32[]{:S(2)}, u32[]{:S(2)}) collective-permute-start(bf16[2,96,384]{2,1,0:T(8,128)(2,1)} %bitcast.29), channel_id=1, source_target_pairs={{0,256},{256,0},{1,257},{257,1},{2,258},{258,2},{3,259},{259,3},{4... | collective-permute-start | bytes 442376 | tf_op jit(solution)/shard_map/ppermute | solution.py:76
  100.1 1.4 slice-start
  102.5 4.3 %collective-permute-start.7 = (bf16[96,384]{1,0:T(8,128)(2,1)S(1)}, bf16[96,384]{1,0:T(8,128)(2,1)S(1)}, u32[]{:S(2)}, u32[]{:S(2)}) collective-permute-start(bf16[96,384]{1,0:T(8,128)(2,1)S(1)} %get-tuple-element.13), channel_id=1, source_target_pairs={{0,16},{16,0},{1,17},{17,1},{2,18},{18,2},{3,19},{19,3},{4,20},{20... | collective-permute-start | bytes 221192 | tf_op jit(solution)/shard_map/ppermute | solution.py:78
  105.6 1.2 copy-start.8
  110.4 61.3 %all-to-all-start.2 = ((bf16[16,96,384]{2,1,0:T(8,128)(2,1)}), bf16[16,96,384]{2,1,0:T(8,128)(2,1)}, u32[]{:S(2)}, u32[]{:S(2)}) async-start(bf16[16,96,384]{2,1,0:T(8,128)(2,1)} %bitcast.90), calls=%async_computation.3 | async-start | bytes 2359296 | tf_op jit(solution)/shard_map/all_to_all | solution.py:95
  117.5 4.2 %collective-permute-start.3 = (bf16[8,96,384]{2,1,0:T(8,128)(2,1)}, bf16[8,96,384]{2,1,0:T(8,128)(2,1)}, u32[]{:S(2)}, u32[]{:S(2)}) collective-permute-start(bf16[8,96,384]{2,1,0:T(8,128)(2,1)} %all-to-all-done), channel_id=1, source_target_pairs={{0,16},{16,0},{1,17},{17,1},{2,18},{18,2},{3,19},{19,3},{4,20},{20... | collective-permute-start | bytes 1769480 | tf_op jit(solution)/shard_map/ppermute | solution.py:87
  157.9 8.0 %collective-permute-start.2 = (bf16[2,24,384]{2,1,0:T(8,128)(2,1)S(1)}, bf16[2,24,384]{2,1,0:T(8,128)(2,1)}, u32[]{:S(2)}, u32[]{:S(2)}) collective-permute-start(bf16[2,24,384]{2,1,0:T(8,128)(2,1)S(1)} %dynamic-slice_bitcast_fusion.5), channel_id=1, source_target_pairs={{0,256},{256,0},{1,257},{257,1},{2,258},{258,2},{3,259},{259,3},{4... | collective-permute-start | bytes 110600 | tf_op jit(solution)/shard_map/ppermute | solution.py:67
  163.5 6.5 %collective-permute-start.1 = (bf16[96,192]{0,1:T(8,128)(2,1)}, bf16[96,192]{0,1:T(8,128)(2,1)S(1)}, u32[]{:S(2)}, u32[]{:S(2)}) collective-permute-start(bf16[96,192]{0,1:T(8,128)(2,1)} %bitcast.7), channel_id=1, source_target_pairs={{0,256},{256,0},{1,257},{257,1},{2,258},{258,2},{3,259},{259,3},{4... | collective-permute-start | bytes 110600 | tf_op jit(solution)/shard_map/ppermute | solution.py:66
  171.6 4.7 %copy-start.5 = (f32[1,24,768]{2,1,0:T(8,128)S(1)}, f32[1,24,768]{2,1,0:T(8,128)}, u32[]{:S(2)}) copy-start(f32[1,24,768]{2,1,0:T(8,128)} %param.17) | copy-start | bytes 221188
  174.1 7.4 %collective-permute-start.9 = (bf16[192,384]{1,0:T(8,128)(2,1)S(1)}, bf16[192,384]{1,0:T(8,128)(2,1)S(1)}, u32[]{:S(2)}, u32[]{:S(2)}) collective-permute-start(bf16[192,384]{1,0:T(8,128)(2,1)S(1)} %slice.67), channel_id=1, source_target_pairs={{0,256},{256,0},{1,257},{257,1},{2,258},{258,2},{3,259},{259,3},{4... | collective-permute-start | bytes 442376 | tf_op jit(solution)/shard_map/ppermute | solution.py:97
  (1 other events, 0.8 us)
Sparse Core Ops, SparseCore 0:
  31.1 43.7 all-gather.1
Sparse Core Ops, SparseCore 1:
  100.2 56.7 reduce-scatter.1

commit v2 on v1

v2 whole, which is shorter than its diff:
```python
import jax
import jax.numpy as jnp
from jax import lax
from jax.experimental import pallas as pl
from jax.experimental.pallas import tpu as pltpu
from jax.sharding import Mesh, PartitionSpec as P

keep_rate = 0.95
damping = 0.03
swap = ((0, 1), (1, 0))
DP = ("xh", "z", "c")
MP = ("xl", "y")
QUAD = ("xh", "c")
bf16, f32 = jnp.bfloat16, jnp.float32


def dot(a, b, da, db):
    return lax.dot_general(a, b, (((da,), (db,)), ((), ())), preferred_element_type=f32)


def pick(a, index, axis):
    return lax.dynamic_index_in_dim(a, index, axis, keepdims=False)


def factor_kernel(core, act, sel, grad, mine, other, t_in, t_out):
    c = core[0]
    for j in range(4):
        low = act[:, j * 384 : (j + 1) * 384]
        high = act[:, 1536 + j * 384 : 1536 + (j + 1) * 384]
        t_in[j * 384 : (j + 1) * 384, :] = (dot(low, sel[0], 0, 0) + dot(high, sel[1], 0, 0)).astype(bf16)
    for j in range(2):
        t_out[j * 384 : (j + 1) * 384, :] = dot(grad[:, j * 384 : (j + 1) * 384], grad[...], 0, 0)
    for target, core_at in ((mine, c), (other, 1 - c)):
        for z in range(8):
            row = pl.multiple_of(z * 192 + core_at * 96, 96)
            target[z, 0:96, :] = t_in[pl.ds(row, 96), :]
            row = pl.multiple_of(z * 48 + core_at * 24, 24)
            first, second = t_out[pl.ds(row, 24), :], t_out[pl.ds(pl.multiple_of(384 + row, 24), 24), :]
            pair = jnp.concatenate([first, second], axis=0).astype(bf16)
            target[z, 96:144, :] = pair[:, :384]
            target[z, 144:192, :] = pair[:, 384:]


def factor_parts(core, act, sel, grad):
    vmem = pl.BlockSpec(memory_space=pltpu.VMEM)
    return pl.pallas_call(
        factor_kernel,
        out_shape=[jax.ShapeDtypeStruct((8, 192, 384), bf16)] * 2,
        in_specs=[pl.BlockSpec(memory_space=pltpu.SMEM), vmem, vmem, vmem],
        out_specs=[vmem, vmem],
        scratch_shapes=[pltpu.VMEM((1536, 384), bf16), pltpu.VMEM((768, 768), f32)],
        compiler_params=pltpu.CompilerParams(vmem_limit_bytes=32 * 1024 * 1024),
        cost_estimate=pl.CostEstimate(flops=3_000_000_000, bytes_accessed=8_000_000, transcendentals=0),
    )(core, act, sel, grad)


def per_device(
    activations,
    output_grad,
    weight_grad,
    input_basis,
    input_eigen,
    output_basis,
    output_eigen,
    input_factor,
    output_factor,
):
    xh, c = lax.axis_index("xh"), lax.axis_index("c")
    m = lax.axis_index(MP)
    tokens = activations.shape[0] * 32

    halves = jnp.stack([weight_grad[:, :384], weight_grad[:, 384:]])
    send = jnp.broadcast_to(halves[None], (8, 2, 96, 384)).reshape(16, 96, 384)
    grad_rows = lax.all_to_all(send, ("z", "c"), 0, 0).reshape(1536, 384)

    basis_out = output_basis[0]
    basis_far = lax.ppermute(basis_out, "xh", swap)
    basis_pair = jnp.where(xh == 0, jnp.stack([basis_out, basis_far]), jnp.stack([basis_far, basis_out]))
    basis_all = lax.all_gather(basis_pair, ("z", "c"), axis=0)
    v = basis_all.transpose(1, 0, 2, 3).reshape(768, 768)

    selected = lax.dynamic_slice_in_dim(activations, m * 192, 192, 1)
    sel = jnp.stack([jnp.pad(selected, ((0, 0), (0, 192))), jnp.pad(selected, ((0, 0), (192, 0)))])
    mine, other = factor_parts(c.astype(jnp.int32).reshape(1), activations, sel, output_grad)
    came = lax.ppermute(other, "c", swap)
    pair = (mine.astype(f32) + came.astype(f32)).astype(bf16)
    summed = lax.psum_scatter(pair, "z", scatter_dimension=0, tiled=False)
    in_sum = summed[:96].reshape(96, 2, 192)
    out_sum = summed[96:].reshape(2, 2, 24, 384)
    in_came = lax.ppermute(pick(in_sum, 1 - xh, 1), "xh", swap)
    out_came = lax.ppermute(pick(out_sum, 1 - xh, 1), "xh", swap)
    in_total = pick(in_sum, xh, 1).astype(f32) + in_came.astype(f32)
    out_total = pick(out_sum, xh, 1).astype(f32) + out_came.astype(f32)
    new_input = keep_rate * input_factor + (1.0 - keep_rate) * (in_total.T / tokens)
    new_output = keep_rate * output_factor + (1.0 - keep_rate) * (
        out_total.transpose(1, 0, 2).reshape(1, 24, 768) / tokens
    )

    ut = input_basis.T
    ut_mine = lax.dynamic_slice_in_dim(ut, xh * 1536, 1536, 1)
    ut_other = lax.dynamic_slice_in_dim(ut, (1 - xh) * 1536, 1536, 1)
    ut_far = lax.ppermute(ut_other, "xh", swap)
    near = jnp.where(xh == 0, jnp.stack([ut_mine, ut_far]), jnp.stack([ut_far, ut_mine]))
    far = lax.ppermute(near, "c", swap)
    block = jnp.where(c == 0, jnp.stack([near, far], axis=1), jnp.stack([far, near], axis=1)).reshape(384, 1536)

    grad_rows, pair_done = lax.optimization_barrier((grad_rows, pair))
    left_part = dot(block, grad_rows, 1, 0).astype(bf16).reshape(4, 96, 384)
    left_parts = lax.all_to_all(left_part, QUAD, 0, 0).astype(f32).reshape(2, 2, 96, 384)
    left_two = (left_parts[0] + left_parts[1]).astype(bf16)
    left = jnp.concatenate([left_two[0], left_two[1]], axis=1)
    rotated = dot(left, v, 1, 0)
    denominator = input_eigen[:, None] * output_eigen[0][None, :] + damping
    scaled = (rotated / denominator).astype(bf16)
    back = dot(scaled, v, 1, 1).astype(bf16)

    back_halves = jnp.stack([back[:, :384], back[:, 384:]])
    send = jnp.broadcast_to(back_halves[None], (2, 2, 96, 384)).reshape(4, 96, 384)
    back_group = lax.all_to_all(send, QUAD, 0, 0).reshape(384, 384)
    out_part = dot(block, back_group, 0, 0).astype(bf16).reshape(16, 96, 384)
    out_parts = lax.all_to_all(out_part, ("z", "c"), 0, 0).reshape(8, 2, 96, 384)
    total = jnp.sum(out_parts.astype(f32), axis=0).astype(bf16)
    result = jnp.concatenate([total[0], total[1]], axis=1)
    return (new_input, new_output, result)


def solution(mesh):
    fine = Mesh(mesh.devices.reshape(2, 8, 2, 2, 8), DP + MP)
    placed = (
        P(DP, None),
        P(DP, MP),
        P(DP, MP),
        P(None, DP),
        P(DP),
        P(MP, DP, None),
        P(MP, None),
        P(MP, DP),
        P(MP, DP, None),
    )
    return jax.shard_map(
        per_device,
        mesh=fine,
        in_specs=placed,
        out_specs=(P(MP, DP), P(MP, DP, None), P(DP, MP)),
        check_vma=False,
    )
```

time: 202 us -> 145 us (0.72)
  the two profiles are of different devices: /device:TPU:33 before, /device:TPU:72 now
where the time goes in v2:
time: 145 us; the launch traced here: 144 us
  starting transfers between devices  44.5 us (31%)
  waiting for transfers between devices  42.6 us (29%)
  between operations  15.8 us (11%)
  other arithmetic  11.3 us (8%)
  blocking collectives  11 us (8%)
  local copies, waits for them, and re-layouts  9.24 us (6%)
  matrix products  7.15 us (5%)
  Pallas kernels  2.71 us (2%)
    reduce_scatter x1, waiting for transfers between devices, per_device(): summed = lax.psum_scatter(pair, 'z', scatter_dimension=0, tiled=False)  17.4 us
    ppermute x1, starting transfers between devices, per_device(): out_came = lax.ppermute(pick(out_sum, 1 - xh, 1), 'xh', swap)  12.1 us
    all_to_all x1, blocking collectives, per_device(): back_group = lax.all_to_all(send, QUAD, 0, 0).reshape(384, 384)  11 us
    all_to_all x1, starting transfers between devices, per_device(): grad_rows = lax.all_to_all(send, ('z', 'c'), 0, 0).reshape(1536, 384)  10.1 us
    all_to_all x1, waiting for transfers between devices, per_device(): lax.all_to_all(left_part, QUAD, 0, 0).astype(f32).reshape(2, 2, 96, 384)  7.27 us
    all_gather x1, waiting for transfers between devices, per_device(): basis_all = lax.all_gather(basis_pair, ('z', 'c'), axis=0)  7.2 us
    dot_general x3, matrix products, dot(): lax.dot_general(a, b, (((da,), (db,)), ((), ())), preferred_element_type=...  7.15 us
    all_to_all x1, starting transfers between devices, per_device(): lax.all_to_all(out_part, ('z', 'c'), 0, 0).reshape(8, 2, 96, 384)  5.19 us
  transfers between devices with their start and end apart: 11, of which 7 were waited for; matrix products, arithmetic and copies ran while one was open for 15% of the time, Pallas kernels for 2%

profile of v2, /device:TPU:72, one launch (start us, length us, event | category | flops | bytes accessed | tf_op | source)
XLA Modules:
  0.0 144.4 jit_solution(1191111859275437850)
XLA Ops:
  8.0 2.0 %dynamic-slice_bitcast_fusion.1 = (bf16[1,1,96,1536]{3,2,1,0:T(8,128)(2,1)S(1)}, bf16[96,1536]{1,0:T(8,128)(2,1)}, bf16[1,96,1536]{2,1,0:T(8,128)(2,1)}) fusion(bf16[3072,96]{0,1:T(8,128)(2,1)} %param.12, s32[]{:T(128)S(6)} %select_n.77, s32[]{:T(128)S(6)} %select_n.78), kind=kLoop, calls=%fused_computation.17 | loop fusion | bytes 1474568 | tf_op jit(solution)/shard_map/stack | solution.py:103
  10.0 4.9 %collective-permute-start.3 = (bf16[96,1536]{1,0:T(8,128)(2,1)}, bf16[96,1536]{1,0:T(8,128)(2,1)}, u32[]{:S(2)}, u32[]{:S(2)}) collective-permute-start(bf16[96,1536]{1,0:T(8,128)(2,1)} %get-tuple-element.10), channel_id=1, source_target_pairs={{0,256},{256,0},{1,257},{257,1},{2,258},{258,2},{3,259},{259,3},{4... | collective-permute-start | bytes 884744 | tf_op jit(solution)/shard_map/ppermute | solution.py:102
  16.2 10.1 %all-to-all-start = ((bf16[16,96,384]{2,1,0:T(8,128)(2,1)}), bf16[16,96,384]{2,1,0:T(8,128)(2,1)}, u32[]{:S(2)}, u32[]{:S(2)}) async-start(bf16[16,96,384]{2,1,0:T(8,128)(2,1)} %bitcast.22), calls=%async_computation.1 | async-start | bytes 2359296 | tf_op jit(solution)/shard_map/all_to_all | solution.py:74
  26.3 2.4 %collective-permute-start.5 = (bf16[24,768]{1,0:T(8,128)(2,1)S(1)}, bf16[24,768]{1,0:T(8,128)(2,1)S(1)}, u32[]{:S(2)}, u32[]{:S(2)}) collective-permute-start(bf16[24,768]{1,0:T(8,128)(2,1)S(1)} %bitcast.77), channel_id=1, source_target_pairs={{0,256},{256,0},{1,257},{257,1},{2,258},{258,2},{3,259},{259,3},{4... | collective-permute-start | bytes 110600 | tf_op jit(solution)/shard_map/ppermute | solution.py:77
  30.2 3.5 %collective-permute-done.5 = bf16[24,768]{1,0:T(8,128)(2,1)S(1)} collective-permute-done((bf16[24,768]{1,0:T(8,128)(2,1)S(1)}, bf16[24,768]{1,0:T(8,128)(2,1)S(1)}, u32[]{:S(2)}, u32[]{:S(2)}) %collective-permute-start.5) | collective-permute-done | bytes 36896 | tf_op jit(solution)/shard_map/ppermute | solution.py:77
  34.4 1.9 %copy-done = bf16[512,3072]{1,0:T(8,128)(2,1)S(1)} copy-done((bf16[512,3072]{1,0:T(8,128)(2,1)S(1)}, bf16[512,3072]{1,0:T(8,128)(2,1)}, u32[]{:S(2)}) %copy-start) | copy-done | bytes 3145752
  37.4 2.7 %shard_map.112 = (bf16[8,192,384]{2,1,0:T(8,128)(2,1)S(1)}, bf16[8,192,384]{2,1,0:T(8,128)(2,1)S(1)}) custom-call(s32[1]{0:T(128)} %bitcast.core, bf16[512,3072]{1,0:T(8,128)(2,1)S(1)} %copy-done, bf16[2,512,384]{2,1,0:T(8,128)(2,1)S(1)} %pad_maximum_fusion.sel, bf16[512,768]{1,0:T(8,128)(2,1)S(1)} %copy-done.1), custom_call_target="tpu_custom_call" | custom-call | flops 3000000000 | bytes 8000000 | tf_op jit(solution)/shard_map/pallas_call | solution.py:46
  40.1 1.9 %collective-permute-start = (bf16[8,192,384]{2,1,0:T(8,128)(2,1)S(1)}, bf16[8,192,384]{2,1,0:T(8,128)(2,1)}, u32[]{:S(2)}, u32[]{:S(2)}) collective-permute-start(bf16[8,192,384]{2,1,0:T(8,128)(2,1)S(1)} %get-tuple-element.7), channel_id=1, source_target_pairs={{0,16},{16,0},{1,17},{17,1},{2,18},{18,2},{3,19},{19,3},{4,20},{20... | collective-permute-start | bytes 3538952 | tf_op jit(solution)/shard_map/ppermute | solution.py:85
  42.0 2.0 %maximum_select_fusion.2 = bf16[2,96,1536]{2,1,0:T(8,128)(2,1)} fusion(bf16[1,96,1536]{2,1,0:T(8,128)(2,1)} %bitcast.16, bf16[1,96,1536]{2,1,0:T(8,128)(2,1)S(1)} %copy-done.3, pred[]{:T(512)S(6)} %eq.8), kind=kLoop, calls=%fused_computation.9 | loop fusion | flops 884736 | bytes 1179649 | tf_op jit(solution)/shard_map/jit(_where)/select_n | solution.py:103
  44.0 2.4 %collective-permute-start.4 = (bf16[2,96,1536]{2,1,0:T(8,128)(2,1)}, bf16[2,96,1536]{2,1,0:T(8,128)(2,1)}, u32[]{:S(2)}, u32[]{:S(2)}) collective-permute-start(bf16[2,96,1536]{2,1,0:T(8,128)(2,1)} %maximum_select_fusion.2), channel_id=1, source_target_pairs={{0,16},{16,0},{1,17},{17,1},{2,18},{18,2},{3,19},{19,3},{4,20},{20... | collective-permute-start | bytes 1769480 | tf_op jit(solution)/shard_map/ppermute | solution.py:104
  48.4 2.4 %maximum_select_fusion = bf16[2,2,96,1536]{3,2,1,0:T(8,128)(2,1)} fusion(bf16[2,1,96,1536]{3,2,1,0:T(8,128)(2,1)} %bitcast.18, bf16[2,1,96,1536]{3,2,1,0:T(8,128)(2,1)S(1)} %maximum_select_fusion.1, pred[]{:T(512)S(6)} %eq.7), kind=kLoop, calls=%fused_computation.3 | loop fusion | flops 1769472 | bytes 2359297 | tf_op jit(solution)/shard_map/jit(_where)/select_n | solution.py:105
  50.8 2.7 %add_convert_fusion = bf16[8,192,384]{2,1,0:T(8,128)(2,1)} fusion(bf16[8,192,384]{2,1,0:T(8,128)(2,1)} %collective-permute-done, bf16[8,192,384]{2,1,0:T(8,128)(2,1)S(1)} %get-tuple-element.6), kind=kLoop, calls=%fused_computation.1 | loop fusion | flops 2359296 | bytes 3538944 | tf_op jit(solution)/shard_map/convert_element_type | solution.py:86
  54.9 2.8 %convolution_convert_fusion.1 = bf16[384,384]{1,0:T(8,128)(2,1)} fusion(bf16[384,1536]{1,0:T(8,128)(2,1)S(1)} %bitcast.70, bf16[1536,384]{1,0:T(8,128)(2,1)} %bitcast.23), kind=kOutput, calls=%fused_computation.2 | convolution fusion | flops 453132288 | bytes 2654208 | tf_op jit(solution)/shard_map/dot_general | solution.py:18
  57.7 3.5 %all-to-all-start.1 = ((bf16[4,96,384]{2,1,0:T(8,128)(2,1)}), bf16[4,96,384]{2,1,0:T(8,128)(2,1)S(1)}, u32[]{:S(2)}, u32[]{:S(2)}) async-start(bf16[4,96,384]{2,1,0:T(8,128)(2,1)} %bitcast.24), calls=%async_computation.2 | async-start | bytes 589824 | tf_op jit(solution)/shard_map/all_to_all | solution.py:109
  61.8 7.3 %all-to-all-done.1 = bf16[4,96,384]{2,1,0:T(8,128)(2,1)S(1)} async-done(((bf16[4,96,384]{2,1,0:T(8,128)(2,1)}), bf16[4,96,384]{2,1,0:T(8,128)(2,1)S(1)}, u32[]{:S(2)}, u32[]{:S(2)}) %all-to-all-start.1) | async-done | bytes 294944 | tf_op jit(solution)/shard_map/all_to_all | solution.py:109
  69.1 7.2 %all-gather.2.cloned.1.call-done = bf16[16,2,24,768]{3,2,0,1:T(8,128)(2,1)} async-done(((bf16[1,2,24,768]{3,2,0,1:T(8,128)(2,1)}), bf16[16,2,24,768]{3,2,0,1:T(8,128)(2,1)}) %all-gather.2.cloned.1.call-update) | async-done | bytes 1179664 | tf_op jit(solution)/shard_map/all_gather | solution.py:79
  76.3 2.4 %convolution_convert_fusion.2 = bf16[96,768]{1,0:T(8,128)(2,1)S(1)} fusion(bf16[768,768]{1,0:T(8,128)(2,1)} %bitcast.80, bf16[96,384]{1,0:T(8,128)(2,1)S(1)} %get-tuple-element.19, bf16[96,384]{1,0:T(8,128)(2,1)S(1)} %get-tuple-element.18, f32[768]{0:T(1024)S(1)} %reduce.1, f32[96]{0:T(128)S(1)} %copy-done.9), kind=kOutput, calls=%fused_computation.5 | convolution fusion | flops 227155968 | bytes 1478016 | tf_op jit(solution)/shard_map/dot_general | solution.py:18
  78.8 11.0 %all_to_all.20 = bf16[4,96,384]{2,1,0:T(8,128)(2,1)S(1)} all-to-all(bf16[4,96,384]{2,1,0:T(8,128)(2,1)S(1)} %bitcast.72), channel_id=1, replica_groups=mesh['xh'=2,'z'=8,'c'=2,'xl'=2,'y'=8] {'xh','c'}, dimensions={0} | all-to-all | bytes 589824 | tf_op jit(solution)/shard_map/all_to_all | solution.py:119
  89.8 2.0 %convolution_convert_fusion = bf16[1536,384]{1,0:T(8,128)(2,1)} fusion(bf16[384,1536]{1,0:T(8,128)(2,1)S(1)} %bitcast.71, bf16[384,384]{1,0:T(8,128)(2,1)S(1)} %bitcast.73), kind=kOutput, calls=%fused_computation | convolution fusion | flops 453574656 | bytes 2654208 | tf_op jit(solution)/shard_map/dot_general | solution.py:18
  91.8 5.2 %all-to-all-start.3 = ((bf16[16,96,384]{2,1,0:T(8,128)(2,1)}), bf16[16,96,384]{2,1,0:T(8,128)(2,1)S(1)}, u32[]{:S(2)}, u32[]{:S(2)}) async-start(bf16[16,96,384]{2,1,0:T(8,128)(2,1)} %bitcast.36), calls=%async_computation.4 | async-start | bytes 2359296 | tf_op jit(solution)/shard_map/all_to_all | solution.py:121
  97.0 17.4 %reduce-scatter.2.cloned.1.call-done = bf16[1,192,384]{2,1,0:T(8,128)(2,1)} async-done(((bf16[8,192,384]{2,1,0:T(8,128)(2,1)}), bf16[1,192,384]{2,1,0:T(8,128)(2,1)}) %reduce-scatter.2.cloned.1.call-update) | async-done | bytes 147472 | tf_op jit(solution)/shard_map/reduce_scatter | solution.py:87
  115.4 12.1 %collective-permute-start.2 = (bf16[2,24,384]{2,1,0:T(8,128)(2,1)S(1)}, bf16[2,24,384]{2,1,0:T(8,128)(2,1)S(1)}, u32[]{:S(2)}, u32[]{:S(2)}) collective-permute-start(bf16[2,24,384]{2,1,0:T(8,128)(2,1)S(1)} %dynamic-slice_bitcast_fusion.3), channel_id=1, source_target_pairs={{0,256},{256,0},{1,257},{257,1},{2,258},{258,2},{3,259},{259,3},{4... | collective-permute-start | bytes 110600 | tf_op jit(solution)/shard_map/ppermute | solution.py:91
  128.0 1.9 %collective-permute-start.1 = (bf16[96,192]{0,1:T(8,128)(2,1)S(1)}, bf16[96,192]{0,1:T(8,128)(2,1)S(1)}, u32[]{:S(2)}, u32[]{:S(2)}) collective-permute-start(bf16[96,192]{0,1:T(8,128)(2,1)S(1)} %bitcast.76), channel_id=1, source_target_pairs={{0,256},{256,0},{1,257},{257,1},{2,258},{258,2},{3,259},{259,3},{4... | collective-permute-start | bytes 110600 | tf_op jit(solution)/shard_map/ppermute | solution.py:90
  130.8 4.6 %collective-permute-done.1 = bf16[96,192]{0,1:T(8,128)(2,1)S(1)} collective-permute-done((bf16[96,192]{0,1:T(8,128)(2,1)S(1)}, bf16[96,192]{0,1:T(8,128)(2,1)S(1)}, u32[]{:S(2)}, u32[]{:S(2)}) %collective-permute-start.1) | collective-permute-done | bytes 36896 | tf_op jit(solution)/shard_map/ppermute | solution.py:90
  (58 shorter events, 12.3 us)
Async XLA Ops:
  8.0 7.0 %copy-start.4 = (bf16[96,768]{1,0:T(8,128)(2,1)S(1)}, bf16[96,768]{1,0:T(8,128)(2,1)}, u32[]{:S(2)}) copy-start(bf16[96,768]{1,0:T(8,128)(2,1)} %param.11) | copy-start | bytes 442372
  10.0 32.0 %collective-permute-start.3 = (bf16[96,1536]{1,0:T(8,128)(2,1)}, bf16[96,1536]{1,0:T(8,128)(2,1)}, u32[]{:S(2)}, u32[]{:S(2)}) collective-permute-start(bf16[96,1536]{1,0:T(8,128)(2,1)} %get-tuple-element.10), channel_id=1, source_target_pairs={{0,256},{256,0},{1,257},{257,1},{2,258},{258,2},{3,259},{259,3},{4... | collective-permute-start | bytes 884744 | tf_op jit(solution)/shard_map/ppermute | solution.py:102
  16.1 10.2 %copy-start.7 = (bf16[1,24,768]{2,1,0:T(8,128)(2,1)S(1)}, bf16[1,24,768]{2,1,0:T(8,128)(2,1)}, u32[]{:S(2)}) copy-start(bf16[1,24,768]{2,1,0:T(8,128)(2,1)} %param.14) | copy-start | bytes 110596
  16.2 38.8 %all-to-all-start = ((bf16[16,96,384]{2,1,0:T(8,128)(2,1)}), bf16[16,96,384]{2,1,0:T(8,128)(2,1)}, u32[]{:S(2)}, u32[]{:S(2)}) async-start(bf16[16,96,384]{2,1,0:T(8,128)(2,1)} %bitcast.22), calls=%async_computation.1 | async-start | bytes 2359296 | tf_op jit(solution)/shard_map/all_to_all | solution.py:74
  26.3 50.1 %all-gather.2.cloned.1.call-start = ((), (), s32[]{:S(2)}) async-start(), calls=%async_computation.6 | async-start | bytes 1253376 | tf_op jit(solution)/shard_map/all_gather | solution.py:79
  26.3 7.4 %collective-permute-start.5 = (bf16[24,768]{1,0:T(8,128)(2,1)S(1)}, bf16[24,768]{1,0:T(8,128)(2,1)S(1)}, u32[]{:S(2)}, u32[]{:S(2)}) collective-permute-start(bf16[24,768]{1,0:T(8,128)(2,1)S(1)} %bitcast.77), channel_id=1, source_target_pairs={{0,256},{256,0},{1,257},{257,1},{2,258},{258,2},{3,259},{259,3},{4... | collective-permute-start | bytes 110600 | tf_op jit(solution)/shard_map/ppermute | solution.py:77
  34.3 1.9 %copy-start = (bf16[512,3072]{1,0:T(8,128)(2,1)S(1)}, bf16[512,3072]{1,0:T(8,128)(2,1)}, u32[]{:S(2)}) copy-start(bf16[512,3072]{1,0:T(8,128)(2,1)} %act.1) | copy-start | bytes 9437188
  36.2 1.1 copy-start.1
  37.4 4.7 %copy-start.3 = (bf16[1,96,1536]{2,1,0:T(8,128)(2,1)S(1)}, bf16[1,96,1536]{2,1,0:T(8,128)(2,1)}, u32[]{:S(2)}) copy-start(bf16[1,96,1536]{2,1,0:T(8,128)(2,1)} %get-tuple-element.11) | copy-start | bytes 884740
  40.1 10.7 %collective-permute-start = (bf16[8,192,384]{2,1,0:T(8,128)(2,1)S(1)}, bf16[8,192,384]{2,1,0:T(8,128)(2,1)}, u32[]{:S(2)}, u32[]{:S(2)}) collective-permute-start(bf16[8,192,384]{2,1,0:T(8,128)(2,1)S(1)} %get-tuple-element.7), channel_id=1, source_target_pairs={{0,16},{16,0},{1,17},{17,1},{2,18},{18,2},{3,19},{19,3},{4,20},{20... | collective-permute-start | bytes 3538952 | tf_op jit(solution)/shard_map/ppermute | solution.py:85
  44.0 4.4 %collective-permute-start.4 = (bf16[2,96,1536]{2,1,0:T(8,128)(2,1)}, bf16[2,96,1536]{2,1,0:T(8,128)(2,1)}, u32[]{:S(2)}, u32[]{:S(2)}) collective-permute-start(bf16[2,96,1536]{2,1,0:T(8,128)(2,1)} %maximum_select_fusion.2), channel_id=1, source_target_pairs={{0,16},{16,0},{1,17},{17,1},{2,18},{18,2},{3,19},{19,3},{4,20},{20... | collective-permute-start | bytes 1769480 | tf_op jit(solution)/shard_map/ppermute | solution.py:104
  50.8 4.1 %copy-start.2 = (bf16[2,2,96,1536]{3,2,1,0:T(8,128)(2,1)S(1)}, bf16[2,2,96,1536]{3,2,1,0:T(8,128)(2,1)}, u32[]{:S(2)}) copy-start(bf16[2,2,96,1536]{3,2,1,0:T(8,128)(2,1)} %maximum_select_fusion) | copy-start | bytes 3538948
  54.9 6.3 %copy-start.8 = (f32[1,768]{1,0:T(1,128)S(1)}, f32[1,768]{1,0:T(1,128)}, u32[]{:S(2)}) copy-start(f32[1,768]{1,0:T(1,128)} %param.15) | copy-start | bytes 9220
  57.7 11.3 %all-to-all-start.1 = ((bf16[4,96,384]{2,1,0:T(8,128)(2,1)}), bf16[4,96,384]{2,1,0:T(8,128)(2,1)S(1)}, u32[]{:S(2)}, u32[]{:S(2)}) async-start(bf16[4,96,384]{2,1,0:T(8,128)(2,1)} %bitcast.24), calls=%async_computation.2 | async-start | bytes 589824 | tf_op jit(solution)/shard_map/all_to_all | solution.py:109
  61.2 53.2 %reduce-scatter.2.cloned.1.call-start = ((), (), s32[]{:S(2)}) async-start(), calls=%async_computation.5 | async-start | bytes 1327104 | tf_op jit(solution)/shard_map/reduce_scatter | solution.py:87
  61.7 14.6 %copy-start.9 = (f32[96]{0:T(128)S(1)}, f32[96]{0:T(128)}, u32[]{:S(2)}) copy-start(f32[96]{0:T(128)} %param.13) | copy-start | bytes 1156
  91.8 44.3 %all-to-all-start.3 = ((bf16[16,96,384]{2,1,0:T(8,128)(2,1)}), bf16[16,96,384]{2,1,0:T(8,128)(2,1)S(1)}, u32[]{:S(2)}, u32[]{:S(2)}) async-start(bf16[16,96,384]{2,1,0:T(8,128)(2,1)} %bitcast.36), calls=%async_computation.4 | async-start | bytes 2359296 | tf_op jit(solution)/shard_map/all_to_all | solution.py:121
  97.0 33.2 %copy-start.6 = (f32[1,24,768]{2,1,0:T(8,128)S(1)}, f32[1,24,768]{2,1,0:T(8,128)}, u32[]{:S(2)}) copy-start(f32[1,24,768]{2,1,0:T(8,128)} %param.17) | copy-start | bytes 221188
  97.0 38.4 %copy-start.5 = (f32[192,96]{1,0:T(8,128)S(1)}, f32[192,96]{1,0:T(8,128)}, u32[]{:S(2)}) copy-start(f32[192,96]{1,0:T(8,128)} %param.16) | copy-start | bytes 221188
  115.4 14.7 %collective-permute-start.2 = (bf16[2,24,384]{2,1,0:T(8,128)(2,1)S(1)}, bf16[2,24,384]{2,1,0:T(8,128)(2,1)S(1)}, u32[]{:S(2)}, u32[]{:S(2)}) collective-permute-start(bf16[2,24,384]{2,1,0:T(8,128)(2,1)S(1)} %dynamic-slice_bitcast_fusion.3), channel_id=1, source_target_pairs={{0,256},{256,0},{1,257},{257,1},{2,258},{258,2},{3,259},{259,3},{4... | collective-permute-start | bytes 110600 | tf_op jit(solution)/shard_map/ppermute | solution.py:91
  128.0 7.5 %collective-permute-start.1 = (bf16[96,192]{0,1:T(8,128)(2,1)S(1)}, bf16[96,192]{0,1:T(8,128)(2,1)S(1)}, u32[]{:S(2)}, u32[]{:S(2)}) collective-permute-start(bf16[96,192]{0,1:T(8,128)(2,1)S(1)} %bitcast.76), channel_id=1, source_target_pairs={{0,256},{256,0},{1,257},{257,1},{2,258},{258,2},{3,259},{259,3},{4... | collective-permute-start | bytes 110600 | tf_op jit(solution)/shard_map/ppermute | solution.py:90
Sparse Core Ops, SparseCore 0:
  34.5 41.8 all-gather.1
Sparse Core Ops, SparseCore 1:
  64.5 49.9 reduce-scatter.1

commit v3 on v2

--- a/solution.py
+++ b/solution.py
@@ -10,7 +10,6 @@
 swap = ((0, 1), (1, 0))
 DP = ("xh", "z", "c")
 MP = ("xl", "y")
-QUAD = ("xh", "c")
 bf16, f32 = jnp.bfloat16, jnp.float32
 
 
@@ -69,22 +68,56 @@
     m = lax.axis_index(MP)
     tokens = activations.shape[0] * 32
 
-    halves = jnp.stack([weight_grad[:, :384], weight_grad[:, 384:]])
-    send = jnp.broadcast_to(halves[None], (8, 2, 96, 384)).reshape(16, 96, 384)
-    grad_rows = lax.all_to_all(send, ("z", "c"), 0, 0).reshape(1536, 384)
-
-    basis_out = output_basis[0]
-    basis_far = lax.ppermute(basis_out, "xh", swap)
-    basis_pair = jnp.where(xh == 0, jnp.stack([basis_out, basis_far]), jnp.stack([basis_far, basis_out]))
-    basis_all = lax.all_gather(basis_pair, ("z", "c"), axis=0)
-    v = basis_all.transpose(1, 0, 2, 3).reshape(768, 768)
+    rows = jnp.concatenate([weight_grad, output_basis[0]], axis=0)
+    halves = jnp.stack([rows[:, :384], rows[:, 384:]])
+    send = jnp.broadcast_to(halves[None], (8, 2, 120, 384)).reshape(16, 120, 384)
+    came_rows = lax.all_to_all(send, ("z", "c"), 0, 0)
 
     selected = lax.dynamic_slice_in_dim(activations, m * 192, 192, 1)
     sel = jnp.stack([jnp.pad(selected, ((0, 0), (0, 192))), jnp.pad(selected, ((0, 0), (192, 0)))])
     mine, other = factor_parts(c.astype(jnp.int32).reshape(1), activations, sel, output_grad)
     came = lax.ppermute(other, "c", swap)
     pair = (mine.astype(f32) + came.astype(f32)).astype(bf16)
-    summed = lax.psum_scatter(pair, "z", scatter_dimension=0, tiled=False)
+    basis_in, _ = lax.optimization_barrier((input_basis, send))
+    ut = basis_in.T
+    ut_mine = lax.dynamic_slice_in_dim(ut, xh * 1536, 1536, 1)
+    ut_other = lax.dynamic_slice_in_dim(ut, (1 - xh) * 1536, 1536, 1)
+    ut_far = lax.ppermute(ut_other, "xh", swap)
+    near = jnp.where(xh == 0, jnp.stack([ut_mine, ut_far]), jnp.stack([ut_far, ut_mine]))
+    far = lax.ppermute(near, "c", swap)
+    block = jnp.concatenate([near, far], axis=0).reshape(384, 1536)
+
+    eigen_far = lax.ppermute(input_eigen, "xh", swap)
+    came_rows, pair, eigen_far = lax.optimization_barrier((came_rows, pair, eigen_far))
+    left_part = dot(block, came_rows[:, :96].reshape(1536, 384), 1, 0)
+    left_send, v_mine, pair = lax.optimization_barrier((left_part.astype(bf16), came_rows[:, 96:].reshape(384, 384), pair))
+    left_came = lax.ppermute(left_send, "xh", swap)
+    v_came = lax.ppermute(v_mine, "xh", swap)
+    v_near = jnp.where(xh == 0, jnp.concatenate([v_mine, v_came]), jnp.concatenate([v_came, v_mine]))
+    v_far = lax.ppermute(v_near, "c", swap)
+    v = jnp.concatenate([v_near, v_far], axis=1)
+    left_half = (left_part + left_came.astype(f32)).astype(bf16)
+    left_far = lax.ppermute(left_half[192:], "c", swap)
+    left = jnp.where(
+        c == 0,
+        jnp.concatenate([left_half[:192], left_far], axis=1),
+        jnp.concatenate([left_far, left_half[:192]], axis=1),
+    )
+    rotated = dot(left, v, 1, 0)
+    eigen = jnp.where(xh == 0, jnp.stack([input_eigen, eigen_far]), jnp.stack([eigen_far, input_eigen]))
+    eigen_out = output_eigen[0]
+    eigen_out = jnp.where(c == 0, eigen_out, jnp.concatenate([eigen_out[384:], eigen_out[:384]]))
+    denominator = eigen.reshape(192, 1) * eigen_out[None, :] + damping
+    scaled = (rotated / denominator).astype(bf16)
+    back = dot(scaled, v, 1, 1).astype(bf16)
+
+    low, high = back[:, :384], back[:, 384:]
+    back_far = lax.ppermute(jnp.where(c == 0, high, low), "c", swap)
+    back_group = jnp.concatenate([jnp.where(c == 0, low, high), back_far], axis=0)
+    out_part = dot(block, back_group, 0, 0).astype(bf16).reshape(16, 96, 384)
+    came = lax.all_to_all(pair, "z", 0, 0)
+    out_part, came = lax.optimization_barrier((out_part, came))
+    summed = jnp.sum(came.astype(f32), axis=0).astype(bf16)
     in_sum = summed[:96].reshape(96, 2, 192)
     out_sum = summed[96:].reshape(2, 2, 24, 384)
     in_came = lax.ppermute(pick(in_sum, 1 - xh, 1), "xh", swap)
@@ -96,28 +129,6 @@
         out_total.transpose(1, 0, 2).reshape(1, 24, 768) / tokens
     )
 
-    ut = input_basis.T
-    ut_mine = lax.dynamic_slice_in_dim(ut, xh * 1536, 1536, 1)
-    ut_other = lax.dynamic_slice_in_dim(ut, (1 - xh) * 1536, 1536, 1)
-    ut_far = lax.ppermute(ut_other, "xh", swap)
-    near = jnp.where(xh == 0, jnp.stack([ut_mine, ut_far]), jnp.stack([ut_far, ut_mine]))
-    far = lax.ppermute(near, "c", swap)
-    block = jnp.where(c == 0, jnp.stack([near, far], axis=1), jnp.stack([far, near], axis=1)).reshape(384, 1536)
-
-    grad_rows, pair_done = lax.optimization_barrier((grad_rows, pair))
-    left_part = dot(block, grad_rows, 1, 0).astype(bf16).reshape(4, 96, 384)
-    left_parts = lax.all_to_all(left_part, QUAD, 0, 0).astype(f32).reshape(2, 2, 96, 384)
-    left_two = (left_parts[0] + left_parts[1]).astype(bf16)
-    left = jnp.concatenate([left_two[0], left_two[1]], axis=1)
-    rotated = dot(left, v, 1, 0)
-    denominator = input_eigen[:, None] * output_eigen[0][None, :] + damping
-    scaled = (rotated / denominator).astype(bf16)
-    back = dot(scaled, v, 1, 1).astype(bf16)
-
-    back_halves = jnp.stack([back[:, :384], back[:, 384:]])
-    send = jnp.broadcast_to(back_halves[None], (2, 2, 96, 384)).reshape(4, 96, 384)
-    back_group = lax.all_to_all(send, QUAD, 0, 0).reshape(384, 384)
-    out_part = dot(block, back_group, 0, 0).astype(bf16).reshape(16, 96, 384)
     out_parts = lax.all_to_all(out_part, ("z", "c"), 0, 0).reshape(8, 2, 96, 384)
     total = jnp.sum(out_parts.astype(f32), axis=0).astype(bf16)
     result = jnp.concatenate([total[0], total[1]], axis=1)

time: 145 us -> 131 us (0.903)
  the two profiles are of different devices: /device:TPU:72 before, /device:TPU:1 now
where the time goes in v3:
time: 131 us; the launch traced here: 130 us
  starting transfers between devices  55.8 us (43%)
  waiting for transfers between devices  48.8 us (37%)
  other arithmetic  9.45 us (7%)
  local copies, waits for them, and re-layouts  7.14 us (5%)
  matrix products  5.31 us (4%)
  Pallas kernels  2.69 us (2%)
    all_to_all x1, waiting for transfers between devices, per_device(): lax.all_to_all(out_part, ('z', 'c'), 0, 0).reshape(8, 2, 96, 384)  20.5 us
    all_to_all x1, waiting for transfers between devices, per_device(): came_rows = lax.all_to_all(send, ('z', 'c'), 0, 0)  12.2 us
    all_to_all x1, starting transfers between devices, per_device(): came_rows = lax.all_to_all(send, ('z', 'c'), 0, 0)  12 us
    all_to_all x1, waiting for transfers between devices, per_device(): came = lax.all_to_all(pair, 'z', 0, 0)  8.27 us
    dot_general x3, matrix products, dot(): lax.dot_general(a, b, (((da,), (db,)), ((), ())), preferred_element_type=...  5.31 us
    ppermute x1, starting transfers between devices, per_device(): v_came = lax.ppermute(v_mine, 'xh', swap)  4.65 us
    ppermute x1, starting transfers between devices, per_device(): eigen_far = lax.ppermute(input_eigen, 'xh', swap)  4.65 us
    ppermute x1, starting transfers between devices, per_device(): in_came = lax.ppermute(pick(in_sum, 1 - xh, 1), 'xh', swap)  4.65 us
  transfers between devices with their start and end apart: 14, of which 9 were waited for; matrix products, arithmetic and copies ran while one was open for 12% of the time, Pallas kernels for 2%

profile of v3, /device:TPU:1, one launch (start us, length us, event | category | flops | bytes accessed | tf_op | source)
XLA Modules:
  0.0 130.2 jit_solution(6796011981701297634)
XLA Ops:
  2.9 12.0 %all-to-all-start = ((bf16[16,120,384]{2,1,0:T(8,128)(2,1)}), bf16[16,120,384]{2,1,0:T(8,128)(2,1)}, u32[]{:S(2)}, u32[]{:S(2)}) async-start(bf16[16,120,384]{2,1,0:T(8,128)(2,1)} %bitcast.3), calls=%async_computation | async-start | bytes 2949120 | tf_op jit(solution)/shard_map/all_to_all | solution.py:74
  15.6 4.6 %collective-permute-start = (bf16[96,1536]{1,0:T(8,128)(2,1)}, bf16[96,1536]{1,0:T(8,128)(2,1)}, u32[]{:S(2)}, u32[]{:S(2)}) collective-permute-start(bf16[96,1536]{1,0:T(8,128)(2,1)} %get-tuple-element.26), channel_id=1, source_target_pairs={{0,256},{256,0},{1,257},{257,1},{2,258},{258,2},{3,259},{259,3},{4... | collective-permute-start | bytes 884744 | tf_op jit(solution)/shard_map/ppermute | solution.py:85
  22.3 2.7 %shard_map.112 = (bf16[8,192,384]{2,1,0:T(8,128)(2,1)S(1)}, bf16[8,192,384]{2,1,0:T(8,128)(2,1)S(1)}) custom-call(s32[1]{0:T(128)} %bitcast.10.core, bf16[512,3072]{1,0:T(8,128)(2,1)S(1)} %copy-done, bf16[2,512,384]{2,1,0:T(8,128)(2,1)S(1)} %pad_maximum_fusion.4.sel, bf16[512,768]{1,0:T(8,128)(2,1)S(1)} %copy-done.1), custom_call_target="tpu_custom_call" | custom-call | flops 3000000000 | bytes 8000000 | tf_op jit(solution)/shard_map/pallas_call | solution.py:45
  25.0 2.3 %collective-permute-start.2 = (bf16[8,192,384]{2,1,0:T(8,128)(2,1)S(1)}, bf16[8,192,384]{2,1,0:T(8,128)(2,1)}, u32[]{:S(2)}, u32[]{:S(2)}) collective-permute-start(bf16[8,192,384]{2,1,0:T(8,128)(2,1)S(1)} %get-tuple-element.16), channel_id=1, source_target_pairs={{0,16},{16,0},{1,17},{17,1},{2,18},{18,2},{3,19},{19,3},{4,20},{20... | collective-permute-start | bytes 3538952 | tf_op jit(solution)/shard_map/ppermute | solution.py:79
  28.9 2.9 %collective-permute-start.1 = (bf16[2,96,1536]{2,1,0:T(8,128)(2,1)S(1)}, bf16[2,96,1536]{2,1,0:T(8,128)(2,1)S(1)}, u32[]{:S(2)}, u32[]{:S(2)}) collective-permute-start(bf16[2,96,1536]{2,1,0:T(8,128)(2,1)S(1)} %maximum_select_fusion), channel_id=1, source_target_pairs={{0,16},{16,0},{1,17},{17,1},{2,18},{18,2},{3,19},{19,3},{4,20},{20... | collective-permute-start | bytes 1769480 | tf_op jit(solution)/shard_map/ppermute | solution.py:87
  31.8 4.7 %collective-permute-start.3 = (f32[96]{0:T(128)S(1)}, f32[96]{0:T(128)S(1)}, u32[]{:S(2)}, u32[]{:S(2)}) collective-permute-start(f32[96]{0:T(128)S(1)} %copy-done.6), channel_id=1, source_target_pairs={{0,256},{256,0},{1,257},{257,1},{2,258},{258,2},{3,259},{259,3},{4... | collective-permute-start | bytes 1160 | tf_op jit(solution)/shard_map/ppermute | solution.py:90
  36.6 2.6 %add_convert_fusion = bf16[8,192,384]{2,1,0:T(8,128)(2,1)} fusion(bf16[8,192,384]{2,1,0:T(8,128)(2,1)} %collective-permute-done.2, bf16[8,192,384]{2,1,0:T(8,128)(2,1)S(1)} %get-tuple-element.15), kind=kLoop, calls=%fused_computation.1 | loop fusion | flops 2359296 | bytes 3538944 | tf_op jit(solution)/shard_map/convert_element_type | solution.py:80
  39.2 12.2 %all-to-all-done = bf16[16,120,384]{2,1,0:T(8,128)(2,1)} async-done(((bf16[16,120,384]{2,1,0:T(8,128)(2,1)}), bf16[16,120,384]{2,1,0:T(8,128)(2,1)}, u32[]{:S(2)}, u32[]{:S(2)}) %all-to-all-start) | async-done | bytes 1474592 | tf_op jit(solution)/shard_map/all_to_all | solution.py:74
  54.6 4.7 %collective-permute-start.6 = (bf16[384,384]{1,0:T(8,128)(2,1)S(1)}, bf16[384,384]{1,0:T(8,128)(2,1)}, u32[]{:S(2)}, u32[]{:S(2)}) collective-permute-start(bf16[384,384]{1,0:T(8,128)(2,1)S(1)} %bitcast.52), channel_id=1, source_target_pairs={{0,256},{256,0},{1,257},{257,1},{2,258},{258,2},{3,259},{259,3},{4... | collective-permute-start | bytes 884744 | tf_op jit(solution)/shard_map/ppermute | solution.py:95
  59.2 3.6 %all-to-all-start.1 = ((bf16[8,192,384]{2,1,0:T(8,128)(2,1)}), bf16[8,192,384]{2,1,0:T(8,128)(2,1)S(1)}, u32[]{:S(2)}, u32[]{:S(2)}) async-start(bf16[8,192,384]{2,1,0:T(8,128)(2,1)} %add_convert_fusion), calls=%async_computation.1 | async-start | bytes 2359296 | tf_op jit(solution)/shard_map/all_to_all | solution.py:118
  62.8 2.1 %collective-permute-start.4 = (bf16[384,384]{1,0:T(8,128)(2,1)S(1)}, bf16[384,384]{1,0:T(8,128)(2,1)S(1)}, u32[]{:S(2)}, u32[]{:S(2)}) collective-permute-start(bf16[384,384]{1,0:T(8,128)(2,1)S(1)} %get-tuple-element.19), channel_id=1, source_target_pairs={{0,256},{256,0},{1,257},{257,1},{2,258},{258,2},{3,259},{259,3},{4... | collective-permute-start | bytes 884744 | tf_op jit(solution)/shard_map/ppermute | solution.py:94
  65.0 1.8 %collective-permute-done.6 = bf16[384,384]{1,0:T(8,128)(2,1)} collective-permute-done((bf16[384,384]{1,0:T(8,128)(2,1)S(1)}, bf16[384,384]{1,0:T(8,128)(2,1)}, u32[]{:S(2)}, u32[]{:S(2)}) %collective-permute-start.6) | collective-permute-done | bytes 294944 | tf_op jit(solution)/shard_map/ppermute | solution.py:95
  66.8 2.1 %maximum_select_fusion.1 = bf16[768,384]{1,0:T(8,128)(2,1)} fusion(bf16[384,384]{1,0:T(8,128)(2,1)} %collective-permute-done.6, bf16[384,384]{1,0:T(8,128)(2,1)S(1)} %bitcast.53, pred[]{:T(512)S(6)} %eq.4), kind=kLoop, calls=%fused_computation.9 | loop fusion | flops 2654208 | bytes 1179649 | tf_op jit(solution)/shard_map/jit(_where)/select_n | solution.py:96
  68.9 2.3 %collective-permute-start.7 = (bf16[768,384]{1,0:T(8,128)(2,1)}, bf16[768,384]{1,0:T(8,128)(2,1)}, u32[]{:S(2)}, u32[]{:S(2)}) collective-permute-start(bf16[768,384]{1,0:T(8,128)(2,1)} %maximum_select_fusion.1), channel_id=1, source_target_pairs={{0,16},{16,0},{1,17},{17,1},{2,18},{18,2},{3,19},{19,3},{4,20},{20... | collective-permute-start | bytes 1769480 | tf_op jit(solution)/shard_map/ppermute | solution.py:97
  71.2 2.8 %collective-permute-done.4 = bf16[384,384]{1,0:T(8,128)(2,1)S(1)} collective-permute-done((bf16[384,384]{1,0:T(8,128)(2,1)S(1)}, bf16[384,384]{1,0:T(8,128)(2,1)S(1)}, u32[]{:S(2)}, u32[]{:S(2)}) %collective-permute-start.4) | collective-permute-done | bytes 294944 | tf_op jit(solution)/shard_map/ppermute | solution.py:94
  74.1 3.6 %collective-permute-start.5 = (bf16[192,384]{1,0:T(8,128)(2,1)S(1)}, bf16[192,384]{1,0:T(8,128)(2,1)S(1)}, u32[]{:S(2)}, u32[]{:S(2)}) collective-permute-start(bf16[192,384]{1,0:T(8,128)(2,1)S(1)} %get-tuple-element.30), channel_id=1, source_target_pairs={{0,16},{16,0},{1,17},{17,1},{2,18},{18,2},{3,19},{19,3},{4,20},{20... | collective-permute-start | bytes 442376 | tf_op jit(solution)/shard_map/ppermute | solution.py:100
  78.7 2.5 %convolution_convert_fusion.1 = bf16[192,768]{1,0:T(8,128)(2,1)S(1)} fusion(bf16[768,384]{1,0:T(8,128)(2,1)} %collective-permute-done.7, bf16[768,384]{1,0:T(8,128)(2,1)} %maximum_select_fusion.1, bf16[192,384]{1,0:T(8,128)(2,1)S(1)} %collective-permute-done.5, bf16[192,384]{1,0:T(8,128)(2,1)S(1)} %get-tuple-element.29, f32[768]{0:T(1024)S(1)} %fusion.29, ...), kind=kOutput, calls=%fused_computation.4 | convolution fusion | flops 459767808 | bytes 1773313 | tf_op jit(solution)/shard_map/dot_general | solution.py:17
  81.2 2.3 %collective-permute-start.8 = (bf16[192,384]{1,0:T(8,128)(2,1)S(1)}, bf16[192,384]{1,0:T(8,128)(2,1)S(1)}, u32[]{:S(2)}, u32[]{:S(2)}) collective-permute-start(bf16[192,384]{1,0:T(8,128)(2,1)S(1)} %get-tuple-element.28), channel_id=1, source_target_pairs={{0,16},{16,0},{1,17},{17,1},{2,18},{18,2},{3,19},{19,3},{4,20},{20... | collective-permute-start | bytes 442376 | tf_op jit(solution)/shard_map/ppermute | solution.py:115
  84.5 2.0 %convolution_convert_fusion = bf16[1536,384]{1,0:T(8,128)(2,1)} fusion(bf16[384,1536]{1,0:T(8,128)(2,1)S(1)} %bitcast.49, bf16[192,384]{1,0:T(8,128)(2,1)S(1)} %collective-permute-done.8, bf16[192,384]{1,0:T(8,128)(2,1)S(1)} %get-tuple-element.27), kind=kOutput, calls=%fused_computation | convolution fusion | flops 454164480 | bytes 2654208 | tf_op jit(solution)/shard_map/dot_general | solution.py:17
  86.5 8.3 %all-to-all-done.1 = bf16[8,192,384]{2,1,0:T(8,128)(2,1)S(1)} async-done(((bf16[8,192,384]{2,1,0:T(8,128)(2,1)}), bf16[8,192,384]{2,1,0:T(8,128)(2,1)S(1)}, u32[]{:S(2)}, u32[]{:S(2)}) %all-to-all-start.1) | async-done | bytes 1179680 | tf_op jit(solution)/shard_map/all_to_all | solution.py:118
  94.8 4.0 %all-to-all-start.2 = ((bf16[16,96,384]{2,1,0:T(8,128)(2,1)}), bf16[16,96,384]{2,1,0:T(8,128)(2,1)S(1)}, u32[]{:S(2)}, u32[]{:S(2)}) async-start(bf16[16,96,384]{2,1,0:T(8,128)(2,1)} %bitcast.17), calls=%async_computation.2 | async-start | bytes 2359296 | tf_op jit(solution)/shard_map/all_to_all | solution.py:132
  99.0 2.1 %collective-permute-start.10 = (bf16[2,24,384]{2,1,0:T(8,128)(2,1)S(1)}, bf16[2,24,384]{2,1,0:T(8,128)(2,1)S(1)}, u32[]{:S(2)}, u32[]{:S(2)}) collective-permute-start(bf16[2,24,384]{2,1,0:T(8,128)(2,1)S(1)} %dynamic-slice_bitcast_fusion.2), channel_id=1, source_target_pairs={{0,256},{256,0},{1,257},{257,1},{2,258},{258,2},{3,259},{259,3},{4... | collective-permute-start | bytes 110600 | tf_op jit(solution)/shard_map/ppermute | solution.py:124
  101.6 4.7 %collective-permute-start.9 = (bf16[96,192]{0,1:T(8,128)(2,1)S(1)}, bf16[96,192]{0,1:T(8,128)(2,1)S(1)}, u32[]{:S(2)}, u32[]{:S(2)}) collective-permute-start(bf16[96,192]{0,1:T(8,128)(2,1)S(1)} %bitcast.56), channel_id=1, source_target_pairs={{0,256},{256,0},{1,257},{257,1},{2,258},{258,2},{3,259},{259,3},{4... | collective-permute-start | bytes 110600 | tf_op jit(solution)/shard_map/ppermute | solution.py:123
  108.9 20.5 %all-to-all-done.2 = bf16[16,96,384]{2,1,0:T(8,128)(2,1)S(1)} async-done(((bf16[16,96,384]{2,1,0:T(8,128)(2,1)}), bf16[16,96,384]{2,1,0:T(8,128)(2,1)S(1)}, u32[]{:S(2)}, u32[]{:S(2)}) %all-to-all-start.2) | async-done | bytes 1179680 | tf_op jit(solution)/shard_map/all_to_all | solution.py:132
  (57 shorter events, 16.0 us)
Async XLA Ops:
  2.8 12.0 %copy-start.2 = (bf16[3072,96]{0,1:T(8,128)(2,1)S(1)}, bf16[3072,96]{0,1:T(8,128)(2,1)}, u32[]{:S(2)}) copy-start(bf16[3072,96]{0,1:T(8,128)(2,1)} %param.12) | copy-start | bytes 1769476
  2.9 48.5 %all-to-all-start = ((bf16[16,120,384]{2,1,0:T(8,128)(2,1)}), bf16[16,120,384]{2,1,0:T(8,128)(2,1)}, u32[]{:S(2)}, u32[]{:S(2)}) async-start(bf16[16,120,384]{2,1,0:T(8,128)(2,1)} %bitcast.3), calls=%async_computation | async-start | bytes 2949120 | tf_op jit(solution)/shard_map/all_to_all | solution.py:74
  14.8 7.0 %copy-start.1 = (bf16[512,768]{1,0:T(8,128)(2,1)S(1)}, bf16[512,768]{1,0:T(8,128)(2,1)}, u32[]{:S(2)}) copy-start(bf16[512,768]{1,0:T(8,128)(2,1)} %grad.1) | copy-start | bytes 2359300
  15.6 12.2 %collective-permute-start = (bf16[96,1536]{1,0:T(8,128)(2,1)}, bf16[96,1536]{1,0:T(8,128)(2,1)}, u32[]{:S(2)}, u32[]{:S(2)}) collective-permute-start(bf16[96,1536]{1,0:T(8,128)(2,1)} %get-tuple-element.26), channel_id=1, source_target_pairs={{0,256},{256,0},{1,257},{257,1},{2,258},{258,2},{3,259},{259,3},{4... | collective-permute-start | bytes 884744 | tf_op jit(solution)/shard_map/ppermute | solution.py:85
  20.3 2.0 %copy-start = (bf16[512,3072]{1,0:T(8,128)(2,1)S(1)}, bf16[512,3072]{1,0:T(8,128)(2,1)}, u32[]{:S(2)}) copy-start(bf16[512,3072]{1,0:T(8,128)(2,1)} %act.1) | copy-start | bytes 9437188
  25.0 6.8 %copy-start.6 = (f32[96]{0:T(128)S(1)}, f32[96]{0:T(128)}, u32[]{:S(2)}) copy-start(f32[96]{0:T(128)} %param.13) | copy-start | bytes 1156
  25.0 11.6 %collective-permute-start.2 = (bf16[8,192,384]{2,1,0:T(8,128)(2,1)S(1)}, bf16[8,192,384]{2,1,0:T(8,128)(2,1)}, u32[]{:S(2)}, u32[]{:S(2)}) collective-permute-start(bf16[8,192,384]{2,1,0:T(8,128)(2,1)S(1)} %get-tuple-element.16), channel_id=1, source_target_pairs={{0,16},{16,0},{1,17},{17,1},{2,18},{18,2},{3,19},{19,3},{4,20},{20... | collective-permute-start | bytes 3538952 | tf_op jit(solution)/shard_map/ppermute | solution.py:79
  28.9 7.5 %collective-permute-start.1 = (bf16[2,96,1536]{2,1,0:T(8,128)(2,1)S(1)}, bf16[2,96,1536]{2,1,0:T(8,128)(2,1)S(1)}, u32[]{:S(2)}, u32[]{:S(2)}) collective-permute-start(bf16[2,96,1536]{2,1,0:T(8,128)(2,1)S(1)} %maximum_select_fusion), channel_id=1, source_target_pairs={{0,16},{16,0},{1,17},{17,1},{2,18},{18,2},{3,19},{19,3},{4,20},{20... | collective-permute-start | bytes 1769480 | tf_op jit(solution)/shard_map/ppermute | solution.py:87
  31.8 7.4 %collective-permute-start.3 = (f32[96]{0:T(128)S(1)}, f32[96]{0:T(128)S(1)}, u32[]{:S(2)}, u32[]{:S(2)}) collective-permute-start(f32[96]{0:T(128)S(1)} %copy-done.6), channel_id=1, source_target_pairs={{0,256},{256,0},{1,257},{257,1},{2,258},{258,2},{3,259},{259,3},{4... | collective-permute-start | bytes 1160 | tf_op jit(solution)/shard_map/ppermute | solution.py:90
  54.6 10.4 %copy-start.5 = (f32[1,768]{1,0:T(1,128)S(1)}, f32[1,768]{1,0:T(1,128)}, u32[]{:S(2)}) copy-start(f32[1,768]{1,0:T(1,128)} %param.15) | copy-start | bytes 9220
  54.6 12.2 %collective-permute-start.6 = (bf16[384,384]{1,0:T(8,128)(2,1)S(1)}, bf16[384,384]{1,0:T(8,128)(2,1)}, u32[]{:S(2)}, u32[]{:S(2)}) collective-permute-start(bf16[384,384]{1,0:T(8,128)(2,1)S(1)} %bitcast.52), channel_id=1, source_target_pairs={{0,256},{256,0},{1,257},{257,1},{2,258},{258,2},{3,259},{259,3},{4... | collective-permute-start | bytes 884744 | tf_op jit(solution)/shard_map/ppermute | solution.py:95
  59.2 35.5 %all-to-all-start.1 = ((bf16[8,192,384]{2,1,0:T(8,128)(2,1)}), bf16[8,192,384]{2,1,0:T(8,128)(2,1)S(1)}, u32[]{:S(2)}, u32[]{:S(2)}) async-start(bf16[8,192,384]{2,1,0:T(8,128)(2,1)} %add_convert_fusion), calls=%async_computation.1 | async-start | bytes 2359296 | tf_op jit(solution)/shard_map/all_to_all | solution.py:118
  62.8 11.1 %collective-permute-start.4 = (bf16[384,384]{1,0:T(8,128)(2,1)S(1)}, bf16[384,384]{1,0:T(8,128)(2,1)S(1)}, u32[]{:S(2)}, u32[]{:S(2)}) collective-permute-start(bf16[384,384]{1,0:T(8,128)(2,1)S(1)} %get-tuple-element.19), channel_id=1, source_target_pairs={{0,256},{256,0},{1,257},{257,1},{2,258},{258,2},{3,259},{259,3},{4... | collective-permute-start | bytes 884744 | tf_op jit(solution)/shard_map/ppermute | solution.py:94
  68.9 9.8 %collective-permute-start.7 = (bf16[768,384]{1,0:T(8,128)(2,1)}, bf16[768,384]{1,0:T(8,128)(2,1)}, u32[]{:S(2)}, u32[]{:S(2)}) collective-permute-start(bf16[768,384]{1,0:T(8,128)(2,1)} %maximum_select_fusion.1), channel_id=1, source_target_pairs={{0,16},{16,0},{1,17},{17,1},{2,18},{18,2},{3,19},{19,3},{4,20},{20... | collective-permute-start | bytes 1769480 | tf_op jit(solution)/shard_map/ppermute | solution.py:97
  74.1 4.6 %collective-permute-start.5 = (bf16[192,384]{1,0:T(8,128)(2,1)S(1)}, bf16[192,384]{1,0:T(8,128)(2,1)S(1)}, u32[]{:S(2)}, u32[]{:S(2)}) collective-permute-start(bf16[192,384]{1,0:T(8,128)(2,1)S(1)} %get-tuple-element.30), channel_id=1, source_target_pairs={{0,16},{16,0},{1,17},{17,1},{2,18},{18,2},{3,19},{19,3},{4,20},{20... | collective-permute-start | bytes 442376 | tf_op jit(solution)/shard_map/ppermute | solution.py:100
  81.2 3.3 %collective-permute-start.8 = (bf16[192,384]{1,0:T(8,128)(2,1)S(1)}, bf16[192,384]{1,0:T(8,128)(2,1)S(1)}, u32[]{:S(2)}, u32[]{:S(2)}) collective-permute-start(bf16[192,384]{1,0:T(8,128)(2,1)S(1)} %get-tuple-element.28), channel_id=1, source_target_pairs={{0,16},{16,0},{1,17},{17,1},{2,18},{18,2},{3,19},{19,3},{4,20},{20... | collective-permute-start | bytes 442376 | tf_op jit(solution)/shard_map/ppermute | solution.py:115
  94.8 34.6 %all-to-all-start.2 = ((bf16[16,96,384]{2,1,0:T(8,128)(2,1)}), bf16[16,96,384]{2,1,0:T(8,128)(2,1)S(1)}, u32[]{:S(2)}, u32[]{:S(2)}) async-start(bf16[16,96,384]{2,1,0:T(8,128)(2,1)} %bitcast.17), calls=%async_computation.2 | async-start | bytes 2359296 | tf_op jit(solution)/shard_map/all_to_all | solution.py:132
  98.8 7.8 %copy-start.4 = (f32[1,24,768]{2,1,0:T(8,128)S(1)}, f32[1,24,768]{2,1,0:T(8,128)}, u32[]{:S(2)}) copy-start(f32[1,24,768]{2,1,0:T(8,128)} %param.17) | copy-start | bytes 221188
  98.9 9.3 %copy-start.3 = (f32[192,96]{1,0:T(8,128)S(1)}, f32[192,96]{1,0:T(8,128)}, u32[]{:S(2)}) copy-start(f32[192,96]{1,0:T(8,128)} %param.16) | copy-start | bytes 221188
  99.0 7.4 %collective-permute-start.10 = (bf16[2,24,384]{2,1,0:T(8,128)(2,1)S(1)}, bf16[2,24,384]{2,1,0:T(8,128)(2,1)S(1)}, u32[]{:S(2)}, u32[]{:S(2)}) collective-permute-start(bf16[2,24,384]{2,1,0:T(8,128)(2,1)S(1)} %dynamic-slice_bitcast_fusion.2), channel_id=1, source_target_pairs={{0,256},{256,0},{1,257},{257,1},{2,258},{258,2},{3,259},{259,3},{4... | collective-permute-start | bytes 110600 | tf_op jit(solution)/shard_map/ppermute | solution.py:124
  101.6 6.6 %collective-permute-start.9 = (bf16[96,192]{0,1:T(8,128)(2,1)S(1)}, bf16[96,192]{0,1:T(8,128)(2,1)S(1)}, u32[]{:S(2)}, u32[]{:S(2)}) collective-permute-start(bf16[96,192]{0,1:T(8,128)(2,1)S(1)} %bitcast.56), channel_id=1, source_target_pairs={{0,256},{256,0},{1,257},{257,1},{2,258},{258,2},{3,259},{259,3},{4... | collective-permute-start | bytes 110600 | tf_op jit(solution)/shard_map/ppermute | solution.py:123

commit v4 on v3

v4 whole, which is shorter than its diff:
```python
import jax
import jax.numpy as jnp
from jax import lax
from jax.experimental import pallas as pl
from jax.experimental.pallas import tpu as pltpu
from jax.sharding import Mesh, PartitionSpec as P

keep_rate = 0.95
damping = 0.03
swap = ((0, 1), (1, 0))
DP = ("xh", "z", "c")
MP = ("xl", "y")
bf16, f32 = jnp.bfloat16, jnp.float32


def dot(a, b, da, db):
    return lax.dot_general(a, b, (((da,), (db,)), ((), ())), preferred_element_type=f32)


def pick(a, index, axis):
    return lax.dynamic_index_in_dim(a, index, axis, keepdims=False)


def factor_kernel(place, act, sel, grad, mine, other, t_in, t_out):
    xh, c = place[0], place[1]
    for j in range(8):
        t_in[j * 384 : (j + 1) * 384, :] = dot(act[:, j * 384 : (j + 1) * 384], sel[...], 0, 0)
    for j in range(2):
        t_out[j * 384 : (j + 1) * 384, :] = dot(grad[:, j * 384 : (j + 1) * 384], grad[...], 0, 0)
    for target, core_at in ((mine, c), (other, 1 - c)):
        for side, half in ((0, xh), (1, 1 - xh)):
            for z in range(8):
                row = pl.multiple_of(half * 1536 + z * 192 + core_at * 96, 96)
                low, high = t_in[pl.ds(row, 48), :], t_in[pl.ds(pl.multiple_of(row + 48, 48), 48), :]
                target[z, side, 0:48, :] = jnp.concatenate([low, high], axis=1).astype(bf16)
                row = pl.multiple_of(half * 384 + z * 48 + core_at * 24, 24)
                part = t_out[pl.ds(row, 24), :]
                target[z, side, 48:96, :] = jnp.concatenate([part[:, :384], part[:, 384:]], axis=0).astype(bf16)


def factor_parts(place, act, sel, grad):
    vmem = pl.BlockSpec(memory_space=pltpu.VMEM)
    return pl.pallas_call(
        factor_kernel,
        out_shape=[jax.ShapeDtypeStruct((8, 2, 96, 384), bf16)] * 2,
        in_specs=[pl.BlockSpec(memory_space=pltpu.SMEM), vmem, vmem, vmem],
        out_specs=[vmem, vmem],
        scratch_shapes=[pltpu.VMEM((3072, 192), f32), pltpu.VMEM((768, 768), f32)],
        compiler_params=pltpu.CompilerParams(vmem_limit_bytes=32 * 1024 * 1024),
        cost_estimate=pl.CostEstimate(flops=1_250_000_000, bytes_accessed=8_000_000, transcendentals=0),
    )(place, act, sel, grad)


def left_kernel(near, far, came, eigen, wide, narrow, v, rows):
    for s in range(16):
        rows[s * 96 : (s + 1) * 96, :] = came[s, :96, :]
    for at, basis in ((0, near), (192, far)):
        left = dot(basis[...], rows[...], 1, 0)
        wide[at : at + 192, :] = left
        narrow[at : at + 192, :] = left.astype(bf16)
    for s in range(8):
        v[s * 48 : (s + 1) * 48, :] = came[2 * s : 2 * s + 2, 96:, :].reshape(48, 384)
    rest, parts = eigen[...], []
    for _ in range(3):
        parts.append(rest.astype(bf16).astype(f32))
        rest = rest - parts[-1]
    three = jnp.concatenate(parts + [jnp.zeros((13, 128), f32)], axis=0).astype(bf16)
    v[384:, :] = jnp.concatenate([three, jnp.zeros((16, 256), bf16)], axis=1)


def left_parts(near, far, came, eigen):
    vmem = pl.BlockSpec(memory_space=pltpu.VMEM)
    return pl.pallas_call(
        left_kernel,
        out_shape=[
            jax.ShapeDtypeStruct((384, 384), f32),
            jax.ShapeDtypeStruct((384, 384), bf16),
            jax.ShapeDtypeStruct((400, 384), bf16),
        ],
        in_specs=[vmem] * 4,
        out_specs=[vmem] * 3,
        scratch_shapes=[pltpu.VMEM((1536, 384), bf16)],
        compiler_params=pltpu.CompilerParams(vmem_limit_bytes=16 * 1024 * 1024),
        cost_estimate=pl.CostEstimate(flops=453_000_000, bytes_accessed=3_600_000, transcendentals=0),
    )(near, far, came, eigen)


def column(row):
    ids = lax.broadcasted_iota(jnp.int32, (96, 128), 0) == lax.broadcasted_iota(jnp.int32, (96, 128), 1)
    return jnp.sum(jnp.where(ids, jnp.broadcast_to(row, (96, 128)), 0.0), axis=1, keepdims=True)


def middle_kernel(place, near, far, near_v, far_v, near_v_core, far_v_core, eigen, eigen_out, keep, send):
    same = place[0] == place[1]
    first = jnp.where(same, near[...], far[...])
    second = jnp.where(same, far[...], near[...])
    three = far_v[384:, :128].astype(f32)
    mine, other = column(eigen[...]), column(three[0:1] + three[1:2] + three[2:3])
    low, high = jnp.concatenate([mine, other], axis=0), jnp.concatenate([other, mine], axis=0)
    eigen_rows = jnp.where(place[0] == 0, low, high)
    scaled = []
    for at, (v_first, v_second) in enumerate(((near_v, far_v), (near_v_core, far_v_core))):
        rotated = dot(first, v_first[:384, :], 1, 0) + dot(second, v_second[:384, :], 1, 0)
        denominator = eigen_rows * eigen_out[:, at * 384 : (at + 1) * 384] + damping
        scaled.append((rotated / denominator).astype(bf16))
    back_first = dot(scaled[0], near_v[:384, :], 1, 1) + dot(scaled[1], near_v_core[:384, :], 1, 1)
    back_second = dot(scaled[0], far_v[:384, :], 1, 1) + dot(scaled[1], far_v_core[:384, :], 1, 1)
    keep[...] = jnp.where(same, back_first, back_second).astype(bf16)
    send[...] = jnp.where(same, back_second, back_first).astype(bf16)


def middle(place, *arrays):
    vmem = pl.BlockSpec(memory_space=pltpu.VMEM)
    return pl.pallas_call(
        middle_kernel,
        out_shape=[jax.ShapeDtypeStruct((192, 384), bf16)] * 2,
        in_specs=[pl.BlockSpec(memory_space=pltpu.SMEM)] + [vmem] * len(arrays),
        out_specs=[vmem, vmem],
        compiler_params=pltpu.CompilerParams(vmem_limit_bytes=16 * 1024 * 1024),
        cost_estimate=pl.CostEstimate(flops=453_000_000, bytes_accessed=2_000_000, transcendentals=0),
    )(place, *arrays)


def out_kernel(near, far, keep, came, out):
    for j in range(4):
        part = dot(near[:, j * 384 : (j + 1) * 384], keep[...], 0, 0)
        part += dot(far[:, j * 384 : (j + 1) * 384], came[...], 0, 0)
        for i in range(4):
            out[j * 4 + i] = part[i * 96 : (i + 1) * 96, :].astype(bf16)


def out_parts_of(near, far, keep, came):
    vmem = pl.BlockSpec(memory_space=pltpu.VMEM)
    return pl.pallas_call(
        out_kernel,
        out_shape=jax.ShapeDtypeStruct((16, 96, 384), bf16),
        in_specs=[vmem] * 4,
        out_specs=vmem,
        compiler_params=pltpu.CompilerParams(vmem_limit_bytes=16 * 1024 * 1024),
        cost_estimate=pl.CostEstimate(flops=453_000_000, bytes_accessed=2_800_000, transcendentals=0),
    )(near, far, keep, came)


def per_device(
    activations,
    output_grad,
    weight_grad,
    input_basis,
    input_eigen,
    output_basis,
    output_eigen,
    input_factor,
    output_factor,
):
    xh, c = lax.axis_index("xh"), lax.axis_index("c")
    m = lax.axis_index(MP)
    tokens = activations.shape[0] * 32

    rows = jnp.concatenate([weight_grad, output_basis[0]], axis=0)
    halves = jnp.stack([rows[:, :384], rows[:, 384:]])
    send = jnp.broadcast_to(halves[None], (8, 2, 120, 384)).reshape(16, 120, 384)
    came_rows = lax.all_to_all(send, ("z", "c"), 0, 0)

    basis_in, _ = lax.optimization_barrier((input_basis, send))
    ut = basis_in.T
    ut_mine = lax.dynamic_slice_in_dim(ut, xh * 1536, 1536, 1)
    ut_other = lax.dynamic_slice_in_dim(ut, (1 - xh) * 1536, 1536, 1)
    ut_far = lax.ppermute(ut_other, "xh", swap)

    activations, _ = lax.optimization_barrier((activations, send))
    selected = lax.dynamic_slice_in_dim(activations, m * 192, 192, 1)
    place = jnp.stack([xh, c]).astype(jnp.int32)
    mine, other = factor_parts(place, activations, selected, output_grad)
    other, ut_far = lax.optimization_barrier((other, ut_far))
    came = lax.ppermute(other, "c", swap)
    pair = (mine.astype(f32) + came.astype(f32)).astype(bf16)

    near = jnp.where(xh == 0, jnp.stack([ut_mine, ut_far]), jnp.stack([ut_far, ut_mine]))
    near = near.reshape(192, 1536)
    far = lax.ppermute(near, "c", swap)

    came_rows, pair, far = lax.optimization_barrier((came_rows, pair, far))
    eigen = jnp.pad(input_eigen, (0, 32)).reshape(1, 128)
    left_part, left_send, v_near = left_parts(near, far, came_rows, eigen)
    left_came = lax.ppermute(left_send, "xh", swap)
    v_far = lax.ppermute(v_near, "xh", swap)
    left_half = (left_part + left_came.astype(f32)).astype(bf16)
    left_far = lax.ppermute(left_half[192:], "c", swap)
    v_far, _ = lax.optimization_barrier((v_far, left_far))
    v_near_core, v_far_core = lax.ppermute(v_near, "c", swap), lax.ppermute(v_far, "c", swap)
    eigen_out = jnp.where(c == 0, output_eigen, jnp.concatenate([output_eigen[:, 384:], output_eigen[:, :384]], axis=1))
    keep, send_back = middle(
        place, left_half[:192], left_far, v_near, v_far, v_near_core, v_far_core, eigen, eigen_out
    )
    back_far = lax.ppermute(send_back, "c", swap)
    out_part = out_parts_of(near, far, keep, back_far)

    came = lax.all_to_all(pair, "z", 0, 0)
    out_part, came = lax.optimization_barrier((out_part, came))
    sides = jnp.sum(came.astype(f32), axis=0)
    total = sides[0] + lax.ppermute(sides[1].astype(bf16), "xh", swap).astype(f32)
    in_total = total[:48].reshape(48, 2, 192).transpose(2, 1, 0).reshape(192, 96)
    out_total = jnp.concatenate([total[48:72], total[72:]], axis=1)[None]
    new_input = keep_rate * input_factor + (1.0 - keep_rate) * (in_total / tokens)
    new_output = keep_rate * output_factor + (1.0 - keep_rate) * (out_total / tokens)

    out_parts = lax.all_to_all(out_part, ("z", "c"), 0, 0).reshape(8, 2, 96, 384)
    total = jnp.sum(out_parts.astype(f32), axis=0).astype(bf16)
    result = jnp.concatenate([total[0], total[1]], axis=1)
    return (new_input, new_output, result)


def solution(mesh):
    fine = Mesh(mesh.devices.reshape(2, 8, 2, 2, 8), DP + MP)
    placed = (
        P(DP, None),
        P(DP, MP),
        P(DP, MP),
        P(None, DP),
        P(DP),
        P(MP, DP, None),
        P(MP, None),
        P(MP, DP),
        P(MP, DP, None),
    )
    return jax.shard_map(
        per_device,
        mesh=fine,
        in_specs=placed,
        out_specs=(P(MP, DP), P(MP, DP, None), P(DP, MP)),
        check_vma=False,
    )
```

time: 131 us -> 125 us (0.954)
  matrix products: 5.31 us -> 0 us
  Pallas kernels: 2.69 us -> 7.91 us
  starting transfers between devices: 55.8 us -> 52 us
  other arithmetic: 9.45 us -> 6.85 us
  waiting for transfers between devices: 48.8 us -> 50.4 us
    ppermute x6 -> x5, starting transfers between devices: 20.7 us -> 13.5 us  [the longest x1 4.68 us: per_device(): lax.ppermute(sides[1].astype(bf16), 'xh', swap).astype(f32)]
    all_to_all x1, waiting for transfers between devices: 8.27 us -> 1.75 us  [per_device(): came = lax.all_to_all(pair, 'z', 0, 0)]
    dot_general x3 -> x0, matrix products: 5.31 us -> none  [dot(): lax.dot_general(a, b, (((da,), (db,)), ((), ())), preferred_element_type=...]
    pallas_call x1 -> x4, Pallas kernels: 2.69 us -> 7.91 us  [the longest x1 3.4 us: factor_parts(): pl.pallas_call(factor_kernel, out_shape=[jax.ShapeDtypeStruct((8, 2, 96,...]
    all_to_all x1, waiting for transfers between devices: 12.2 us -> 16.1 us  [per_device(): came_rows = lax.all_to_all(send, ('z', 'c'), 0, 0)]
    unnamed x15 -> x20, local copies, waits for them, and re-layouts: 0.6 us -> 3.76 us
    ppermute x1, waiting for transfers between devices: 2.76 us -> 5.43 us  [per_device(): left_came = lax.ppermute(left_send, 'xh', swap)]
    ppermute x1, starting transfers between devices: 2.14 us -> 4.65 us  [per_device(): left_came = lax.ppermute(left_send, 'xh', swap)]
  transfers between devices with their start and end apart: 14 -> 13, of which waited for: 9 -> 9; matrix products, arithmetic and copies ran while one was open for 12% -> 6% of each run, Pallas kernels for 2% -> 6%
where the time goes in v4:
time: 125 us
  starting transfers between devices  52 us (42%)
  waiting for transfers between devices  50.4 us (40%)
  Pallas kernels  7.91 us (6%)
  other arithmetic  6.85 us (5%)
  local copies, waits for them, and re-layouts  6.4 us (5%)
    all_to_all x1, waiting for transfers between devices, per_device(): lax.all_to_all(out_part, ('z', 'c'), 0, 0).reshape(8, 2, 96, 384)  20.2 us
    all_to_all x1, waiting for transfers between devices, per_device(): came_rows = lax.all_to_all(send, ('z', 'c'), 0, 0)  16.1 us
    all_to_all x1, starting transfers between devices, per_device(): came_rows = lax.all_to_all(send, ('z', 'c'), 0, 0)  12 us
    all_to_all x1, starting transfers between devices, per_device(): lax.all_to_all(out_part, ('z', 'c'), 0, 0).reshape(8, 2, 96, 384)  5.44 us
    ppermute x1, waiting for transfers between devices, per_device(): left_came = lax.ppermute(left_send, 'xh', swap)  5.43 us
    ppermute x1, starting transfers between devices, per_device(): ut_far = lax.ppermute(ut_other, 'xh', swap)  4.81 us
    ppermute x1, starting transfers between devices, per_device(): lax.ppermute(sides[1].astype(bf16), 'xh', swap).astype(f32)  4.68 us
    ppermute x1, starting transfers between devices, per_device(): left_came = lax.ppermute(left_send, 'xh', swap)  4.65 us
  transfers between devices with their start and end apart: 13, of which 9 were waited for; matrix products, arithmetic and copies ran while one was open for 6% of the time, Pallas kernels for 6%

profile of v4, /device:TPU:1, one launch (start us, length us, event | category | flops | bytes accessed | tf_op | source)
XLA Modules:
  0.0 124.5 jit_solution(12734166987560657996)
XLA Ops:
  2.9 12.0 %all-to-all-start = ((bf16[16,120,384]{2,1,0:T(8,128)(2,1)}), bf16[16,120,384]{2,1,0:T(8,128)(2,1)S(1)}, u32[]{:S(2)}, u32[]{:S(2)}) async-start(bf16[16,120,384]{2,1,0:T(8,128)(2,1)} %bitcast.3), calls=%async_computation | async-start | bytes 2949120 | tf_op jit(solution)/shard_map/all_to_all | solution.py:162
  14.9 4.8 %collective-permute-start = (bf16[96,1536]{1,0:T(8,128)(2,1)S(1)}, bf16[96,1536]{1,0:T(8,128)(2,1)S(1)}, u32[]{:S(2)}, u32[]{:S(2)}) collective-permute-start(bf16[96,1536]{1,0:T(8,128)(2,1)S(1)} %get-tuple-element.44), channel_id=1, source_target_pairs={{0,256},{256,0},{1,257},{257,1},{2,258},{258,2},{3,259},{259,3},{4... | collective-permute-start | bytes 884744 | tf_op jit(solution)/shard_map/ppermute | solution.py:168
  21.0 1.9 %copy-done.2 = bf16[512,3072]{1,0:T(8,128)(2,1)S(1)} copy-done((bf16[512,3072]{1,0:T(8,128)(2,1)S(1)}, bf16[512,3072]{1,0:T(8,128)(2,1)}, u32[]{:S(2)}) %copy-start.2) | copy-done | bytes 3145752
  22.9 3.4 %shard_map.112 = (bf16[8,2,96,384]{3,2,1,0:T(8,128)(2,1)S(1)}, bf16[8,2,96,384]{3,2,1,0:T(8,128)(2,1)}) custom-call(s32[2]{0:T(128)S(1)} %pad_add_fusion.place, bf16[512,3072]{1,0:T(8,128)(2,1)S(1)} %copy-done.2, bf16[512,192]{1,0:T(8,128)(2,1)S(1)} %constant_dynamic-slice_fusion.sel, bf16[512,768]{1,0:T(8,128)(2,1)S(1)} %copy-done.3), custom_call_target="tpu_custom_call" | custom-call | flops 1250000000 | bytes 8000000 | tf_op jit(solution)/shard_map/pallas_call | solution.py:43
  27.3 2.5 %collective-permute-start.1 = (bf16[8,2,96,384]{3,2,1,0:T(8,128)(2,1)}, bf16[8,2,96,384]{3,2,1,0:T(8,128)(2,1)}, u32[]{:S(2)}, u32[]{:S(2)}) collective-permute-start(bf16[8,2,96,384]{3,2,1,0:T(8,128)(2,1)} %get-tuple-element.25), channel_id=1, source_target_pairs={{0,16},{16,0},{1,17},{17,1},{2,18},{18,2},{3,19},{19,3},{4,20},{20... | collective-permute-start | bytes 3538952 | tf_op jit(solution)/shard_map/ppermute | solution.py:175
  29.9 2.1 %collective-permute-start.2 = (bf16[192,1536]{1,0:T(8,128)(2,1)S(1)}, bf16[192,1536]{1,0:T(8,128)(2,1)S(1)}, u32[]{:S(2)}, u32[]{:S(2)}) collective-permute-start(bf16[192,1536]{1,0:T(8,128)(2,1)S(1)} %bitcast.36), channel_id=1, source_target_pairs={{0,16},{16,0},{1,17},{17,1},{2,18},{18,2},{3,19},{19,3},{4,20},{20... | collective-permute-start | bytes 1769480 | tf_op jit(solution)/shard_map/ppermute | solution.py:180
  32.6 2.6 %add_convert_fusion = bf16[8,2,96,384]{3,2,1,0:T(8,128)(2,1)} fusion(bf16[8,2,96,384]{3,2,1,0:T(8,128)(2,1)} %collective-permute-done.1, bf16[8,2,96,384]{3,2,1,0:T(8,128)(2,1)S(1)} %copy-done.1), kind=kLoop, calls=%fused_computation.1 | loop fusion | flops 2359296 | bytes 3538944 | tf_op jit(solution)/shard_map/convert_element_type | solution.py:176
  35.2 16.1 %all-to-all-done.came = bf16[16,120,384]{2,1,0:T(8,128)(2,1)S(1)} async-done(((bf16[16,120,384]{2,1,0:T(8,128)(2,1)}), bf16[16,120,384]{2,1,0:T(8,128)(2,1)S(1)}, u32[]{:S(2)}, u32[]{:S(2)}) %all-to-all-start) | async-done | bytes 1474592 | tf_op jit(solution)/shard_map/all_to_all | solution.py:162
  51.3 4.3 %all-to-all-start.1 = ((bf16[8,2,96,384]{3,2,1,0:T(8,128)(2,1)}), bf16[8,2,96,384]{3,2,1,0:T(8,128)(2,1)}, u32[]{:S(2)}, u32[]{:S(2)}) async-start(bf16[8,2,96,384]{3,2,1,0:T(8,128)(2,1)} %add_convert_fusion), calls=%async_computation.1 | async-start | bytes 2359296 | tf_op jit(solution)/shard_map/all_to_all | solution.py:198
  56.4 4.7 %collective-permute-start.3 = (bf16[384,384]{1,0:T(8,128)(2,1)S(1)}, bf16[384,384]{1,0:T(8,128)(2,1)S(1)}, u32[]{:S(2)}, u32[]{:S(2)}) collective-permute-start(bf16[384,384]{1,0:T(8,128)(2,1)S(1)} %get-tuple-element.29), channel_id=1, source_target_pairs={{0,256},{256,0},{1,257},{257,1},{2,258},{258,2},{3,259},{259,3},{4... | collective-permute-start | bytes 884744 | tf_op jit(solution)/shard_map/ppermute | solution.py:185
  61.1 2.1 %collective-permute-start.5 = (bf16[400,384]{1,0:T(8,128)(2,1)S(1)}, bf16[400,384]{1,0:T(8,128)(2,1)S(1)}, u32[]{:S(2)}, u32[]{:S(2)}) collective-permute-start(bf16[400,384]{1,0:T(8,128)(2,1)S(1)} %get-tuple-element.30.near_v), channel_id=1, source_target_pairs={{0,256},{256,0},{1,257},{257,1},{2,258},{258,2},{3,259},{259,3},{4... | collective-permute-start | bytes 921608 | tf_op jit(solution)/shard_map/ppermute | solution.py:186
  63.2 5.4 %collective-permute-done.3 = bf16[384,384]{1,0:T(8,128)(2,1)S(1)} collective-permute-done((bf16[384,384]{1,0:T(8,128)(2,1)S(1)}, bf16[384,384]{1,0:T(8,128)(2,1)S(1)}, u32[]{:S(2)}, u32[]{:S(2)}) %collective-permute-start.3) | collective-permute-done | bytes 294944 | tf_op jit(solution)/shard_map/ppermute | solution.py:185
  68.8 2.8 %collective-permute-start.4 = (bf16[192,384]{1,0:T(8,128)(2,1)S(1)}, bf16[192,384]{1,0:T(8,128)(2,1)S(1)}, u32[]{:S(2)}, u32[]{:S(2)}) collective-permute-start(bf16[192,384]{1,0:T(8,128)(2,1)S(1)} %get-tuple-element.45), channel_id=1, source_target_pairs={{0,16},{16,0},{1,17},{17,1},{2,18},{18,2},{3,19},{19,3},{4,20},{20... | collective-permute-start | bytes 442376 | tf_op jit(solution)/shard_map/ppermute | solution.py:188
  71.6 1.9 %collective-permute-start.6 = (bf16[400,384]{1,0:T(8,128)(2,1)S(1)}, bf16[400,384]{1,0:T(8,128)(2,1)S(1)}, u32[]{:S(2)}, u32[]{:S(2)}) collective-permute-start(bf16[400,384]{1,0:T(8,128)(2,1)S(1)} %get-tuple-element.30.near_v), channel_id=1, source_target_pairs={{0,16},{16,0},{1,17},{17,1},{2,18},{18,2},{3,19},{19,3},{4,20},{20... | collective-permute-start | bytes 921608 | tf_op jit(solution)/shard_map/ppermute | solution.py:190
  73.5 1.7 %collective-permute-done.5.far_v = bf16[400,384]{1,0:T(8,128)(2,1)S(1)} collective-permute-done((bf16[400,384]{1,0:T(8,128)(2,1)S(1)}, bf16[400,384]{1,0:T(8,128)(2,1)S(1)}, u32[]{:S(2)}, u32[]{:S(2)}) %collective-permute-start.5) | collective-permute-done | bytes 307232 | tf_op jit(solution)/shard_map/ppermute | solution.py:186
  75.2 2.5 %collective-permute-start.7 = (bf16[400,384]{1,0:T(8,128)(2,1)S(1)}, bf16[400,384]{1,0:T(8,128)(2,1)S(1)}, u32[]{:S(2)}, u32[]{:S(2)}) collective-permute-start(bf16[400,384]{1,0:T(8,128)(2,1)S(1)} %collective-permute-done.5.far_v), channel_id=1, source_target_pairs={{0,16},{16,0},{1,17},{17,1},{2,18},{18,2},{3,19},{19,3},{4,20},{20... | collective-permute-start | bytes 921608 | tf_op jit(solution)/shard_map/ppermute | solution.py:190
  78.9 1.6 %shard_map.114 = (bf16[192,384]{1,0:T(8,128)(2,1)S(1)}, bf16[192,384]{1,0:T(8,128)(2,1)S(1)}) custom-call(s32[2]{0:T(128)S(1)} %pad_add_fusion.place, bf16[192,384]{1,0:T(8,128)(2,1)S(1)} %get-tuple-element.46.near, bf16[192,384]{1,0:T(8,128)(2,1)S(1)} %collective-permute-done.4.far, bf16[400,384]{1,0:T(8,128)(2,1)S(1)} %get-tuple-element.30.near_v, ...), custom_call_target="tpu_custom_call" | custom-call | flops 453000000 | bytes 2000000 | tf_op jit(solution)/shard_map/pallas_call | solution.py:114
  80.6 2.3 %collective-permute-start.8 = (bf16[192,384]{1,0:T(8,128)(2,1)S(1)}, bf16[192,384]{1,0:T(8,128)(2,1)S(1)}, u32[]{:S(2)}, u32[]{:S(2)}) collective-permute-start(bf16[192,384]{1,0:T(8,128)(2,1)S(1)} %get-tuple-element.33), channel_id=1, source_target_pairs={{0,16},{16,0},{1,17},{17,1},{2,18},{18,2},{3,19},{19,3},{4,20},{20... | collective-permute-start | bytes 442376 | tf_op jit(solution)/shard_map/ppermute | solution.py:195
  83.9 2.1 %shard_map.115 = bf16[16,96,384]{2,1,0:T(8,128)(2,1)} custom-call(bf16[192,1536]{1,0:T(8,128)(2,1)S(1)} %bitcast.38, bf16[192,1536]{1,0:T(8,128)(2,1)S(1)} %collective-permute-done.2.far, bf16[192,384]{1,0:T(8,128)(2,1)S(1)} %get-tuple-element.32.keep, bf16[192,384]{1,0:T(8,128)(2,1)S(1)} %collective-permute-done.8.came), custom_call_target="tpu_custom_call" | custom-call | flops 453000000 | bytes 2800000 | tf_op jit(solution)/shard_map/pallas_call | solution.py:134
  85.9 1.8 %all-to-all-done.1 = bf16[8,2,96,384]{3,2,1,0:T(8,128)(2,1)} async-done(((bf16[8,2,96,384]{3,2,1,0:T(8,128)(2,1)}), bf16[8,2,96,384]{3,2,1,0:T(8,128)(2,1)}, u32[]{:S(2)}, u32[]{:S(2)}) %all-to-all-start.1) | async-done | bytes 1179680 | tf_op jit(solution)/shard_map/all_to_all | solution.py:198
  87.7 5.4 %all-to-all-start.2 = ((bf16[16,96,384]{2,1,0:T(8,128)(2,1)}), bf16[16,96,384]{2,1,0:T(8,128)(2,1)S(1)}, u32[]{:S(2)}, u32[]{:S(2)}) async-start(bf16[16,96,384]{2,1,0:T(8,128)(2,1)} %shard_map.115), calls=%async_computation.2 | async-start | bytes 2359296 | tf_op jit(solution)/shard_map/all_to_all | solution.py:207
  94.6 4.7 %collective-permute-start.9 = (bf16[96,384]{1,0:T(8,128)(2,1)S(1)}, bf16[96,384]{1,0:T(8,128)(2,1)S(1)}, u32[]{:S(2)}, u32[]{:S(2)}) collective-permute-start(bf16[96,384]{1,0:T(8,128)(2,1)S(1)} %fusion.4), channel_id=1, source_target_pairs={{0,256},{256,0},{1,257},{257,1},{2,258},{258,2},{3,259},{259,3},{4... | collective-permute-start | bytes 221192 | tf_op jit(solution)/shard_map/ppermute | solution.py:201
  99.4 2.4 %collective-permute-done.9 = bf16[96,384]{1,0:T(8,128)(2,1)S(1)} collective-permute-done((bf16[96,384]{1,0:T(8,128)(2,1)S(1)}, bf16[96,384]{1,0:T(8,128)(2,1)S(1)}, u32[]{:S(2)}, u32[]{:S(2)}) %collective-permute-start.9) | collective-permute-done | bytes 73760 | tf_op jit(solution)/shard_map/ppermute | solution.py:201
  103.5 20.2 %all-to-all-done.2 = bf16[16,96,384]{2,1,0:T(8,128)(2,1)S(1)} async-done(((bf16[16,96,384]{2,1,0:T(8,128)(2,1)}), bf16[16,96,384]{2,1,0:T(8,128)(2,1)S(1)}, u32[]{:S(2)}, u32[]{:S(2)}) %all-to-all-start.2) | async-done | bytes 1179680 | tf_op jit(solution)/shard_map/all_to_all | solution.py:207
  (51 shorter events, 12.3 us)
Async XLA Ops:
  2.9 12.0 %copy-start.4 = (bf16[3072,96]{0,1:T(8,128)(2,1)S(1)}, bf16[3072,96]{0,1:T(8,128)(2,1)}, u32[]{:S(2)}) copy-start(bf16[3072,96]{0,1:T(8,128)(2,1)} %param.12) | copy-start | bytes 1769476
  2.9 48.4 %all-to-all-start = ((bf16[16,120,384]{2,1,0:T(8,128)(2,1)}), bf16[16,120,384]{2,1,0:T(8,128)(2,1)S(1)}, u32[]{:S(2)}, u32[]{:S(2)}) async-start(bf16[16,120,384]{2,1,0:T(8,128)(2,1)} %bitcast.3), calls=%async_computation | async-start | bytes 2949120 | tf_op jit(solution)/shard_map/all_to_all | solution.py:162
  14.8 6.1 %copy-start.3 = (bf16[512,768]{1,0:T(8,128)(2,1)S(1)}, bf16[512,768]{1,0:T(8,128)(2,1)}, u32[]{:S(2)}) copy-start(bf16[512,768]{1,0:T(8,128)(2,1)} %grad.1) | copy-start | bytes 2359300
  14.9 12.4 %collective-permute-start = (bf16[96,1536]{1,0:T(8,128)(2,1)S(1)}, bf16[96,1536]{1,0:T(8,128)(2,1)S(1)}, u32[]{:S(2)}, u32[]{:S(2)}) collective-permute-start(bf16[96,1536]{1,0:T(8,128)(2,1)S(1)} %get-tuple-element.44), channel_id=1, source_target_pairs={{0,256},{256,0},{1,257},{257,1},{2,258},{258,2},{3,259},{259,3},{4... | collective-permute-start | bytes 884744 | tf_op jit(solution)/shard_map/ppermute | solution.py:168
  21.0 1.9 %copy-start.2 = (bf16[512,3072]{1,0:T(8,128)(2,1)S(1)}, bf16[512,3072]{1,0:T(8,128)(2,1)}, u32[]{:S(2)}) copy-start(bf16[512,3072]{1,0:T(8,128)(2,1)} %act) | copy-start | bytes 9437188
  26.3 1.0 copy-start
  27.3 5.3 %collective-permute-start.1 = (bf16[8,2,96,384]{3,2,1,0:T(8,128)(2,1)}, bf16[8,2,96,384]{3,2,1,0:T(8,128)(2,1)}, u32[]{:S(2)}, u32[]{:S(2)}) collective-permute-start(bf16[8,2,96,384]{3,2,1,0:T(8,128)(2,1)} %get-tuple-element.25), channel_id=1, source_target_pairs={{0,16},{16,0},{1,17},{17,1},{2,18},{18,2},{3,19},{19,3},{4,20},{20... | collective-permute-start | bytes 3538952 | tf_op jit(solution)/shard_map/ppermute | solution.py:175
  29.8 2.8 %copy-start.1 = (bf16[8,2,96,384]{3,2,1,0:T(8,128)(2,1)S(1)}, bf16[8,2,96,384]{3,2,1,0:T(8,128)(2,1)}, u32[]{:S(2)}) copy-start(bf16[8,2,96,384]{3,2,1,0:T(8,128)(2,1)} %copy-done) | copy-start | bytes 3538948
  29.9 5.3 %collective-permute-start.2 = (bf16[192,1536]{1,0:T(8,128)(2,1)S(1)}, bf16[192,1536]{1,0:T(8,128)(2,1)S(1)}, u32[]{:S(2)}, u32[]{:S(2)}) collective-permute-start(bf16[192,1536]{1,0:T(8,128)(2,1)S(1)} %bitcast.36), channel_id=1, source_target_pairs={{0,16},{16,0},{1,17},{17,1},{2,18},{18,2},{3,19},{19,3},{4,20},{20... | collective-permute-start | bytes 1769480 | tf_op jit(solution)/shard_map/ppermute | solution.py:180
  35.2 20.4 %copy-start.8 = (f32[96]{0:T(128)S(1)}, f32[96]{0:T(128)}, u32[]{:S(2)}) copy-start(f32[96]{0:T(128)} %param.13) | copy-start | bytes 1156
  51.3 36.4 %all-to-all-start.1 = ((bf16[8,2,96,384]{3,2,1,0:T(8,128)(2,1)}), bf16[8,2,96,384]{3,2,1,0:T(8,128)(2,1)}, u32[]{:S(2)}, u32[]{:S(2)}) async-start(bf16[8,2,96,384]{3,2,1,0:T(8,128)(2,1)} %add_convert_fusion), calls=%async_computation.1 | async-start | bytes 2359296 | tf_op jit(solution)/shard_map/all_to_all | solution.py:198
  56.4 21.3 %copy-start.7 = (f32[1,768]{1,0:T(1,128)S(1)}, f32[1,768]{1,0:T(1,128)}, u32[]{:S(2)}) copy-start(f32[1,768]{1,0:T(1,128)} %param.15) | copy-start | bytes 9220
  56.4 12.2 %collective-permute-start.3 = (bf16[384,384]{1,0:T(8,128)(2,1)S(1)}, bf16[384,384]{1,0:T(8,128)(2,1)S(1)}, u32[]{:S(2)}, u32[]{:S(2)}) collective-permute-start(bf16[384,384]{1,0:T(8,128)(2,1)S(1)} %get-tuple-element.29), channel_id=1, source_target_pairs={{0,256},{256,0},{1,257},{257,1},{2,258},{258,2},{3,259},{259,3},{4... | collective-permute-start | bytes 884744 | tf_op jit(solution)/shard_map/ppermute | solution.py:185
  61.1 14.2 %collective-permute-start.5 = (bf16[400,384]{1,0:T(8,128)(2,1)S(1)}, bf16[400,384]{1,0:T(8,128)(2,1)S(1)}, u32[]{:S(2)}, u32[]{:S(2)}) collective-permute-start(bf16[400,384]{1,0:T(8,128)(2,1)S(1)} %get-tuple-element.30.near_v), channel_id=1, source_target_pairs={{0,256},{256,0},{1,257},{257,1},{2,258},{258,2},{3,259},{259,3},{4... | collective-permute-start | bytes 921608 | tf_op jit(solution)/shard_map/ppermute | solution.py:186
  68.8 6.5 %collective-permute-start.4 = (bf16[192,384]{1,0:T(8,128)(2,1)S(1)}, bf16[192,384]{1,0:T(8,128)(2,1)S(1)}, u32[]{:S(2)}, u32[]{:S(2)}) collective-permute-start(bf16[192,384]{1,0:T(8,128)(2,1)S(1)} %get-tuple-element.45), channel_id=1, source_target_pairs={{0,16},{16,0},{1,17},{17,1},{2,18},{18,2},{3,19},{19,3},{4,20},{20... | collective-permute-start | bytes 442376 | tf_op jit(solution)/shard_map/ppermute | solution.py:188
  71.6 6.2 %collective-permute-start.6 = (bf16[400,384]{1,0:T(8,128)(2,1)S(1)}, bf16[400,384]{1,0:T(8,128)(2,1)S(1)}, u32[]{:S(2)}, u32[]{:S(2)}) collective-permute-start(bf16[400,384]{1,0:T(8,128)(2,1)S(1)} %get-tuple-element.30.near_v), channel_id=1, source_target_pairs={{0,16},{16,0},{1,17},{17,1},{2,18},{18,2},{3,19},{19,3},{4,20},{20... | collective-permute-start | bytes 921608 | tf_op jit(solution)/shard_map/ppermute | solution.py:190
  75.2 3.7 %collective-permute-start.7 = (bf16[400,384]{1,0:T(8,128)(2,1)S(1)}, bf16[400,384]{1,0:T(8,128)(2,1)S(1)}, u32[]{:S(2)}, u32[]{:S(2)}) collective-permute-start(bf16[400,384]{1,0:T(8,128)(2,1)S(1)} %collective-permute-done.5.far_v), channel_id=1, source_target_pairs={{0,16},{16,0},{1,17},{17,1},{2,18},{18,2},{3,19},{19,3},{4,20},{20... | collective-permute-start | bytes 921608 | tf_op jit(solution)/shard_map/ppermute | solution.py:190
  80.6 3.3 %collective-permute-start.8 = (bf16[192,384]{1,0:T(8,128)(2,1)S(1)}, bf16[192,384]{1,0:T(8,128)(2,1)S(1)}, u32[]{:S(2)}, u32[]{:S(2)}) collective-permute-start(bf16[192,384]{1,0:T(8,128)(2,1)S(1)} %get-tuple-element.33), channel_id=1, source_target_pairs={{0,16},{16,0},{1,17},{17,1},{2,18},{18,2},{3,19},{19,3},{4,20},{20... | collective-permute-start | bytes 442376 | tf_op jit(solution)/shard_map/ppermute | solution.py:195
  87.7 36.0 %all-to-all-start.2 = ((bf16[16,96,384]{2,1,0:T(8,128)(2,1)}), bf16[16,96,384]{2,1,0:T(8,128)(2,1)S(1)}, u32[]{:S(2)}, u32[]{:S(2)}) async-start(bf16[16,96,384]{2,1,0:T(8,128)(2,1)} %shard_map.115), calls=%async_computation.2 | async-start | bytes 2359296 | tf_op jit(solution)/shard_map/all_to_all | solution.py:207
  93.1 6.2 %copy-start.5 = (f32[192,96]{1,0:T(8,128)S(1)}, f32[192,96]{1,0:T(8,128)}, u32[]{:S(2)}) copy-start(f32[192,96]{1,0:T(8,128)} %param.16) | copy-start | bytes 221188
  94.6 8.2 %copy-start.6 = (f32[1,24,768]{2,1,0:T(8,128)S(1)}, f32[1,24,768]{2,1,0:T(8,128)}, u32[]{:S(2)}) copy-start(f32[1,24,768]{2,1,0:T(8,128)} %param.17) | copy-start | bytes 221188
  94.6 7.2 %collective-permute-start.9 = (bf16[96,384]{1,0:T(8,128)(2,1)S(1)}, bf16[96,384]{1,0:T(8,128)(2,1)S(1)}, u32[]{:S(2)}, u32[]{:S(2)}) collective-permute-start(bf16[96,384]{1,0:T(8,128)(2,1)S(1)} %fusion.4), channel_id=1, source_target_pairs={{0,256},{256,0},{1,257},{257,1},{2,258},{258,2},{3,259},{259,3},{4... | collective-permute-start | bytes 221192 | tf_op jit(solution)/shard_map/ppermute | solution.py:201

commit v5 on v4

--- a/solution.py
+++ b/solution.py
@@ -32,17 +32,17 @@
             for z in range(8):
                 row = pl.multiple_of(half * 1536 + z * 192 + core_at * 96, 96)
                 low, high = t_in[pl.ds(row, 48), :], t_in[pl.ds(pl.multiple_of(row + 48, 48), 48), :]
-                target[z, side, 0:48, :] = jnp.concatenate([low, high], axis=1).astype(bf16)
+                target[side, z, 0:48, :] = jnp.concatenate([low, high], axis=1).astype(bf16)
                 row = pl.multiple_of(half * 384 + z * 48 + core_at * 24, 24)
                 part = t_out[pl.ds(row, 24), :]
-                target[z, side, 48:96, :] = jnp.concatenate([part[:, :384], part[:, 384:]], axis=0).astype(bf16)
+                target[side, z, 48:96, :] = jnp.concatenate([part[:, :384], part[:, 384:]], axis=0).astype(bf16)
 
 
 def factor_parts(place, act, sel, grad):
     vmem = pl.BlockSpec(memory_space=pltpu.VMEM)
     return pl.pallas_call(
         factor_kernel,
-        out_shape=[jax.ShapeDtypeStruct((8, 2, 96, 384), bf16)] * 2,
+        out_shape=[jax.ShapeDtypeStruct((2, 8, 96, 384), bf16)] * 2,
         in_specs=[pl.BlockSpec(memory_space=pltpu.SMEM), vmem, vmem, vmem],
         out_specs=[vmem, vmem],
         scratch_shapes=[pltpu.VMEM((3072, 192), f32), pltpu.VMEM((768, 768), f32)],
@@ -90,55 +90,44 @@
     return jnp.sum(jnp.where(ids, jnp.broadcast_to(row, (96, 128)), 0.0), axis=1, keepdims=True)
 
 
-def middle_kernel(place, near, far, near_v, far_v, near_v_core, far_v_core, eigen, eigen_out, keep, send):
+def tail_kernel(place, left, left_core, near_v, far_v, near_v_core, far_v_core, eigen, eigen_out, near, far, out):
     same = place[0] == place[1]
-    first = jnp.where(same, near[...], far[...])
-    second = jnp.where(same, far[...], near[...])
-    three = far_v[384:, :128].astype(f32)
-    mine, other = column(eigen[...]), column(three[0:1] + three[1:2] + three[2:3])
-    low, high = jnp.concatenate([mine, other], axis=0), jnp.concatenate([other, mine], axis=0)
-    eigen_rows = jnp.where(place[0] == 0, low, high)
-    scaled = []
-    for at, (v_first, v_second) in enumerate(((near_v, far_v), (near_v_core, far_v_core))):
-        rotated = dot(first, v_first[:384, :], 1, 0) + dot(second, v_second[:384, :], 1, 0)
-        denominator = eigen_rows * eigen_out[:, at * 384 : (at + 1) * 384] + damping
-        scaled.append((rotated / denominator).astype(bf16))
-    back_first = dot(scaled[0], near_v[:384, :], 1, 1) + dot(scaled[1], near_v_core[:384, :], 1, 1)
-    back_second = dot(scaled[0], far_v[:384, :], 1, 1) + dot(scaled[1], far_v_core[:384, :], 1, 1)
-    keep[...] = jnp.where(same, back_first, back_second).astype(bf16)
-    send[...] = jnp.where(same, back_second, back_first).astype(bf16)
-
-
-def middle(place, *arrays):
+
+    def third(v):
+        three = v[384:, :128].astype(f32)
+        return column(three[0:1] + three[1:2] + three[2:3])
+
+    half_first = jnp.where(same, near_v[:384, :], far_v[:384, :])
+    half_second = jnp.where(same, near_v_core[:384, :], far_v_core[:384, :])
+    backs = []
+    for r, (mine, other) in enumerate(((column(eigen[...]), third(far_v)), (third(near_v_core), third(far_v_core)))):
+        low, high = jnp.concatenate([mine, other], axis=0), jnp.concatenate([other, mine], axis=0)
+        eigen_rows = jnp.where(place[0] == 0, low, high)
+        own, came = left[r * 192 : (r + 1) * 192, :], left_core[(1 - r) * 192 : (2 - r) * 192, :]
+        first, second = jnp.where(same, own, came), jnp.where(same, came, own)
+        scaled = []
+        for at, (v_first, v_second) in enumerate(((near_v, far_v), (near_v_core, far_v_core))):
+            rotated = dot(first, v_first[:384, :], 1, 0) + dot(second, v_second[:384, :], 1, 0)
+            denominator = eigen_rows * eigen_out[:, at * 384 : (at + 1) * 384] + damping
+            scaled.append((rotated / denominator).astype(bf16))
+        backs.append((dot(scaled[0], half_first, 1, 1) + dot(scaled[1], half_second, 1, 1)).astype(bf16))
+    for j in range(4):
+        part = dot(near[:, j * 384 : (j + 1) * 384], backs[0], 0, 0)
+        part += dot(far[:, j * 384 : (j + 1) * 384], backs[1], 0, 0)
+        for i in range(4):
+            out[j * 4 + i] = part[i * 96 : (i + 1) * 96, :].astype(bf16)
+
+
+def tail(place, *arrays):
     vmem = pl.BlockSpec(memory_space=pltpu.VMEM)
     return pl.pallas_call(
-        middle_kernel,
-        out_shape=[jax.ShapeDtypeStruct((192, 384), bf16)] * 2,
+        tail_kernel,
+        out_shape=jax.ShapeDtypeStruct((16, 96, 384), bf16),
         in_specs=[pl.BlockSpec(memory_space=pltpu.SMEM)] + [vmem] * len(arrays),
-        out_specs=[vmem, vmem],
-        compiler_params=pltpu.CompilerParams(vmem_limit_bytes=16 * 1024 * 1024),
-        cost_estimate=pl.CostEstimate(flops=453_000_000, bytes_accessed=2_000_000, transcendentals=0),
+        out_specs=vmem,
+        compiler_params=pltpu.CompilerParams(vmem_limit_bytes=24 * 1024 * 1024),
+        cost_estimate=pl.CostEstimate(flops=1_130_000_000, bytes_accessed=4_800_000, transcendentals=0),
     )(place, *arrays)
-
-
-def out_kernel(near, far, keep, came, out):
-    for j in range(4):
-        part = dot(near[:, j * 384 : (j + 1) * 384], keep[...], 0, 0)
-        part += dot(far[:, j * 384 : (j + 1) * 384], came[...], 0, 0)
-        for i in range(4):
-            out[j * 4 + i] = part[i * 96 : (i + 1) * 96, :].astype(bf16)
-
-
-def out_parts_of(near, far, keep, came):
-    vmem = pl.BlockSpec(memory_space=pltpu.VMEM)
-    return pl.pallas_call(
-        out_kernel,
-        out_shape=jax.ShapeDtypeStruct((16, 96, 384), bf16),
-        in_specs=[vmem] * 4,
-        out_specs=vmem,
-        compiler_params=pltpu.CompilerParams(vmem_limit_bytes=16 * 1024 * 1024),
-        cost_estimate=pl.CostEstimate(flops=453_000_000, bytes_accessed=2_800_000, transcendentals=0),
-    )(near, far, keep, came)
 
 
 def per_device(
@@ -167,38 +156,39 @@
     ut_other = lax.dynamic_slice_in_dim(ut, (1 - xh) * 1536, 1536, 1)
     ut_far = lax.ppermute(ut_other, "xh", swap)
 
-    activations, _ = lax.optimization_barrier((activations, send))
     selected = lax.dynamic_slice_in_dim(activations, m * 192, 192, 1)
     place = jnp.stack([xh, c]).astype(jnp.int32)
     mine, other = factor_parts(place, activations, selected, output_grad)
     other, ut_far = lax.optimization_barrier((other, ut_far))
     came = lax.ppermute(other, "c", swap)
-    pair = (mine.astype(f32) + came.astype(f32)).astype(bf16)
+    pair_far = (mine[1].astype(f32) + came[1].astype(f32)).astype(bf16)
+    pair_near = (mine[0].astype(f32) + came[0].astype(f32)).astype(bf16)
+    pair_near, _ = lax.optimization_barrier((pair_near, pair_far))
+    came = lax.ppermute(pair_far, "xh", swap)
+    four = (pair_near.astype(f32) + came.astype(f32)).astype(bf16)
 
     near = jnp.where(xh == 0, jnp.stack([ut_mine, ut_far]), jnp.stack([ut_far, ut_mine]))
     near = near.reshape(192, 1536)
     far = lax.ppermute(near, "c", swap)
 
-    came_rows, pair, far = lax.optimization_barrier((came_rows, pair, far))
+    came_rows, pair_near, far = lax.optimization_barrier((came_rows, pair_near, far))
     eigen = jnp.pad(input_eigen, (0, 32)).reshape(1, 128)
     left_part, left_send, v_near = left_parts(near, far, came_rows, eigen)
+    v_far = lax.ppermute(v_near, "xh", swap)
+    v_near_core = lax.ppermute(v_near, "c", swap)
     left_came = lax.ppermute(left_send, "xh", swap)
-    v_far = lax.ppermute(v_near, "xh", swap)
+    left_came, v_far = lax.optimization_barrier((left_came, v_far))
     left_half = (left_part + left_came.astype(f32)).astype(bf16)
-    left_far = lax.ppermute(left_half[192:], "c", swap)
-    v_far, _ = lax.optimization_barrier((v_far, left_far))
-    v_near_core, v_far_core = lax.ppermute(v_near, "c", swap), lax.ppermute(v_far, "c", swap)
+    left_core = lax.ppermute(left_half, "c", swap)
+    v_far_core = lax.ppermute(v_far, "c", swap)
     eigen_out = jnp.where(c == 0, output_eigen, jnp.concatenate([output_eigen[:, 384:], output_eigen[:, :384]], axis=1))
-    keep, send_back = middle(
-        place, left_half[:192], left_far, v_near, v_far, v_near_core, v_far_core, eigen, eigen_out
+    out_part = tail(
+        place, left_half, left_core, v_near, v_far, v_near_core, v_far_core, eigen, eigen_out, near, far
     )
-    back_far = lax.ppermute(send_back, "c", swap)
-    out_part = out_parts_of(near, far, keep, back_far)
-
-    came = lax.all_to_all(pair, "z", 0, 0)
+
+    came = lax.all_to_all(four, "z", 0, 0)
     out_part, came = lax.optimization_barrier((out_part, came))
-    sides = jnp.sum(came.astype(f32), axis=0)
-    total = sides[0] + lax.ppermute(sides[1].astype(bf16), "xh", swap).astype(f32)
+    total = jnp.sum(came.astype(f32), axis=0)
     in_total = total[:48].reshape(48, 2, 192).transpose(2, 1, 0).reshape(192, 96)
     out_total = jnp.concatenate([total[48:72], total[72:]], axis=1)[None]
     new_input = keep_rate * input_factor + (1.0 - keep_rate) * (in_total / tokens)

time: 125 us -> 122 us (0.976)
  starting transfers between devices: 52 us -> 47.8 us
  waiting for transfers between devices: 50.4 us -> 48.2 us
  other arithmetic: 6.85 us -> 8.69 us
    all_to_all x1, waiting for transfers between devices: 20.2 us -> 27.7 us  [per_device(): lax.all_to_all(out_part, ('z', 'c'), 0, 0).reshape(8, 2, 96, 384)]
    all_to_all x1, waiting for transfers between devices: 16.1 us -> 11.5 us  [per_device(): came_rows = lax.all_to_all(send, ('z', 'c'), 0, 0)]
    ppermute x5 -> x4, waiting for transfers between devices: 4.58 us -> 1.41 us  [the longest x1 1.4 us: per_device(): v_far_core = lax.ppermute(v_far, 'c', swap)]
    ppermute x5 -> x4, starting transfers between devices: 14.2 us -> 11.3 us  [the longest x1 4.64 us: per_device(): came = lax.ppermute(pair_far, 'xh', swap)]
    ppermute x1, starting transfers between devices: 4.65 us -> 2.13 us  [per_device(): left_came = lax.ppermute(left_send, 'xh', swap)]
    ppermute x1, starting transfers between devices: 2.13 us -> 4.64 us  [per_device(): v_far = lax.ppermute(v_near, 'xh', swap)]
    ppermute x1, waiting for transfers between devices: 5.43 us -> 2.95 us  [per_device(): left_came = lax.ppermute(left_send, 'xh', swap)]
    all_to_all x1, waiting for transfers between devices: 1.75 us -> 3.98 us  [per_device(): came = lax.all_to_all(four, 'z', 0, 0)]
  transfers between devices with their start and end apart: 13 -> 12, of which waited for: 9 -> 6; matrix products, arithmetic and copies ran while one was open for 6% -> 7% of each run, Pallas kernels for 6% -> 7%
where the time goes in v5:
time: 122 us; the launch traced here: 121 us
  waiting for transfers between devices  48.2 us (40%)
  starting transfers between devices  47.8 us (39%)
  Pallas kernels  9.05 us (7%)
  other arithmetic  8.69 us (7%)
  local copies, waits for them, and re-layouts  6.37 us (5%)
    all_to_all x1, waiting for transfers between devices, per_device(): lax.all_to_all(out_part, ('z', 'c'), 0, 0).reshape(8, 2, 96, 384)  27.7 us
    all_to_all x1, starting transfers between devices, per_device(): came_rows = lax.all_to_all(send, ('z', 'c'), 0, 0)  12 us
    all_to_all x1, waiting for transfers between devices, per_device(): came_rows = lax.all_to_all(send, ('z', 'c'), 0, 0)  11.5 us
    ppermute x1, starting transfers between devices, per_device(): ut_far = lax.ppermute(ut_other, 'xh', swap)  4.81 us
    ppermute x1, starting transfers between devices, per_device(): came = lax.ppermute(pair_far, 'xh', swap)  4.64 us
    ppermute x1, starting transfers between devices, per_device(): v_far = lax.ppermute(v_near, 'xh', swap)  4.64 us
    all_to_all x1, starting transfers between devices, per_device(): came = lax.all_to_all(four, 'z', 0, 0)  4.33 us
    pallas_call x1, Pallas kernels, tail(): pl.pallas_call(tail_kernel, out_shape=jax.ShapeDtypeStruct((16, 96, 384),...  4.17 us
  transfers between devices with their start and end apart: 12, of which 6 were waited for; matrix products, arithmetic and copies ran while one was open for 7% of the time, Pallas kernels for 7%

profile of v5, /device:TPU:1, one launch (start us, length us, event | category | flops | bytes accessed | tf_op | source)
XLA Modules:
  0.0 121.0 jit_solution(14294795107234399024)
XLA Ops:
  1.6 1.3 %broadcast_in_dim.2 = bf16[8,2,120,384]{3,2,1,0:T(8,128)(2,1)} broadcast(bf16[2,120,384]{2,1,0:T(8,128)(2,1)S(1)} %pad_maximum_fusion), dimensions={1,2,3} | broadcast | bytes 1658880 | tf_op jit(solution)/shard_map/broadcast_in_dim | solution.py:150
  2.9 12.0 %all-to-all-start = ((bf16[16,120,384]{2,1,0:T(8,128)(2,1)}), bf16[16,120,384]{2,1,0:T(8,128)(2,1)S(1)}, u32[]{:S(2)}, u32[]{:S(2)}) async-start(bf16[16,120,384]{2,1,0:T(8,128)(2,1)} %bitcast.5), calls=%async_computation | async-start | bytes 2949120 | tf_op jit(solution)/shard_map/all_to_all | solution.py:151
  14.9 4.8 %collective-permute-start = (bf16[96,1536]{1,0:T(8,128)(2,1)S(1)}, bf16[96,1536]{1,0:T(8,128)(2,1)S(1)}, u32[]{:S(2)}, u32[]{:S(2)}) collective-permute-start(bf16[96,1536]{1,0:T(8,128)(2,1)S(1)} %get-tuple-element.42), channel_id=1, source_target_pairs={{0,256},{256,0},{1,257},{257,1},{2,258},{258,2},{3,259},{259,3},{4... | collective-permute-start | bytes 884744 | tf_op jit(solution)/shard_map/ppermute | solution.py:157
  21.0 1.9 %copy-done.2 = bf16[512,3072]{1,0:T(8,128)(2,1)S(1)} copy-done((bf16[512,3072]{1,0:T(8,128)(2,1)S(1)}, bf16[512,3072]{1,0:T(8,128)(2,1)}, u32[]{:S(2)}) %copy-start.2) | copy-done | bytes 3145752
  22.9 3.4 %shard_map.112 = (bf16[2,8,96,384]{3,2,1,0:T(8,128)(2,1)S(1)}, bf16[2,8,96,384]{3,2,1,0:T(8,128)(2,1)}) custom-call(s32[2]{0:T(128)S(1)} %pad_add_fusion.place, bf16[512,3072]{1,0:T(8,128)(2,1)S(1)} %copy-done.2, bf16[512,192]{1,0:T(8,128)(2,1)S(1)} %constant_dynamic-slice_fusion.sel, bf16[512,768]{1,0:T(8,128)(2,1)S(1)} %copy-done.5), custom_call_target="tpu_custom_call" | custom-call | flops 1250000000 | bytes 8000000 | tf_op jit(solution)/shard_map/pallas_call | solution.py:43
  27.3 2.5 %collective-permute-start.1 = (bf16[2,8,96,384]{3,2,1,0:T(8,128)(2,1)}, bf16[2,8,96,384]{3,2,1,0:T(8,128)(2,1)}, u32[]{:S(2)}, u32[]{:S(2)}) collective-permute-start(bf16[2,8,96,384]{3,2,1,0:T(8,128)(2,1)} %get-tuple-element.22), channel_id=1, source_target_pairs={{0,16},{16,0},{1,17},{17,1},{2,18},{18,2},{3,19},{19,3},{4,20},{20... | collective-permute-start | bytes 3538952 | tf_op jit(solution)/shard_map/ppermute | solution.py:163
  29.9 2.1 %collective-permute-start.2 = (bf16[192,1536]{1,0:T(8,128)(2,1)S(1)}, bf16[192,1536]{1,0:T(8,128)(2,1)S(1)}, u32[]{:S(2)}, u32[]{:S(2)}) collective-permute-start(bf16[192,1536]{1,0:T(8,128)(2,1)S(1)} %bitcast.34), channel_id=1, source_target_pairs={{0,16},{16,0},{1,17},{17,1},{2,18},{18,2},{3,19},{19,3},{4,20},{20... | collective-permute-start | bytes 1769480 | tf_op jit(solution)/shard_map/ppermute | solution.py:172
  32.6 2.6 %fusion.1 = (bf16[8,96,384]{2,1,0:T(8,128)(2,1)}, bf16[8,96,384]{2,1,0:T(8,128)(2,1)}) fusion(bf16[2,8,96,384]{3,2,1,0:T(8,128)(2,1)} %collective-permute-done.1, bf16[2,8,96,384]{3,2,1,0:T(8,128)(2,1)S(1)} %copy-done.1), kind=kLoop, calls=%fused_computation.5 | loop fusion | flops 2359296 | bytes 3538944 | tf_op jit(solution)/shard_map/convert_element_type | solution.py:164
  35.2 4.6 %collective-permute-start.8 = (bf16[8,96,384]{2,1,0:T(8,128)(2,1)}, bf16[8,96,384]{2,1,0:T(8,128)(2,1)}, u32[]{:S(2)}, u32[]{:S(2)}) collective-permute-start(bf16[8,96,384]{2,1,0:T(8,128)(2,1)} %get-tuple-element.39), channel_id=1, source_target_pairs={{0,256},{256,0},{1,257},{257,1},{2,258},{258,2},{3,259},{259,3},{4... | collective-permute-start | bytes 1769480 | tf_op jit(solution)/shard_map/ppermute | solution.py:167
  39.9 11.5 %all-to-all-done.came = bf16[16,120,384]{2,1,0:T(8,128)(2,1)S(1)} async-done(((bf16[16,120,384]{2,1,0:T(8,128)(2,1)}), bf16[16,120,384]{2,1,0:T(8,128)(2,1)S(1)}, u32[]{:S(2)}, u32[]{:S(2)}) %all-to-all-start) | async-done | bytes 1474592 | tf_op jit(solution)/shard_map/all_to_all | solution.py:151
  51.3 1.5 %shard_map.113 = (f32[384,384]{1,0:T(8,128)S(1)}, bf16[384,384]{1,0:T(8,128)(2,1)}, bf16[400,384]{1,0:T(8,128)(2,1)S(1)}) custom-call(bf16[192,1536]{1,0:T(8,128)(2,1)S(1)} %bitcast.35, bf16[192,1536]{1,0:T(8,128)(2,1)S(1)} %collective-permute-done.2.far, bf16[16,120,384]{2,1,0:T(8,128)(2,1)S(1)} %all-to-all-done.came, f32[1,128]{1,0:T(1,128)S(1)} %pad_bitcast_fusion.eigen), custom_call_target="tpu_custom_call" | custom-call | flops 453000000 | bytes 3600000 | tf_op jit(solution)/shard_map/pallas_call | solution.py:73
  52.8 4.6 %collective-permute-start.4 = (bf16[400,384]{1,0:T(8,128)(2,1)S(1)}, bf16[400,384]{1,0:T(8,128)(2,1)S(1)}, u32[]{:S(2)}, u32[]{:S(2)}) collective-permute-start(bf16[400,384]{1,0:T(8,128)(2,1)S(1)} %get-tuple-element.28.near_v), channel_id=1, source_target_pairs={{0,256},{256,0},{1,257},{257,1},{2,258},{258,2},{3,259},{259,3},{4... | collective-permute-start | bytes 921608 | tf_op jit(solution)/shard_map/ppermute | solution.py:177
  57.5 2.1 %collective-permute-start.3 = (bf16[384,384]{1,0:T(8,128)(2,1)}, bf16[384,384]{1,0:T(8,128)(2,1)S(1)}, u32[]{:S(2)}, u32[]{:S(2)}) collective-permute-start(bf16[384,384]{1,0:T(8,128)(2,1)} %get-tuple-element.27), channel_id=1, source_target_pairs={{0,256},{256,0},{1,257},{257,1},{2,258},{258,2},{3,259},{259,3},{4... | collective-permute-start | bytes 884744 | tf_op jit(solution)/shard_map/ppermute | solution.py:179
  59.6 2.2 %add_convert_fusion = bf16[8,96,384]{2,1,0:T(8,128)(2,1)} fusion(bf16[8,96,384]{2,1,0:T(8,128)(2,1)} %collective-permute-done.8, bf16[8,96,384]{2,1,0:T(8,128)(2,1)} %get-tuple-element.23), kind=kLoop, calls=%fused_computation.1 | loop fusion | flops 1179648 | bytes 1769472 | tf_op jit(solution)/shard_map/convert_element_type | solution.py:168
  61.9 4.3 %all-to-all-start.1 = ((bf16[8,96,384]{2,1,0:T(8,128)(2,1)}), bf16[8,96,384]{2,1,0:T(8,128)(2,1)}, u32[]{:S(2)}, u32[]{:S(2)}) async-start(bf16[8,96,384]{2,1,0:T(8,128)(2,1)} %add_convert_fusion), calls=%async_computation.1 | async-start | bytes 1179648 | tf_op jit(solution)/shard_map/all_to_all | solution.py:189
  66.2 2.4 %collective-permute-start.6 = (bf16[400,384]{1,0:T(8,128)(2,1)S(1)}, bf16[400,384]{1,0:T(8,128)(2,1)S(1)}, u32[]{:S(2)}, u32[]{:S(2)}) collective-permute-start(bf16[400,384]{1,0:T(8,128)(2,1)S(1)} %get-tuple-element.28.near_v), channel_id=1, source_target_pairs={{0,16},{16,0},{1,17},{17,1},{2,18},{18,2},{3,19},{19,3},{4,20},{20... | collective-permute-start | bytes 921608 | tf_op jit(solution)/shard_map/ppermute | solution.py:178
  68.6 2.9 %collective-permute-done.3 = bf16[384,384]{1,0:T(8,128)(2,1)S(1)} collective-permute-done((bf16[384,384]{1,0:T(8,128)(2,1)}, bf16[384,384]{1,0:T(8,128)(2,1)S(1)}, u32[]{:S(2)}, u32[]{:S(2)}) %collective-permute-start.3) | collective-permute-done | bytes 294944 | tf_op jit(solution)/shard_map/ppermute | solution.py:179
  71.6 2.3 %collective-permute-start.5 = (bf16[384,384]{1,0:T(8,128)(2,1)S(1)}, bf16[384,384]{1,0:T(8,128)(2,1)S(1)}, u32[]{:S(2)}, u32[]{:S(2)}) collective-permute-start(bf16[384,384]{1,0:T(8,128)(2,1)S(1)} %add_convert_fusion.3.left), channel_id=1, source_target_pairs={{0,16},{16,0},{1,17},{17,1},{2,18},{18,2},{3,19},{19,3},{4,20},{20... | collective-permute-start | bytes 884744 | tf_op jit(solution)/shard_map/ppermute | solution.py:182
  73.9 2.0 %collective-permute-start.7 = (bf16[400,384]{1,0:T(8,128)(2,1)S(1)}, bf16[400,384]{1,0:T(8,128)(2,1)S(1)}, u32[]{:S(2)}, u32[]{:S(2)}) collective-permute-start(bf16[400,384]{1,0:T(8,128)(2,1)S(1)} %collective-permute-done.4.far_v), channel_id=1, source_target_pairs={{0,16},{16,0},{1,17},{17,1},{2,18},{18,2},{3,19},{19,3},{4,20},{20... | collective-permute-start | bytes 921608 | tf_op jit(solution)/shard_map/ppermute | solution.py:183
  76.0 1.4 %collective-permute-done.7.far_v_core = bf16[400,384]{1,0:T(8,128)(2,1)S(1)} collective-permute-done((bf16[400,384]{1,0:T(8,128)(2,1)S(1)}, bf16[400,384]{1,0:T(8,128)(2,1)S(1)}, u32[]{:S(2)}, u32[]{:S(2)}) %collective-permute-start.7) | collective-permute-done | bytes 307232 | tf_op jit(solution)/shard_map/ppermute | solution.py:183
  77.4 4.2 %shard_map.114 = bf16[16,96,384]{2,1,0:T(8,128)(2,1)} custom-call(s32[2]{0:T(128)S(1)} %copy-done.4, bf16[384,384]{1,0:T(8,128)(2,1)S(1)} %add_convert_fusion.3.left, bf16[384,384]{1,0:T(8,128)(2,1)S(1)} %collective-permute-done.5.left_core, bf16[400,384]{1,0:T(8,128)(2,1)S(1)} %get-tuple-element.28.near_v, ...), custom_call_target="tpu_custom_call" | custom-call | flops 1130000000 | bytes 4800000 | tf_op jit(solution)/shard_map/pallas_call | solution.py:123
  81.6 4.0 %all-to-all-done.1 = bf16[8,96,384]{2,1,0:T(8,128)(2,1)} async-done(((bf16[8,96,384]{2,1,0:T(8,128)(2,1)}), bf16[8,96,384]{2,1,0:T(8,128)(2,1)}, u32[]{:S(2)}, u32[]{:S(2)}) %all-to-all-start.1) | async-done | bytes 589856 | tf_op jit(solution)/shard_map/all_to_all | solution.py:189
  85.5 4.0 %all-to-all-start.2 = ((bf16[16,96,384]{2,1,0:T(8,128)(2,1)}), bf16[16,96,384]{2,1,0:T(8,128)(2,1)S(1)}, u32[]{:S(2)}, u32[]{:S(2)}) async-start(bf16[16,96,384]{2,1,0:T(8,128)(2,1)} %shard_map.114), calls=%async_computation.2 | async-start | bytes 2359296 | tf_op jit(solution)/shard_map/all_to_all | solution.py:197
  92.4 27.7 %all-to-all-done.2 = bf16[16,96,384]{2,1,0:T(8,128)(2,1)S(1)} async-done(((bf16[16,96,384]{2,1,0:T(8,128)(2,1)}), bf16[16,96,384]{2,1,0:T(8,128)(2,1)S(1)}, u32[]{:S(2)}, u32[]{:S(2)}) %all-to-all-start.2) | async-done | bytes 1179680 | tf_op jit(solution)/shard_map/all_to_all | solution.py:197
  (50 shorter events, 7.7 us)
Async XLA Ops:
  2.9 12.0 %copy-start.6 = (bf16[3072,96]{0,1:T(8,128)(2,1)S(1)}, bf16[3072,96]{0,1:T(8,128)(2,1)}, u32[]{:S(2)}) copy-start(bf16[3072,96]{0,1:T(8,128)(2,1)} %param.12) | copy-start | bytes 1769476
  2.9 48.4 %all-to-all-start = ((bf16[16,120,384]{2,1,0:T(8,128)(2,1)}), bf16[16,120,384]{2,1,0:T(8,128)(2,1)S(1)}, u32[]{:S(2)}, u32[]{:S(2)}) async-start(bf16[16,120,384]{2,1,0:T(8,128)(2,1)} %bitcast.5), calls=%async_computation | async-start | bytes 2949120 | tf_op jit(solution)/shard_map/all_to_all | solution.py:151
  14.8 6.1 %copy-start.5 = (bf16[512,768]{1,0:T(8,128)(2,1)S(1)}, bf16[512,768]{1,0:T(8,128)(2,1)}, u32[]{:S(2)}) copy-start(bf16[512,768]{1,0:T(8,128)(2,1)} %grad.1) | copy-start | bytes 2359300
  14.9 12.3 %collective-permute-start = (bf16[96,1536]{1,0:T(8,128)(2,1)S(1)}, bf16[96,1536]{1,0:T(8,128)(2,1)S(1)}, u32[]{:S(2)}, u32[]{:S(2)}) collective-permute-start(bf16[96,1536]{1,0:T(8,128)(2,1)S(1)} %get-tuple-element.42), channel_id=1, source_target_pairs={{0,256},{256,0},{1,257},{257,1},{2,258},{258,2},{3,259},{259,3},{4... | collective-permute-start | bytes 884744 | tf_op jit(solution)/shard_map/ppermute | solution.py:157
  19.8 6.4 %copy-start.3 = (s32[2]{0:T(128)}, s32[2]{0:T(128)S(1)}, u32[]{:S(2)}) copy-start(s32[2]{0:T(128)S(1)} %pad_add_fusion.place) | copy-start | bytes 28
  21.0 1.9 %copy-start.2 = (bf16[512,3072]{1,0:T(8,128)(2,1)S(1)}, bf16[512,3072]{1,0:T(8,128)(2,1)}, u32[]{:S(2)}) copy-start(bf16[512,3072]{1,0:T(8,128)(2,1)} %act.1) | copy-start | bytes 9437188
  26.2 1.0 copy-start
  27.3 5.3 %collective-permute-start.1 = (bf16[2,8,96,384]{3,2,1,0:T(8,128)(2,1)}, bf16[2,8,96,384]{3,2,1,0:T(8,128)(2,1)}, u32[]{:S(2)}, u32[]{:S(2)}) collective-permute-start(bf16[2,8,96,384]{3,2,1,0:T(8,128)(2,1)} %get-tuple-element.22), channel_id=1, source_target_pairs={{0,16},{16,0},{1,17},{17,1},{2,18},{18,2},{3,19},{19,3},{4,20},{20... | collective-permute-start | bytes 3538952 | tf_op jit(solution)/shard_map/ppermute | solution.py:163
  29.8 2.8 %copy-start.1 = (bf16[2,8,96,384]{3,2,1,0:T(8,128)(2,1)S(1)}, bf16[2,8,96,384]{3,2,1,0:T(8,128)(2,1)}, u32[]{:S(2)}) copy-start(bf16[2,8,96,384]{3,2,1,0:T(8,128)(2,1)} %copy-done) | copy-start | bytes 3538948
  29.9 9.9 %collective-permute-start.2 = (bf16[192,1536]{1,0:T(8,128)(2,1)S(1)}, bf16[192,1536]{1,0:T(8,128)(2,1)S(1)}, u32[]{:S(2)}, u32[]{:S(2)}) collective-permute-start(bf16[192,1536]{1,0:T(8,128)(2,1)S(1)} %bitcast.34), channel_id=1, source_target_pairs={{0,16},{16,0},{1,17},{17,1},{2,18},{18,2},{3,19},{19,3},{4,20},{20... | collective-permute-start | bytes 1769480 | tf_op jit(solution)/shard_map/ppermute | solution.py:172
  32.6 7.2 %copy-start.10 = (f32[96]{0:T(128)S(1)}, f32[96]{0:T(128)}, u32[]{:S(2)}) copy-start(f32[96]{0:T(128)} %param.13) | copy-start | bytes 1156
  35.2 24.4 %collective-permute-start.8 = (bf16[8,96,384]{2,1,0:T(8,128)(2,1)}, bf16[8,96,384]{2,1,0:T(8,128)(2,1)}, u32[]{:S(2)}, u32[]{:S(2)}) collective-permute-start(bf16[8,96,384]{2,1,0:T(8,128)(2,1)} %get-tuple-element.39), channel_id=1, source_target_pairs={{0,256},{256,0},{1,257},{257,1},{2,258},{258,2},{3,259},{259,3},{4... | collective-permute-start | bytes 1769480 | tf_op jit(solution)/shard_map/ppermute | solution.py:167
  52.8 18.7 %collective-permute-start.4 = (bf16[400,384]{1,0:T(8,128)(2,1)S(1)}, bf16[400,384]{1,0:T(8,128)(2,1)S(1)}, u32[]{:S(2)}, u32[]{:S(2)}) collective-permute-start(bf16[400,384]{1,0:T(8,128)(2,1)S(1)} %get-tuple-element.28.near_v), channel_id=1, source_target_pairs={{0,256},{256,0},{1,257},{257,1},{2,258},{258,2},{3,259},{259,3},{4... | collective-permute-start | bytes 921608 | tf_op jit(solution)/shard_map/ppermute | solution.py:177
  57.5 14.0 %collective-permute-start.3 = (bf16[384,384]{1,0:T(8,128)(2,1)}, bf16[384,384]{1,0:T(8,128)(2,1)S(1)}, u32[]{:S(2)}, u32[]{:S(2)}) collective-permute-start(bf16[384,384]{1,0:T(8,128)(2,1)} %get-tuple-element.27), channel_id=1, source_target_pairs={{0,256},{256,0},{1,257},{257,1},{2,258},{258,2},{3,259},{259,3},{4... | collective-permute-start | bytes 884744 | tf_op jit(solution)/shard_map/ppermute | solution.py:179
  61.8 14.1 %copy-start.9 = (f32[1,768]{1,0:T(1,128)S(1)}, f32[1,768]{1,0:T(1,128)}, u32[]{:S(2)}) copy-start(f32[1,768]{1,0:T(1,128)} %param.15) | copy-start | bytes 9220
  61.8 15.5 %copy-start.4 = (s32[2]{0:T(128)S(1)}, s32[2]{0:T(128)}, u32[]{:S(2)}) copy-start(s32[2]{0:T(128)} %copy-done.3) | copy-start | bytes 28
  61.9 23.7 %all-to-all-start.1 = ((bf16[8,96,384]{2,1,0:T(8,128)(2,1)}), bf16[8,96,384]{2,1,0:T(8,128)(2,1)}, u32[]{:S(2)}, u32[]{:S(2)}) async-start(bf16[8,96,384]{2,1,0:T(8,128)(2,1)} %add_convert_fusion), calls=%async_computation.1 | async-start | bytes 1179648 | tf_op jit(solution)/shard_map/all_to_all | solution.py:189
  66.2 9.8 %collective-permute-start.6 = (bf16[400,384]{1,0:T(8,128)(2,1)S(1)}, bf16[400,384]{1,0:T(8,128)(2,1)S(1)}, u32[]{:S(2)}, u32[]{:S(2)}) collective-permute-start(bf16[400,384]{1,0:T(8,128)(2,1)S(1)} %get-tuple-element.28.near_v), channel_id=1, source_target_pairs={{0,16},{16,0},{1,17},{17,1},{2,18},{18,2},{3,19},{19,3},{4,20},{20... | collective-permute-start | bytes 921608 | tf_op jit(solution)/shard_map/ppermute | solution.py:178
  71.6 4.4 %collective-permute-start.5 = (bf16[384,384]{1,0:T(8,128)(2,1)S(1)}, bf16[384,384]{1,0:T(8,128)(2,1)S(1)}, u32[]{:S(2)}, u32[]{:S(2)}) collective-permute-start(bf16[384,384]{1,0:T(8,128)(2,1)S(1)} %add_convert_fusion.3.left), channel_id=1, source_target_pairs={{0,16},{16,0},{1,17},{17,1},{2,18},{18,2},{3,19},{19,3},{4,20},{20... | collective-permute-start | bytes 884744 | tf_op jit(solution)/shard_map/ppermute | solution.py:182
  73.9 3.5 %collective-permute-start.7 = (bf16[400,384]{1,0:T(8,128)(2,1)S(1)}, bf16[400,384]{1,0:T(8,128)(2,1)S(1)}, u32[]{:S(2)}, u32[]{:S(2)}) collective-permute-start(bf16[400,384]{1,0:T(8,128)(2,1)S(1)} %collective-permute-done.4.far_v), channel_id=1, source_target_pairs={{0,16},{16,0},{1,17},{17,1},{2,18},{18,2},{3,19},{19,3},{4,20},{20... | collective-permute-start | bytes 921608 | tf_op jit(solution)/shard_map/ppermute | solution.py:183
  81.6 8.0 %copy-start.7 = (f32[192,96]{1,0:T(8,128)S(1)}, f32[192,96]{1,0:T(8,128)}, u32[]{:S(2)}) copy-start(f32[192,96]{1,0:T(8,128)} %param.16) | copy-start | bytes 221188
  85.5 34.6 %all-to-all-start.2 = ((bf16[16,96,384]{2,1,0:T(8,128)(2,1)}), bf16[16,96,384]{2,1,0:T(8,128)(2,1)S(1)}, u32[]{:S(2)}, u32[]{:S(2)}) async-start(bf16[16,96,384]{2,1,0:T(8,128)(2,1)} %shard_map.114), calls=%async_computation.2 | async-start | bytes 2359296 | tf_op jit(solution)/shard_map/all_to_all | solution.py:197
  89.5 2.2 %copy-start.8 = (f32[1,24,768]{2,1,0:T(8,128)S(1)}, f32[1,24,768]{2,1,0:T(8,128)}, u32[]{:S(2)}) copy-start(f32[1,24,768]{2,1,0:T(8,128)} %param.17) | copy-start | bytes 221188

commit v6 on v5

--- a/solution.py
+++ b/solution.py
@@ -51,34 +51,28 @@
     )(place, act, sel, grad)
 
 
-def left_kernel(near, far, came, eigen, wide, narrow, v, rows):
+def left_kernel(near, far, came, eigen, out, rows):
     for s in range(16):
         rows[s * 96 : (s + 1) * 96, :] = came[s, :96, :]
     for at, basis in ((0, near), (192, far)):
-        left = dot(basis[...], rows[...], 1, 0)
-        wide[at : at + 192, :] = left
-        narrow[at : at + 192, :] = left.astype(bf16)
+        out[at : at + 192, :] = dot(basis[...], rows[...], 1, 0).astype(bf16)
     for s in range(8):
-        v[s * 48 : (s + 1) * 48, :] = came[2 * s : 2 * s + 2, 96:, :].reshape(48, 384)
+        out[384 + s * 48 : 384 + (s + 1) * 48, :] = came[2 * s : 2 * s + 2, 96:, :].reshape(48, 384)
     rest, parts = eigen[...], []
     for _ in range(3):
         parts.append(rest.astype(bf16).astype(f32))
         rest = rest - parts[-1]
     three = jnp.concatenate(parts + [jnp.zeros((13, 128), f32)], axis=0).astype(bf16)
-    v[384:, :] = jnp.concatenate([three, jnp.zeros((16, 256), bf16)], axis=1)
+    out[768:, :] = jnp.concatenate([three, jnp.zeros((16, 256), bf16)], axis=1)
 
 
 def left_parts(near, far, came, eigen):
     vmem = pl.BlockSpec(memory_space=pltpu.VMEM)
     return pl.pallas_call(
         left_kernel,
-        out_shape=[
-            jax.ShapeDtypeStruct((384, 384), f32),
-            jax.ShapeDtypeStruct((384, 384), bf16),
-            jax.ShapeDtypeStruct((400, 384), bf16),
-        ],
+        out_shape=jax.ShapeDtypeStruct((784, 384), bf16),
         in_specs=[vmem] * 4,
-        out_specs=[vmem] * 3,
+        out_specs=vmem,
         scratch_shapes=[pltpu.VMEM((1536, 384), bf16)],
         compiler_params=pltpu.CompilerParams(vmem_limit_bytes=16 * 1024 * 1024),
         cost_estimate=pl.CostEstimate(flops=453_000_000, bytes_accessed=3_600_000, transcendentals=0),
@@ -90,24 +84,28 @@
     return jnp.sum(jnp.where(ids, jnp.broadcast_to(row, (96, 128)), 0.0), axis=1, keepdims=True)
 
 
-def tail_kernel(place, left, left_core, near_v, far_v, near_v_core, far_v_core, eigen, eigen_out, near, far, out):
+def tail_kernel(place, mine, mine_far, mine_core, far_core, eigen, eigen_out, near, far, out):
     same = place[0] == place[1]
 
-    def third(v):
-        three = v[384:, :128].astype(f32)
+    def third(group):
+        three = group[768:, :128].astype(f32)
         return column(three[0:1] + three[1:2] + three[2:3])
 
-    half_first = jnp.where(same, near_v[:384, :], far_v[:384, :])
-    half_second = jnp.where(same, near_v_core[:384, :], far_v_core[:384, :])
+    def left(one, two, at):
+        return (one[at : at + 192, :].astype(f32) + two[at : at + 192, :].astype(f32)).astype(bf16)
+
+    basis = slice(384, 768)
+    half_first = jnp.where(same, mine[basis, :], mine_far[basis, :])
+    half_second = jnp.where(same, mine_core[basis, :], far_core[basis, :])
     backs = []
-    for r, (mine, other) in enumerate(((column(eigen[...]), third(far_v)), (third(near_v_core), third(far_v_core)))):
-        low, high = jnp.concatenate([mine, other], axis=0), jnp.concatenate([other, mine], axis=0)
+    for r, (one, two) in enumerate(((column(eigen[...]), third(mine_far)), (third(mine_core), third(far_core)))):
+        low, high = jnp.concatenate([one, two], axis=0), jnp.concatenate([two, one], axis=0)
         eigen_rows = jnp.where(place[0] == 0, low, high)
-        own, came = left[r * 192 : (r + 1) * 192, :], left_core[(1 - r) * 192 : (2 - r) * 192, :]
+        own, came = left(mine, mine_far, r * 192), left(mine_core, far_core, (1 - r) * 192)
         first, second = jnp.where(same, own, came), jnp.where(same, came, own)
         scaled = []
-        for at, (v_first, v_second) in enumerate(((near_v, far_v), (near_v_core, far_v_core))):
-            rotated = dot(first, v_first[:384, :], 1, 0) + dot(second, v_second[:384, :], 1, 0)
+        for at, (v_first, v_second) in enumerate(((mine, mine_far), (mine_core, far_core))):
+            rotated = dot(first, v_first[basis, :], 1, 0) + dot(second, v_second[basis, :], 1, 0)
             denominator = eigen_rows * eigen_out[:, at * 384 : (at + 1) * 384] + damping
             scaled.append((rotated / denominator).astype(bf16))
         backs.append((dot(scaled[0], half_first, 1, 1) + dot(scaled[1], half_second, 1, 1)).astype(bf16))
@@ -173,18 +171,12 @@
 
     came_rows, pair_near, far = lax.optimization_barrier((came_rows, pair_near, far))
     eigen = jnp.pad(input_eigen, (0, 32)).reshape(1, 128)
-    left_part, left_send, v_near = left_parts(near, far, came_rows, eigen)
-    v_far = lax.ppermute(v_near, "xh", swap)
-    v_near_core = lax.ppermute(v_near, "c", swap)
-    left_came = lax.ppermute(left_send, "xh", swap)
-    left_came, v_far = lax.optimization_barrier((left_came, v_far))
-    left_half = (left_part + left_came.astype(f32)).astype(bf16)
-    left_core = lax.ppermute(left_half, "c", swap)
-    v_far_core = lax.ppermute(v_far, "c", swap)
+    mine_rows = left_parts(near, far, came_rows, eigen)
+    far_rows = lax.ppermute(mine_rows, "xh", swap)
+    core_rows = lax.ppermute(mine_rows, "c", swap)
+    far_core = lax.ppermute(far_rows, "c", swap)
     eigen_out = jnp.where(c == 0, output_eigen, jnp.concatenate([output_eigen[:, 384:], output_eigen[:, :384]], axis=1))
-    out_part = tail(
-        place, left_half, left_core, v_near, v_far, v_near_core, v_far_core, eigen, eigen_out, near, far
-    )
+    out_part = tail(place, mine_rows, far_rows, core_rows, far_core, eigen, eigen_out, near, far)
 
     came = lax.all_to_all(four, "z", 0, 0)
     out_part, came = lax.optimization_barrier((out_part, came))

time: 122 us -> 119 us (0.975)
  starting transfers between devices: 47.8 us -> 43.2 us
  waiting for transfers between devices: 48.2 us -> 49.9 us
    ppermute x5 -> x3, starting transfers between devices: 13.5 us -> 9.03 us  [the longest x1 4.65 us: per_device(): far_rows = lax.ppermute(mine_rows, 'xh', swap)]
    ppermute x5 -> x3, waiting for transfers between devices: 4.35 us -> 7.46 us  [the longest x1 5.51 us: per_device(): far_rows = lax.ppermute(mine_rows, 'xh', swap)]
    all_to_all x1, waiting for transfers between devices: 3.98 us -> 2.67 us  [per_device(): came = lax.all_to_all(four, 'z', 0, 0)]
    unnamed x24 -> x20, local copies, waits for them, and re-layouts: 3.76 us -> 3.74 us
  transfers between devices with their start and end apart: 12 -> 10, of which waited for: 6 -> 6; matrix products, arithmetic and copies ran while one was open for 7% -> 8% of each run, Pallas kernels for 7% -> 8%
where the time goes in v6:
time: 119 us; the launch traced here: 118 us
  waiting for transfers between devices  49.9 us (42%)
  starting transfers between devices  43.2 us (36%)
  Pallas kernels  9 us (8%)
  other arithmetic  8.62 us (7%)
  local copies, waits for them, and re-layouts  6.35 us (5%)
    all_to_all x1, waiting for transfers between devices, per_device(): lax.all_to_all(out_part, ('z', 'c'), 0, 0).reshape(8, 2, 96, 384)  27.7 us
    all_to_all x1, starting transfers between devices, per_device(): came_rows = lax.all_to_all(send, ('z', 'c'), 0, 0)  12 us
    all_to_all x1, waiting for transfers between devices, per_device(): came_rows = lax.all_to_all(send, ('z', 'c'), 0, 0)  11.4 us
    ppermute x1, waiting for transfers between devices, per_device(): far_rows = lax.ppermute(mine_rows, 'xh', swap)  5.51 us
    ppermute x1, starting transfers between devices, per_device(): ut_far = lax.ppermute(ut_other, 'xh', swap)  4.81 us
    pallas_call x1, Pallas kernels, tail(): pl.pallas_call(tail_kernel, out_shape=jax.ShapeDtypeStruct((16, 96, 384),...  4.8 us
    ppermute x1, starting transfers between devices, per_device(): far_rows = lax.ppermute(mine_rows, 'xh', swap)  4.65 us
    ppermute x1, starting transfers between devices, per_device(): came = lax.ppermute(pair_far, 'xh', swap)  4.64 us
  transfers between devices with their start and end apart: 10, of which 6 were waited for; matrix products, arithmetic and copies ran while one was open for 8% of the time, Pallas kernels for 8%

profile of v6, /device:TPU:1, one launch (start us, length us, event | category | flops | bytes accessed | tf_op | source)
XLA Modules:
  0.0 118.1 jit_solution(18409372988911092953)
XLA Ops:
  1.6 1.3 %broadcast_in_dim.2 = bf16[8,2,120,384]{3,2,1,0:T(8,128)(2,1)} broadcast(bf16[2,120,384]{2,1,0:T(8,128)(2,1)S(1)} %pad_maximum_fusion), dimensions={1,2,3} | broadcast | bytes 1658880 | tf_op jit(solution)/shard_map/broadcast_in_dim | solution.py:148
  2.9 12.0 %all-to-all-start = ((bf16[16,120,384]{2,1,0:T(8,128)(2,1)}), bf16[16,120,384]{2,1,0:T(8,128)(2,1)S(1)}, u32[]{:S(2)}, u32[]{:S(2)}) async-start(bf16[16,120,384]{2,1,0:T(8,128)(2,1)} %bitcast.5), calls=%async_computation | async-start | bytes 2949120 | tf_op jit(solution)/shard_map/all_to_all | solution.py:149
  14.9 4.8 %collective-permute-start = (bf16[96,1536]{1,0:T(8,128)(2,1)S(1)}, bf16[96,1536]{1,0:T(8,128)(2,1)S(1)}, u32[]{:S(2)}, u32[]{:S(2)}) collective-permute-start(bf16[96,1536]{1,0:T(8,128)(2,1)S(1)} %get-tuple-element.32), channel_id=1, source_target_pairs={{0,256},{256,0},{1,257},{257,1},{2,258},{258,2},{3,259},{259,3},{4... | collective-permute-start | bytes 884744 | tf_op jit(solution)/shard_map/ppermute | solution.py:155
  19.8 1.1 constant_dynamic-slice_fusion.sel
  21.0 1.9 %copy-done.2 = bf16[512,3072]{1,0:T(8,128)(2,1)S(1)} copy-done((bf16[512,3072]{1,0:T(8,128)(2,1)S(1)}, bf16[512,3072]{1,0:T(8,128)(2,1)}, u32[]{:S(2)}) %copy-start.2) | copy-done | bytes 3145752
  22.9 3.4 %shard_map.112 = (bf16[2,8,96,384]{3,2,1,0:T(8,128)(2,1)S(1)}, bf16[2,8,96,384]{3,2,1,0:T(8,128)(2,1)}) custom-call(s32[2]{0:T(128)S(1)} %pad_add_fusion.place, bf16[512,3072]{1,0:T(8,128)(2,1)S(1)} %copy-done.2, bf16[512,192]{1,0:T(8,128)(2,1)S(1)} %constant_dynamic-slice_fusion.sel, bf16[512,768]{1,0:T(8,128)(2,1)S(1)} %copy-done.3), custom_call_target="tpu_custom_call" | custom-call | flops 1250000000 | bytes 8000000 | tf_op jit(solution)/shard_map/pallas_call | solution.py:43
  26.3 1.0 copy-done
  27.3 2.5 %collective-permute-start.1 = (bf16[2,8,96,384]{3,2,1,0:T(8,128)(2,1)}, bf16[2,8,96,384]{3,2,1,0:T(8,128)(2,1)}, u32[]{:S(2)}, u32[]{:S(2)}) collective-permute-start(bf16[2,8,96,384]{3,2,1,0:T(8,128)(2,1)} %get-tuple-element.17), channel_id=1, source_target_pairs={{0,16},{16,0},{1,17},{17,1},{2,18},{18,2},{3,19},{19,3},{4,20},{20... | collective-permute-start | bytes 3538952 | tf_op jit(solution)/shard_map/ppermute | solution.py:161
  29.9 2.1 %collective-permute-start.2 = (bf16[192,1536]{1,0:T(8,128)(2,1)S(1)}, bf16[192,1536]{1,0:T(8,128)(2,1)S(1)}, u32[]{:S(2)}, u32[]{:S(2)}) collective-permute-start(bf16[192,1536]{1,0:T(8,128)(2,1)S(1)} %bitcast.34), channel_id=1, source_target_pairs={{0,16},{16,0},{1,17},{17,1},{2,18},{18,2},{3,19},{19,3},{4,20},{20... | collective-permute-start | bytes 1769480 | tf_op jit(solution)/shard_map/ppermute | solution.py:170
  32.6 2.6 %fusion.1 = (bf16[8,96,384]{2,1,0:T(8,128)(2,1)}, bf16[8,96,384]{2,1,0:T(8,128)(2,1)}) fusion(bf16[2,8,96,384]{3,2,1,0:T(8,128)(2,1)} %collective-permute-done.1, bf16[2,8,96,384]{3,2,1,0:T(8,128)(2,1)S(1)} %copy-done.1), kind=kLoop, calls=%fused_computation.5 | loop fusion | flops 2359296 | bytes 3538944 | tf_op jit(solution)/shard_map/convert_element_type | solution.py:162
  35.2 4.6 %collective-permute-start.6 = (bf16[8,96,384]{2,1,0:T(8,128)(2,1)}, bf16[8,96,384]{2,1,0:T(8,128)(2,1)}, u32[]{:S(2)}, u32[]{:S(2)}) collective-permute-start(bf16[8,96,384]{2,1,0:T(8,128)(2,1)} %get-tuple-element.29), channel_id=1, source_target_pairs={{0,256},{256,0},{1,257},{257,1},{2,258},{258,2},{3,259},{259,3},{4... | collective-permute-start | bytes 1769480 | tf_op jit(solution)/shard_map/ppermute | solution.py:165
  39.9 11.4 %all-to-all-done.came = bf16[16,120,384]{2,1,0:T(8,128)(2,1)S(1)} async-done(((bf16[16,120,384]{2,1,0:T(8,128)(2,1)}), bf16[16,120,384]{2,1,0:T(8,128)(2,1)S(1)}, u32[]{:S(2)}, u32[]{:S(2)}) %all-to-all-start) | async-done | bytes 1474592 | tf_op jit(solution)/shard_map/all_to_all | solution.py:149
  52.1 4.7 %collective-permute-start.3 = (bf16[784,384]{1,0:T(8,128)(2,1)S(1)}, bf16[784,384]{1,0:T(8,128)(2,1)S(1)}, u32[]{:S(2)}, u32[]{:S(2)}) collective-permute-start(bf16[784,384]{1,0:T(8,128)(2,1)S(1)} %shard_map.113.mine), channel_id=1, source_target_pairs={{0,256},{256,0},{1,257},{257,1},{2,258},{258,2},{3,259},{259,3},{4... | collective-permute-start | bytes 1806344 | tf_op jit(solution)/shard_map/ppermute | solution.py:175
  56.8 2.2 %add_convert_fusion = bf16[8,96,384]{2,1,0:T(8,128)(2,1)} fusion(bf16[8,96,384]{2,1,0:T(8,128)(2,1)} %collective-permute-done.6, bf16[8,96,384]{2,1,0:T(8,128)(2,1)} %get-tuple-element.18), kind=kLoop, calls=%fused_computation.1 | loop fusion | flops 1179648 | bytes 1769472 | tf_op jit(solution)/shard_map/convert_element_type | solution.py:166
  59.0 4.2 %all-to-all-start.1 = ((bf16[8,96,384]{2,1,0:T(8,128)(2,1)}), bf16[8,96,384]{2,1,0:T(8,128)(2,1)}, u32[]{:S(2)}, u32[]{:S(2)}) async-start(bf16[8,96,384]{2,1,0:T(8,128)(2,1)} %add_convert_fusion), calls=%async_computation.1 | async-start | bytes 1179648 | tf_op jit(solution)/shard_map/all_to_all | solution.py:181
  63.2 2.3 %collective-permute-start.4 = (bf16[784,384]{1,0:T(8,128)(2,1)S(1)}, bf16[784,384]{1,0:T(8,128)(2,1)S(1)}, u32[]{:S(2)}, u32[]{:S(2)}) collective-permute-start(bf16[784,384]{1,0:T(8,128)(2,1)S(1)} %shard_map.113.mine), channel_id=1, source_target_pairs={{0,16},{16,0},{1,17},{17,1},{2,18},{18,2},{3,19},{19,3},{4,20},{20... | collective-permute-start | bytes 1806344 | tf_op jit(solution)/shard_map/ppermute | solution.py:176
  65.6 5.5 %collective-permute-done.3.mine_far = bf16[784,384]{1,0:T(8,128)(2,1)S(1)} collective-permute-done((bf16[784,384]{1,0:T(8,128)(2,1)S(1)}, bf16[784,384]{1,0:T(8,128)(2,1)S(1)}, u32[]{:S(2)}, u32[]{:S(2)}) %collective-permute-start.3) | collective-permute-done | bytes 602144 | tf_op jit(solution)/shard_map/ppermute | solution.py:175
  71.1 2.0 %collective-permute-start.5 = (bf16[784,384]{1,0:T(8,128)(2,1)S(1)}, bf16[784,384]{1,0:T(8,128)(2,1)}, u32[]{:S(2)}, u32[]{:S(2)}) collective-permute-start(bf16[784,384]{1,0:T(8,128)(2,1)S(1)} %collective-permute-done.3.mine_far), channel_id=1, source_target_pairs={{0,16},{16,0},{1,17},{17,1},{2,18},{18,2},{3,19},{19,3},{4,20},{20... | collective-permute-start | bytes 1806344 | tf_op jit(solution)/shard_map/ppermute | solution.py:177
  73.2 1.9 %collective-permute-done.5.far_core = bf16[784,384]{1,0:T(8,128)(2,1)} collective-permute-done((bf16[784,384]{1,0:T(8,128)(2,1)S(1)}, bf16[784,384]{1,0:T(8,128)(2,1)}, u32[]{:S(2)}, u32[]{:S(2)}) %collective-permute-start.5) | collective-permute-done | bytes 602144 | tf_op jit(solution)/shard_map/ppermute | solution.py:177
  75.1 4.8 %shard_map.114 = bf16[16,96,384]{2,1,0:T(8,128)(2,1)} custom-call(s32[2]{0:T(128)S(1)} %pad_add_fusion.place, bf16[784,384]{1,0:T(8,128)(2,1)S(1)} %shard_map.113.mine, bf16[784,384]{1,0:T(8,128)(2,1)S(1)} %collective-permute-done.3.mine_far, bf16[784,384]{1,0:T(8,128)(2,1)S(1)} %collective-permute-done.4.mine_core, ...), custom_call_target="tpu_custom_call" | custom-call | flops 1130000000 | bytes 4800000 | tf_op jit(solution)/shard_map/pallas_call | solution.py:121
  79.9 2.7 %all-to-all-done.1 = bf16[8,96,384]{2,1,0:T(8,128)(2,1)} async-done(((bf16[8,96,384]{2,1,0:T(8,128)(2,1)}), bf16[8,96,384]{2,1,0:T(8,128)(2,1)}, u32[]{:S(2)}, u32[]{:S(2)}) %all-to-all-start.1) | async-done | bytes 589856 | tf_op jit(solution)/shard_map/all_to_all | solution.py:181
  82.6 4.0 %all-to-all-start.2 = ((bf16[16,96,384]{2,1,0:T(8,128)(2,1)}), bf16[16,96,384]{2,1,0:T(8,128)(2,1)S(1)}, u32[]{:S(2)}, u32[]{:S(2)}) async-start(bf16[16,96,384]{2,1,0:T(8,128)(2,1)} %shard_map.114), calls=%async_computation.2 | async-start | bytes 2359296 | tf_op jit(solution)/shard_map/all_to_all | solution.py:189
  86.7 1.2 convert_reduce_fusion
  89.4 27.7 %all-to-all-done.2 = bf16[16,96,384]{2,1,0:T(8,128)(2,1)S(1)} async-done(((bf16[16,96,384]{2,1,0:T(8,128)(2,1)}), bf16[16,96,384]{2,1,0:T(8,128)(2,1)S(1)}, u32[]{:S(2)}, u32[]{:S(2)}) %all-to-all-start.2) | async-done | bytes 1179680 | tf_op jit(solution)/shard_map/all_to_all | solution.py:189
  (41 shorter events, 5.2 us)
Async XLA Ops:
  2.9 12.0 %copy-start.4 = (bf16[3072,96]{0,1:T(8,128)(2,1)S(1)}, bf16[3072,96]{0,1:T(8,128)(2,1)}, u32[]{:S(2)}) copy-start(bf16[3072,96]{0,1:T(8,128)(2,1)} %param.12) | copy-start | bytes 1769476
  2.9 48.4 %all-to-all-start = ((bf16[16,120,384]{2,1,0:T(8,128)(2,1)}), bf16[16,120,384]{2,1,0:T(8,128)(2,1)S(1)}, u32[]{:S(2)}, u32[]{:S(2)}) async-start(bf16[16,120,384]{2,1,0:T(8,128)(2,1)} %bitcast.5), calls=%async_computation | async-start | bytes 2949120 | tf_op jit(solution)/shard_map/all_to_all | solution.py:149
  14.8 6.1 %copy-start.3 = (bf16[512,768]{1,0:T(8,128)(2,1)S(1)}, bf16[512,768]{1,0:T(8,128)(2,1)}, u32[]{:S(2)}) copy-start(bf16[512,768]{1,0:T(8,128)(2,1)} %grad.1) | copy-start | bytes 2359300
  14.9 12.3 %collective-permute-start = (bf16[96,1536]{1,0:T(8,128)(2,1)S(1)}, bf16[96,1536]{1,0:T(8,128)(2,1)S(1)}, u32[]{:S(2)}, u32[]{:S(2)}) collective-permute-start(bf16[96,1536]{1,0:T(8,128)(2,1)S(1)} %get-tuple-element.32), channel_id=1, source_target_pairs={{0,256},{256,0},{1,257},{257,1},{2,258},{258,2},{3,259},{259,3},{4... | collective-permute-start | bytes 884744 | tf_op jit(solution)/shard_map/ppermute | solution.py:155
  21.0 1.9 %copy-start.2 = (bf16[512,3072]{1,0:T(8,128)(2,1)S(1)}, bf16[512,3072]{1,0:T(8,128)(2,1)}, u32[]{:S(2)}) copy-start(bf16[512,3072]{1,0:T(8,128)(2,1)} %act.1) | copy-start | bytes 9437188
  26.3 1.0 copy-start
  27.3 5.3 %collective-permute-start.1 = (bf16[2,8,96,384]{3,2,1,0:T(8,128)(2,1)}, bf16[2,8,96,384]{3,2,1,0:T(8,128)(2,1)}, u32[]{:S(2)}, u32[]{:S(2)}) collective-permute-start(bf16[2,8,96,384]{3,2,1,0:T(8,128)(2,1)} %get-tuple-element.17), channel_id=1, source_target_pairs={{0,16},{16,0},{1,17},{17,1},{2,18},{18,2},{3,19},{19,3},{4,20},{20... | collective-permute-start | bytes 3538952 | tf_op jit(solution)/shard_map/ppermute | solution.py:161
  29.8 2.8 %copy-start.1 = (bf16[2,8,96,384]{3,2,1,0:T(8,128)(2,1)S(1)}, bf16[2,8,96,384]{3,2,1,0:T(8,128)(2,1)}, u32[]{:S(2)}) copy-start(bf16[2,8,96,384]{3,2,1,0:T(8,128)(2,1)} %copy-done) | copy-start | bytes 3538948
  29.9 9.9 %collective-permute-start.2 = (bf16[192,1536]{1,0:T(8,128)(2,1)S(1)}, bf16[192,1536]{1,0:T(8,128)(2,1)S(1)}, u32[]{:S(2)}, u32[]{:S(2)}) collective-permute-start(bf16[192,1536]{1,0:T(8,128)(2,1)S(1)} %bitcast.34), channel_id=1, source_target_pairs={{0,16},{16,0},{1,17},{17,1},{2,18},{18,2},{3,19},{19,3},{4,20},{20... | collective-permute-start | bytes 1769480 | tf_op jit(solution)/shard_map/ppermute | solution.py:170
  32.6 7.2 %copy-start.8 = (f32[96]{0:T(128)S(1)}, f32[96]{0:T(128)}, u32[]{:S(2)}) copy-start(f32[96]{0:T(128)} %param.13) | copy-start | bytes 1156
  35.2 21.6 %collective-permute-start.6 = (bf16[8,96,384]{2,1,0:T(8,128)(2,1)}, bf16[8,96,384]{2,1,0:T(8,128)(2,1)}, u32[]{:S(2)}, u32[]{:S(2)}) collective-permute-start(bf16[8,96,384]{2,1,0:T(8,128)(2,1)} %get-tuple-element.29), channel_id=1, source_target_pairs={{0,256},{256,0},{1,257},{257,1},{2,258},{258,2},{3,259},{259,3},{4... | collective-permute-start | bytes 1769480 | tf_op jit(solution)/shard_map/ppermute | solution.py:165
  52.1 21.0 %copy-start.7 = (f32[1,768]{1,0:T(1,128)S(1)}, f32[1,768]{1,0:T(1,128)}, u32[]{:S(2)}) copy-start(f32[1,768]{1,0:T(1,128)} %param.15) | copy-start | bytes 9220
  52.1 19.0 %collective-permute-start.3 = (bf16[784,384]{1,0:T(8,128)(2,1)S(1)}, bf16[784,384]{1,0:T(8,128)(2,1)S(1)}, u32[]{:S(2)}, u32[]{:S(2)}) collective-permute-start(bf16[784,384]{1,0:T(8,128)(2,1)S(1)} %shard_map.113.mine), channel_id=1, source_target_pairs={{0,256},{256,0},{1,257},{257,1},{2,258},{258,2},{3,259},{259,3},{4... | collective-permute-start | bytes 1806344 | tf_op jit(solution)/shard_map/ppermute | solution.py:175
  59.0 23.6 %all-to-all-start.1 = ((bf16[8,96,384]{2,1,0:T(8,128)(2,1)}), bf16[8,96,384]{2,1,0:T(8,128)(2,1)}, u32[]{:S(2)}, u32[]{:S(2)}) async-start(bf16[8,96,384]{2,1,0:T(8,128)(2,1)} %add_convert_fusion), calls=%async_computation.1 | async-start | bytes 1179648 | tf_op jit(solution)/shard_map/all_to_all | solution.py:181
  63.2 9.9 %collective-permute-start.4 = (bf16[784,384]{1,0:T(8,128)(2,1)S(1)}, bf16[784,384]{1,0:T(8,128)(2,1)S(1)}, u32[]{:S(2)}, u32[]{:S(2)}) collective-permute-start(bf16[784,384]{1,0:T(8,128)(2,1)S(1)} %shard_map.113.mine), channel_id=1, source_target_pairs={{0,16},{16,0},{1,17},{17,1},{2,18},{18,2},{3,19},{19,3},{4,20},{20... | collective-permute-start | bytes 1806344 | tf_op jit(solution)/shard_map/ppermute | solution.py:176
  71.1 4.0 %collective-permute-start.5 = (bf16[784,384]{1,0:T(8,128)(2,1)S(1)}, bf16[784,384]{1,0:T(8,128)(2,1)}, u32[]{:S(2)}, u32[]{:S(2)}) collective-permute-start(bf16[784,384]{1,0:T(8,128)(2,1)S(1)} %collective-permute-done.3.mine_far), channel_id=1, source_target_pairs={{0,16},{16,0},{1,17},{17,1},{2,18},{18,2},{3,19},{19,3},{4,20},{20... | collective-permute-start | bytes 1806344 | tf_op jit(solution)/shard_map/ppermute | solution.py:177
  79.9 6.7 %copy-start.5 = (f32[192,96]{1,0:T(8,128)S(1)}, f32[192,96]{1,0:T(8,128)}, u32[]{:S(2)}) copy-start(f32[192,96]{1,0:T(8,128)} %param.16) | copy-start | bytes 221188
  82.6 34.6 %all-to-all-start.2 = ((bf16[16,96,384]{2,1,0:T(8,128)(2,1)}), bf16[16,96,384]{2,1,0:T(8,128)(2,1)S(1)}, u32[]{:S(2)}, u32[]{:S(2)}) async-start(bf16[16,96,384]{2,1,0:T(8,128)(2,1)} %shard_map.114), calls=%async_computation.2 | async-start | bytes 2359296 | tf_op jit(solution)/shard_map/all_to_all | solution.py:189
  86.6 2.2 %copy-start.6 = (f32[1,24,768]{2,1,0:T(8,128)S(1)}, f32[1,24,768]{2,1,0:T(8,128)}, u32[]{:S(2)}) copy-start(f32[1,24,768]{2,1,0:T(8,128)} %param.17) | copy-start | bytes 221188

commit v7 on v6

--- a/solution.py
+++ b/solution.py
@@ -84,7 +84,7 @@
     return jnp.sum(jnp.where(ids, jnp.broadcast_to(row, (96, 128)), 0.0), axis=1, keepdims=True)
 
 
-def tail_kernel(place, mine, mine_far, mine_core, far_core, eigen, eigen_out, near, far, out):
+def tail_kernel(place, mine, mine_far, mine_core, far_core, eigen, eigen_out, near, far, out, held, sems):
     same = place[0] == place[1]
 
     def third(group):
@@ -109,11 +109,17 @@
             denominator = eigen_rows * eigen_out[:, at * 384 : (at + 1) * 384] + damping
             scaled.append((rotated / denominator).astype(bf16))
         backs.append((dot(scaled[0], half_first, 1, 1) + dot(scaled[1], half_second, 1, 1)).astype(bf16))
+    copies = []
     for j in range(4):
         part = dot(near[:, j * 384 : (j + 1) * 384], backs[0], 0, 0)
         part += dot(far[:, j * 384 : (j + 1) * 384], backs[1], 0, 0)
         for i in range(4):
-            out[j * 4 + i] = part[i * 96 : (i + 1) * 96, :].astype(bf16)
+            held[j * 4 + i] = part[i * 96 : (i + 1) * 96, :].astype(bf16)
+        quarter = pl.ds(j * 4, 4)
+        copies.append(pltpu.make_async_copy(held.at[quarter], out.at[quarter], sems.at[j]))
+        copies[-1].start()
+    for copy in copies:
+        copy.wait()
 
 
 def tail(place, *arrays):
@@ -122,7 +128,8 @@
         tail_kernel,
         out_shape=jax.ShapeDtypeStruct((16, 96, 384), bf16),
         in_specs=[pl.BlockSpec(memory_space=pltpu.SMEM)] + [vmem] * len(arrays),
-        out_specs=vmem,
+        out_specs=pl.BlockSpec(memory_space=pltpu.HBM),
+        scratch_shapes=[pltpu.VMEM((16, 96, 384), bf16), pltpu.SemaphoreType.DMA((4,))],
         compiler_params=pltpu.CompilerParams(vmem_limit_bytes=24 * 1024 * 1024),
         cost_estimate=pl.CostEstimate(flops=1_130_000_000, bytes_accessed=4_800_000, transcendentals=0),
     )(place, *arrays)

time: 119 us -> 119 us (level)
  transfers between devices with their start and end apart: 10 -> 10, of which waited for: 6 -> 6; matrix products, arithmetic and copies ran while one was open for 8% -> 8% of each run, Pallas kernels for 8% -> 7%
where the time goes in v7:
time: 119 us; the launch traced here: 118 us
  waiting for transfers between devices  50.2 us (42%)
  starting transfers between devices  43.2 us (36%)
  Pallas kernels  8.74 us (7%)
  other arithmetic  8.62 us (7%)
  local copies, waits for them, and re-layouts  6.35 us (5%)
    all_to_all x1, waiting for transfers between devices, per_device(): lax.all_to_all(out_part, ('z', 'c'), 0, 0).reshape(8, 2, 96, 384)  27.7 us
    all_to_all x1, starting transfers between devices, per_device(): came_rows = lax.all_to_all(send, ('z', 'c'), 0, 0)  12 us
    all_to_all x1, waiting for transfers between devices, per_device(): came_rows = lax.all_to_all(send, ('z', 'c'), 0, 0)  11.4 us
    ppermute x1, waiting for transfers between devices, per_device(): far_rows = lax.ppermute(mine_rows, 'xh', swap)  5.51 us
    ppermute x1, starting transfers between devices, per_device(): ut_far = lax.ppermute(ut_other, 'xh', swap)  4.81 us
    ppermute x1, starting transfers between devices, per_device(): far_rows = lax.ppermute(mine_rows, 'xh', swap)  4.65 us
    ppermute x1, starting transfers between devices, per_device(): came = lax.ppermute(pair_far, 'xh', swap)  4.64 us
    pallas_call x1, Pallas kernels, tail(): pl.pallas_call(tail_kernel, out_shape=jax.ShapeDtypeStruct((16, 96, 384),...  4.54 us
  transfers between devices with their start and end apart: 10, of which 6 were waited for; matrix products, arithmetic and copies ran while one was open for 8% of the time, Pallas kernels for 7%

profile of v7, /device:TPU:1, one launch (start us, length us, event | category | flops | bytes accessed | tf_op | source)
XLA Modules:
  0.0 118.1 jit_solution(16917414013022924830)
XLA Ops:
  1.6 1.3 %broadcast_in_dim.2 = bf16[8,2,120,384]{3,2,1,0:T(8,128)(2,1)} broadcast(bf16[2,120,384]{2,1,0:T(8,128)(2,1)S(1)} %pad_maximum_fusion), dimensions={1,2,3} | broadcast | bytes 1658880 | tf_op jit(solution)/shard_map/broadcast_in_dim | solution.py:155
  2.9 12.0 %all-to-all-start = ((bf16[16,120,384]{2,1,0:T(8,128)(2,1)}), bf16[16,120,384]{2,1,0:T(8,128)(2,1)S(1)}, u32[]{:S(2)}, u32[]{:S(2)}) async-start(bf16[16,120,384]{2,1,0:T(8,128)(2,1)} %bitcast.5), calls=%async_computation | async-start | bytes 2949120 | tf_op jit(solution)/shard_map/all_to_all | solution.py:156
  14.9 4.8 %collective-permute-start = (bf16[96,1536]{1,0:T(8,128)(2,1)S(1)}, bf16[96,1536]{1,0:T(8,128)(2,1)S(1)}, u32[]{:S(2)}, u32[]{:S(2)}) collective-permute-start(bf16[96,1536]{1,0:T(8,128)(2,1)S(1)} %get-tuple-element.32), channel_id=1, source_target_pairs={{0,256},{256,0},{1,257},{257,1},{2,258},{258,2},{3,259},{259,3},{4... | collective-permute-start | bytes 884744 | tf_op jit(solution)/shard_map/ppermute | solution.py:162
  19.8 1.1 constant_dynamic-slice_fusion.sel
  21.0 1.9 %copy-done.2 = bf16[512,3072]{1,0:T(8,128)(2,1)S(1)} copy-done((bf16[512,3072]{1,0:T(8,128)(2,1)S(1)}, bf16[512,3072]{1,0:T(8,128)(2,1)}, u32[]{:S(2)}) %copy-start.2) | copy-done | bytes 3145752
  22.9 3.4 %shard_map.112 = (bf16[2,8,96,384]{3,2,1,0:T(8,128)(2,1)S(1)}, bf16[2,8,96,384]{3,2,1,0:T(8,128)(2,1)}) custom-call(s32[2]{0:T(128)S(1)} %pad_add_fusion.place, bf16[512,3072]{1,0:T(8,128)(2,1)S(1)} %copy-done.2, bf16[512,192]{1,0:T(8,128)(2,1)S(1)} %constant_dynamic-slice_fusion.sel, bf16[512,768]{1,0:T(8,128)(2,1)S(1)} %copy-done.3), custom_call_target="tpu_custom_call" | custom-call | flops 1250000000 | bytes 8000000 | tf_op jit(solution)/shard_map/pallas_call | solution.py:43
  26.3 1.0 copy-done
  27.3 2.5 %collective-permute-start.1 = (bf16[2,8,96,384]{3,2,1,0:T(8,128)(2,1)}, bf16[2,8,96,384]{3,2,1,0:T(8,128)(2,1)}, u32[]{:S(2)}, u32[]{:S(2)}) collective-permute-start(bf16[2,8,96,384]{3,2,1,0:T(8,128)(2,1)} %get-tuple-element.17), channel_id=1, source_target_pairs={{0,16},{16,0},{1,17},{17,1},{2,18},{18,2},{3,19},{19,3},{4,20},{20... | collective-permute-start | bytes 3538952 | tf_op jit(solution)/shard_map/ppermute | solution.py:168
  29.9 2.1 %collective-permute-start.2 = (bf16[192,1536]{1,0:T(8,128)(2,1)S(1)}, bf16[192,1536]{1,0:T(8,128)(2,1)S(1)}, u32[]{:S(2)}, u32[]{:S(2)}) collective-permute-start(bf16[192,1536]{1,0:T(8,128)(2,1)S(1)} %bitcast.34), channel_id=1, source_target_pairs={{0,16},{16,0},{1,17},{17,1},{2,18},{18,2},{3,19},{19,3},{4,20},{20... | collective-permute-start | bytes 1769480 | tf_op jit(solution)/shard_map/ppermute | solution.py:177
  32.6 2.6 %fusion.1 = (bf16[8,96,384]{2,1,0:T(8,128)(2,1)}, bf16[8,96,384]{2,1,0:T(8,128)(2,1)}) fusion(bf16[2,8,96,384]{3,2,1,0:T(8,128)(2,1)} %collective-permute-done.1, bf16[2,8,96,384]{3,2,1,0:T(8,128)(2,1)S(1)} %copy-done.1), kind=kLoop, calls=%fused_computation.5 | loop fusion | flops 2359296 | bytes 3538944 | tf_op jit(solution)/shard_map/convert_element_type | solution.py:169
  35.2 4.6 %collective-permute-start.6 = (bf16[8,96,384]{2,1,0:T(8,128)(2,1)}, bf16[8,96,384]{2,1,0:T(8,128)(2,1)}, u32[]{:S(2)}, u32[]{:S(2)}) collective-permute-start(bf16[8,96,384]{2,1,0:T(8,128)(2,1)} %get-tuple-element.29), channel_id=1, source_target_pairs={{0,256},{256,0},{1,257},{257,1},{2,258},{258,2},{3,259},{259,3},{4... | collective-permute-start | bytes 1769480 | tf_op jit(solution)/shard_map/ppermute | solution.py:172
  39.9 11.4 %all-to-all-done.came = bf16[16,120,384]{2,1,0:T(8,128)(2,1)S(1)} async-done(((bf16[16,120,384]{2,1,0:T(8,128)(2,1)}), bf16[16,120,384]{2,1,0:T(8,128)(2,1)S(1)}, u32[]{:S(2)}, u32[]{:S(2)}) %all-to-all-start) | async-done | bytes 1474592 | tf_op jit(solution)/shard_map/all_to_all | solution.py:156
  52.1 4.7 %collective-permute-start.3 = (bf16[784,384]{1,0:T(8,128)(2,1)S(1)}, bf16[784,384]{1,0:T(8,128)(2,1)S(1)}, u32[]{:S(2)}, u32[]{:S(2)}) collective-permute-start(bf16[784,384]{1,0:T(8,128)(2,1)S(1)} %shard_map.113.mine), channel_id=1, source_target_pairs={{0,256},{256,0},{1,257},{257,1},{2,258},{258,2},{3,259},{259,3},{4... | collective-permute-start | bytes 1806344 | tf_op jit(solution)/shard_map/ppermute | solution.py:182
  56.8 2.2 %add_convert_fusion = bf16[8,96,384]{2,1,0:T(8,128)(2,1)} fusion(bf16[8,96,384]{2,1,0:T(8,128)(2,1)} %collective-permute-done.6, bf16[8,96,384]{2,1,0:T(8,128)(2,1)} %get-tuple-element.18), kind=kLoop, calls=%fused_computation.1 | loop fusion | flops 1179648 | bytes 1769472 | tf_op jit(solution)/shard_map/convert_element_type | solution.py:173
  59.0 4.2 %all-to-all-start.1 = ((bf16[8,96,384]{2,1,0:T(8,128)(2,1)}), bf16[8,96,384]{2,1,0:T(8,128)(2,1)}, u32[]{:S(2)}, u32[]{:S(2)}) async-start(bf16[8,96,384]{2,1,0:T(8,128)(2,1)} %add_convert_fusion), calls=%async_computation.1 | async-start | bytes 1179648 | tf_op jit(solution)/shard_map/all_to_all | solution.py:188
  63.2 2.3 %collective-permute-start.4 = (bf16[784,384]{1,0:T(8,128)(2,1)S(1)}, bf16[784,384]{1,0:T(8,128)(2,1)S(1)}, u32[]{:S(2)}, u32[]{:S(2)}) collective-permute-start(bf16[784,384]{1,0:T(8,128)(2,1)S(1)} %shard_map.113.mine), channel_id=1, source_target_pairs={{0,16},{16,0},{1,17},{17,1},{2,18},{18,2},{3,19},{19,3},{4,20},{20... | collective-permute-start | bytes 1806344 | tf_op jit(solution)/shard_map/ppermute | solution.py:183
  65.6 5.5 %collective-permute-done.3.mine_far = bf16[784,384]{1,0:T(8,128)(2,1)S(1)} collective-permute-done((bf16[784,384]{1,0:T(8,128)(2,1)S(1)}, bf16[784,384]{1,0:T(8,128)(2,1)S(1)}, u32[]{:S(2)}, u32[]{:S(2)}) %collective-permute-start.3) | collective-permute-done | bytes 602144 | tf_op jit(solution)/shard_map/ppermute | solution.py:182
  71.1 2.0 %collective-permute-start.5 = (bf16[784,384]{1,0:T(8,128)(2,1)S(1)}, bf16[784,384]{1,0:T(8,128)(2,1)}, u32[]{:S(2)}, u32[]{:S(2)}) collective-permute-start(bf16[784,384]{1,0:T(8,128)(2,1)S(1)} %collective-permute-done.3.mine_far), channel_id=1, source_target_pairs={{0,16},{16,0},{1,17},{17,1},{2,18},{18,2},{3,19},{19,3},{4,20},{20... | collective-permute-start | bytes 1806344 | tf_op jit(solution)/shard_map/ppermute | solution.py:184
  73.2 1.9 %collective-permute-done.5.far_core = bf16[784,384]{1,0:T(8,128)(2,1)} collective-permute-done((bf16[784,384]{1,0:T(8,128)(2,1)S(1)}, bf16[784,384]{1,0:T(8,128)(2,1)}, u32[]{:S(2)}, u32[]{:S(2)}) %collective-permute-start.5) | collective-permute-done | bytes 602144 | tf_op jit(solution)/shard_map/ppermute | solution.py:184
  75.1 4.5 %shard_map.114 = bf16[16,96,384]{2,1,0:T(8,128)(2,1)} custom-call(s32[2]{0:T(128)S(1)} %pad_add_fusion.place, bf16[784,384]{1,0:T(8,128)(2,1)S(1)} %shard_map.113.mine, bf16[784,384]{1,0:T(8,128)(2,1)S(1)} %collective-permute-done.3.mine_far, bf16[784,384]{1,0:T(8,128)(2,1)S(1)} %collective-permute-done.4.mine_core, ...), custom_call_target="tpu_custom_call" | custom-call | flops 1130000000 | bytes 4800000 | tf_op jit(solution)/shard_map/pallas_call | solution.py:127
  79.7 2.9 %all-to-all-done.1 = bf16[8,96,384]{2,1,0:T(8,128)(2,1)} async-done(((bf16[8,96,384]{2,1,0:T(8,128)(2,1)}), bf16[8,96,384]{2,1,0:T(8,128)(2,1)}, u32[]{:S(2)}, u32[]{:S(2)}) %all-to-all-start.1) | async-done | bytes 589856 | tf_op jit(solution)/shard_map/all_to_all | solution.py:188
  82.6 4.0 %all-to-all-start.2 = ((bf16[16,96,384]{2,1,0:T(8,128)(2,1)}), bf16[16,96,384]{2,1,0:T(8,128)(2,1)S(1)}, u32[]{:S(2)}, u32[]{:S(2)}) async-start(bf16[16,96,384]{2,1,0:T(8,128)(2,1)} %shard_map.114), calls=%async_computation.2 | async-start | bytes 2359296 | tf_op jit(solution)/shard_map/all_to_all | solution.py:196
  86.7 1.2 convert_reduce_fusion
  89.4 27.7 %all-to-all-done.2 = bf16[16,96,384]{2,1,0:T(8,128)(2,1)S(1)} async-done(((bf16[16,96,384]{2,1,0:T(8,128)(2,1)}), bf16[16,96,384]{2,1,0:T(8,128)(2,1)S(1)}, u32[]{:S(2)}, u32[]{:S(2)}) %all-to-all-start.2) | async-done | bytes 1179680 | tf_op jit(solution)/shard_map/all_to_all | solution.py:196
  (41 shorter events, 5.2 us)
Async XLA Ops:
  2.9 12.0 %copy-start.4 = (bf16[3072,96]{0,1:T(8,128)(2,1)S(1)}, bf16[3072,96]{0,1:T(8,128)(2,1)}, u32[]{:S(2)}) copy-start(bf16[3072,96]{0,1:T(8,128)(2,1)} %param.12) | copy-start | bytes 1769476
  2.9 48.4 %all-to-all-start = ((bf16[16,120,384]{2,1,0:T(8,128)(2,1)}), bf16[16,120,384]{2,1,0:T(8,128)(2,1)S(1)}, u32[]{:S(2)}, u32[]{:S(2)}) async-start(bf16[16,120,384]{2,1,0:T(8,128)(2,1)} %bitcast.5), calls=%async_computation | async-start | bytes 2949120 | tf_op jit(solution)/shard_map/all_to_all | solution.py:156
  14.8 6.1 %copy-start.3 = (bf16[512,768]{1,0:T(8,128)(2,1)S(1)}, bf16[512,768]{1,0:T(8,128)(2,1)}, u32[]{:S(2)}) copy-start(bf16[512,768]{1,0:T(8,128)(2,1)} %grad.1) | copy-start | bytes 2359300
  14.9 12.3 %collective-permute-start = (bf16[96,1536]{1,0:T(8,128)(2,1)S(1)}, bf16[96,1536]{1,0:T(8,128)(2,1)S(1)}, u32[]{:S(2)}, u32[]{:S(2)}) collective-permute-start(bf16[96,1536]{1,0:T(8,128)(2,1)S(1)} %get-tuple-element.32), channel_id=1, source_target_pairs={{0,256},{256,0},{1,257},{257,1},{2,258},{258,2},{3,259},{259,3},{4... | collective-permute-start | bytes 884744 | tf_op jit(solution)/shard_map/ppermute | solution.py:162
  21.0 1.9 %copy-start.2 = (bf16[512,3072]{1,0:T(8,128)(2,1)S(1)}, bf16[512,3072]{1,0:T(8,128)(2,1)}, u32[]{:S(2)}) copy-start(bf16[512,3072]{1,0:T(8,128)(2,1)} %act.1) | copy-start | bytes 9437188
  26.3 1.0 copy-start
  27.3 5.3 %collective-permute-start.1 = (bf16[2,8,96,384]{3,2,1,0:T(8,128)(2,1)}, bf16[2,8,96,384]{3,2,1,0:T(8,128)(2,1)}, u32[]{:S(2)}, u32[]{:S(2)}) collective-permute-start(bf16[2,8,96,384]{3,2,1,0:T(8,128)(2,1)} %get-tuple-element.17), channel_id=1, source_target_pairs={{0,16},{16,0},{1,17},{17,1},{2,18},{18,2},{3,19},{19,3},{4,20},{20... | collective-permute-start | bytes 3538952 | tf_op jit(solution)/shard_map/ppermute | solution.py:168
  29.8 2.8 %copy-start.1 = (bf16[2,8,96,384]{3,2,1,0:T(8,128)(2,1)S(1)}, bf16[2,8,96,384]{3,2,1,0:T(8,128)(2,1)}, u32[]{:S(2)}) copy-start(bf16[2,8,96,384]{3,2,1,0:T(8,128)(2,1)} %copy-done) | copy-start | bytes 3538948
  29.9 9.9 %collective-permute-start.2 = (bf16[192,1536]{1,0:T(8,128)(2,1)S(1)}, bf16[192,1536]{1,0:T(8,128)(2,1)S(1)}, u32[]{:S(2)}, u32[]{:S(2)}) collective-permute-start(bf16[192,1536]{1,0:T(8,128)(2,1)S(1)} %bitcast.34), channel_id=1, source_target_pairs={{0,16},{16,0},{1,17},{17,1},{2,18},{18,2},{3,19},{19,3},{4,20},{20... | collective-permute-start | bytes 1769480 | tf_op jit(solution)/shard_map/ppermute | solution.py:177
  32.6 7.2 %copy-start.8 = (f32[96]{0:T(128)S(1)}, f32[96]{0:T(128)}, u32[]{:S(2)}) copy-start(f32[96]{0:T(128)} %param.13) | copy-start | bytes 1156
  35.2 21.6 %collective-permute-start.6 = (bf16[8,96,384]{2,1,0:T(8,128)(2,1)}, bf16[8,96,384]{2,1,0:T(8,128)(2,1)}, u32[]{:S(2)}, u32[]{:S(2)}) collective-permute-start(bf16[8,96,384]{2,1,0:T(8,128)(2,1)} %get-tuple-element.29), channel_id=1, source_target_pairs={{0,256},{256,0},{1,257},{257,1},{2,258},{258,2},{3,259},{259,3},{4... | collective-permute-start | bytes 1769480 | tf_op jit(solution)/shard_map/ppermute | solution.py:172
  52.1 21.0 %copy-start.7 = (f32[1,768]{1,0:T(1,128)S(1)}, f32[1,768]{1,0:T(1,128)}, u32[]{:S(2)}) copy-start(f32[1,768]{1,0:T(1,128)} %param.15) | copy-start | bytes 9220
  52.1 19.0 %collective-permute-start.3 = (bf16[784,384]{1,0:T(8,128)(2,1)S(1)}, bf16[784,384]{1,0:T(8,128)(2,1)S(1)}, u32[]{:S(2)}, u32[]{:S(2)}) collective-permute-start(bf16[784,384]{1,0:T(8,128)(2,1)S(1)} %shard_map.113.mine), channel_id=1, source_target_pairs={{0,256},{256,0},{1,257},{257,1},{2,258},{258,2},{3,259},{259,3},{4... | collective-permute-start | bytes 1806344 | tf_op jit(solution)/shard_map/ppermute | solution.py:182
  59.0 23.6 %all-to-all-start.1 = ((bf16[8,96,384]{2,1,0:T(8,128)(2,1)}), bf16[8,96,384]{2,1,0:T(8,128)(2,1)}, u32[]{:S(2)}, u32[]{:S(2)}) async-start(bf16[8,96,384]{2,1,0:T(8,128)(2,1)} %add_convert_fusion), calls=%async_computation.1 | async-start | bytes 1179648 | tf_op jit(solution)/shard_map/all_to_all | solution.py:188
  63.2 9.9 %collective-permute-start.4 = (bf16[784,384]{1,0:T(8,128)(2,1)S(1)}, bf16[784,384]{1,0:T(8,128)(2,1)S(1)}, u32[]{:S(2)}, u32[]{:S(2)}) collective-permute-start(bf16[784,384]{1,0:T(8,128)(2,1)S(1)} %shard_map.113.mine), channel_id=1, source_target_pairs={{0,16},{16,0},{1,17},{17,1},{2,18},{18,2},{3,19},{19,3},{4,20},{20... | collective-permute-start | bytes 1806344 | tf_op jit(solution)/shard_map/ppermute | solution.py:183
  71.1 4.0 %collective-permute-start.5 = (bf16[784,384]{1,0:T(8,128)(2,1)S(1)}, bf16[784,384]{1,0:T(8,128)(2,1)}, u32[]{:S(2)}, u32[]{:S(2)}) collective-permute-start(bf16[784,384]{1,0:T(8,128)(2,1)S(1)} %collective-permute-done.3.mine_far), channel_id=1, source_target_pairs={{0,16},{16,0},{1,17},{17,1},{2,18},{18,2},{3,19},{19,3},{4,20},{20... | collective-permute-start | bytes 1806344 | tf_op jit(solution)/shard_map/ppermute | solution.py:184
  79.7 6.9 %copy-start.5 = (f32[192,96]{1,0:T(8,128)S(1)}, f32[192,96]{1,0:T(8,128)}, u32[]{:S(2)}) copy-start(f32[192,96]{1,0:T(8,128)} %param.16) | copy-start | bytes 221188
  82.6 34.6 %all-to-all-start.2 = ((bf16[16,96,384]{2,1,0:T(8,128)(2,1)}), bf16[16,96,384]{2,1,0:T(8,128)(2,1)S(1)}, u32[]{:S(2)}, u32[]{:S(2)}) async-start(bf16[16,96,384]{2,1,0:T(8,128)(2,1)} %shard_map.114), calls=%async_computation.2 | async-start | bytes 2359296 | tf_op jit(solution)/shard_map/all_to_all | solution.py:196
  86.6 2.2 %copy-start.6 = (f32[1,24,768]{2,1,0:T(8,128)S(1)}, f32[1,24,768]{2,1,0:T(8,128)}, u32[]{:S(2)}) copy-start(f32[1,24,768]{2,1,0:T(8,128)} %param.17) | copy-start | bytes 221188

commit v8 on v7

--- a/solution.py
+++ b/solution.py
@@ -21,10 +21,12 @@
     return lax.dynamic_index_in_dim(a, index, axis, keepdims=False)
 
 
-def factor_kernel(place, act, sel, grad, mine, other, t_in, t_out):
+def factor_kernel(place, act, grad, mine, other, t_in, t_out):
     xh, c = place[0], place[1]
+    both = act[:, pl.ds(pl.multiple_of(place[3] * 128, 128), 256)].astype(f32)
+    sel = jnp.where(place[2] == 1, pltpu.roll(both, 192, 1), both)[:, :192].astype(bf16)
     for j in range(8):
-        t_in[j * 384 : (j + 1) * 384, :] = dot(act[:, j * 384 : (j + 1) * 384], sel[...], 0, 0)
+        t_in[j * 384 : (j + 1) * 384, :] = dot(act[:, j * 384 : (j + 1) * 384], sel, 0, 0)
     for j in range(2):
         t_out[j * 384 : (j + 1) * 384, :] = dot(grad[:, j * 384 : (j + 1) * 384], grad[...], 0, 0)
     for target, core_at in ((mine, c), (other, 1 - c)):
@@ -38,17 +40,17 @@
                 target[side, z, 48:96, :] = jnp.concatenate([part[:, :384], part[:, 384:]], axis=0).astype(bf16)
 
 
-def factor_parts(place, act, sel, grad):
+def factor_parts(place, act, grad):
     vmem = pl.BlockSpec(memory_space=pltpu.VMEM)
     return pl.pallas_call(
         factor_kernel,
         out_shape=[jax.ShapeDtypeStruct((2, 8, 96, 384), bf16)] * 2,
-        in_specs=[pl.BlockSpec(memory_space=pltpu.SMEM), vmem, vmem, vmem],
+        in_specs=[pl.BlockSpec(memory_space=pltpu.SMEM), vmem, vmem],
         out_specs=[vmem, vmem],
         scratch_shapes=[pltpu.VMEM((3072, 192), f32), pltpu.VMEM((768, 768), f32)],
         compiler_params=pltpu.CompilerParams(vmem_limit_bytes=32 * 1024 * 1024),
         cost_estimate=pl.CostEstimate(flops=1_250_000_000, bytes_accessed=8_000_000, transcendentals=0),
-    )(place, act, sel, grad)
+    )(place, act, grad)
 
 
 def left_kernel(near, far, came, eigen, out, rows):
@@ -161,16 +163,14 @@
     ut_other = lax.dynamic_slice_in_dim(ut, (1 - xh) * 1536, 1536, 1)
     ut_far = lax.ppermute(ut_other, "xh", swap)
 
-    selected = lax.dynamic_slice_in_dim(activations, m * 192, 192, 1)
-    place = jnp.stack([xh, c]).astype(jnp.int32)
-    mine, other = factor_parts(place, activations, selected, output_grad)
+    place = jnp.stack([xh, c, m % 2, (m * 3) // 2]).astype(jnp.int32)
+    mine, other = factor_parts(place, activations, output_grad)
     other, ut_far = lax.optimization_barrier((other, ut_far))
     came = lax.ppermute(other, "c", swap)
     pair_far = (mine[1].astype(f32) + came[1].astype(f32)).astype(bf16)
-    pair_near = (mine[0].astype(f32) + came[0].astype(f32)).astype(bf16)
-    pair_near, _ = lax.optimization_barrier((pair_near, pair_far))
-    came = lax.ppermute(pair_far, "xh", swap)
-    four = (pair_near.astype(f32) + came.astype(f32)).astype(bf16)
+    own, _ = lax.optimization_barrier((mine[0], pair_far))
+    pair_near = (own.astype(f32) + came[0].astype(f32)).astype(bf16)
+    sides_far = lax.ppermute(pair_far, "xh", swap)
 
     near = jnp.where(xh == 0, jnp.stack([ut_mine, ut_far]), jnp.stack([ut_far, ut_mine]))
     near = near.reshape(192, 1536)
@@ -180,6 +180,8 @@
     eigen = jnp.pad(input_eigen, (0, 32)).reshape(1, 128)
     mine_rows = left_parts(near, far, came_rows, eigen)
     far_rows = lax.ppermute(mine_rows, "xh", swap)
+    pair_near, _ = lax.optimization_barrier((pair_near, mine_rows))
+    four = (pair_near.astype(f32) + sides_far.astype(f32)).astype(bf16)
     core_rows = lax.ppermute(mine_rows, "c", swap)
     far_core = lax.ppermute(far_rows, "c", swap)
     eigen_out = jnp.where(c == 0, output_eigen, jnp.concatenate([output_eigen[:, 384:], output_eigen[:, :384]], axis=1))

time: 119 us -> 119 us (level)
  other arithmetic: 8.62 us -> 9.94 us
    convert_element_type x1 -> x2, other arithmetic: 2.22 us -> 4.09 us  [the longest x1 2.05 us: per_device(): four = (pair_near.astype(f32) + sides_far.astype(f32)).astype(bf16)]
    all_to_all x1, waiting for transfers between devices: 11.4 us -> 9.89 us  [per_device(): came_rows = lax.all_to_all(send, ('z', 'c'), 0, 0)]
    unnamed x20 -> x22, local copies, waits for them, and re-layouts: 3.75 us -> 3.76 us
  transfers between devices with their start and end apart: 10 -> 10, of which waited for: 6 -> 7; matrix products, arithmetic and copies ran while one was open for 8% -> 8% of each run, Pallas kernels for 7% -> 7%
where the time goes in v8:
time: 119 us; the launch traced here: 118 us
  waiting for transfers between devices  49.8 us (42%)
  starting transfers between devices  43.2 us (36%)
  other arithmetic  9.94 us (8%)
  Pallas kernels  8.75 us (7%)
  local copies, waits for them, and re-layouts  5.29 us (4%)
    all_to_all x1, waiting for transfers between devices, per_device(): lax.all_to_all(out_part, ('z', 'c'), 0, 0).reshape(8, 2, 96, 384)  27.7 us
    all_to_all x1, starting transfers between devices, per_device(): came_rows = lax.all_to_all(send, ('z', 'c'), 0, 0)  12 us
    all_to_all x1, waiting for transfers between devices, per_device(): came_rows = lax.all_to_all(send, ('z', 'c'), 0, 0)  9.89 us
    ppermute x1, waiting for transfers between devices, per_device(): far_rows = lax.ppermute(mine_rows, 'xh', swap)  5.94 us
    ppermute x1, starting transfers between devices, per_device(): ut_far = lax.ppermute(ut_other, 'xh', swap)  4.81 us
    ppermute x1, starting transfers between devices, per_device(): far_rows = lax.ppermute(mine_rows, 'xh', swap)  4.65 us
    ppermute x1, starting transfers between devices, per_device(): sides_far = lax.ppermute(pair_far, 'xh', swap)  4.64 us
    pallas_call x1, Pallas kernels, tail(): pl.pallas_call(tail_kernel, out_shape=jax.ShapeDtypeStruct((16, 96, 384),...  4.49 us
  transfers between devices with their start and end apart: 10, of which 7 were waited for; matrix products, arithmetic and copies ran while one was open for 8% of the time, Pallas kernels for 7%

profile of v8, /device:TPU:1, one launch (start us, length us, event | category | flops | bytes accessed | tf_op | source)
XLA Modules:
  0.0 117.9 jit_solution(936443863703598370)
XLA Ops:
  1.6 1.3 %broadcast_in_dim.2 = bf16[8,2,120,384]{3,2,1,0:T(8,128)(2,1)} broadcast(bf16[2,120,384]{2,1,0:T(8,128)(2,1)S(1)} %pad_maximum_fusion), dimensions={1,2,3} | broadcast | bytes 1658880 | tf_op jit(solution)/shard_map/broadcast_in_dim | solution.py:157
  2.9 12.0 %all-to-all-start = ((bf16[16,120,384]{2,1,0:T(8,128)(2,1)}), bf16[16,120,384]{2,1,0:T(8,128)(2,1)S(1)}, u32[]{:S(2)}, u32[]{:S(2)}) async-start(bf16[16,120,384]{2,1,0:T(8,128)(2,1)} %bitcast.7), calls=%async_computation | async-start | bytes 2949120 | tf_op jit(solution)/shard_map/all_to_all | solution.py:158
  14.9 4.8 %collective-permute-start = (bf16[96,1536]{1,0:T(8,128)(2,1)S(1)}, bf16[96,1536]{1,0:T(8,128)(2,1)S(1)}, u32[]{:S(2)}, u32[]{:S(2)}) collective-permute-start(bf16[96,1536]{1,0:T(8,128)(2,1)S(1)} %get-tuple-element.34), channel_id=1, source_target_pairs={{0,256},{256,0},{1,257},{257,1},{2,258},{258,2},{3,259},{259,3},{4... | collective-permute-start | bytes 884744 | tf_op jit(solution)/shard_map/ppermute | solution.py:164
  19.8 1.9 %copy-done.2 = bf16[512,3072]{1,0:T(8,128)(2,1)S(1)} copy-done((bf16[512,3072]{1,0:T(8,128)(2,1)S(1)}, bf16[512,3072]{1,0:T(8,128)(2,1)}, u32[]{:S(2)}) %copy-start.2) | copy-done | bytes 3145752
  21.7 3.5 %shard_map.112 = (bf16[2,8,96,384]{3,2,1,0:T(8,128)(2,1)S(1)}, bf16[2,8,96,384]{3,2,1,0:T(8,128)(2,1)}) custom-call(s32[4]{0:T(128)S(1)} %pad_add_fusion.place, bf16[512,3072]{1,0:T(8,128)(2,1)S(1)} %copy-done.2, bf16[512,768]{1,0:T(8,128)(2,1)S(1)} %copy-done.3), custom_call_target="tpu_custom_call" | custom-call | flops 1250000000 | bytes 8000000 | tf_op jit(solution)/shard_map/pallas_call | solution.py:45
  25.2 1.0 copy-done
  27.0 2.8 %collective-permute-start.1 = (bf16[2,8,96,384]{3,2,1,0:T(8,128)(2,1)}, bf16[2,8,96,384]{3,2,1,0:T(8,128)(2,1)}, u32[]{:S(2)}, u32[]{:S(2)}) collective-permute-start(bf16[2,8,96,384]{3,2,1,0:T(8,128)(2,1)} %get-tuple-element.19), channel_id=1, source_target_pairs={{0,16},{16,0},{1,17},{17,1},{2,18},{18,2},{3,19},{19,3},{4,20},{20... | collective-permute-start | bytes 3538952 | tf_op jit(solution)/shard_map/ppermute | solution.py:169
  29.9 2.1 %collective-permute-start.2 = (bf16[192,1536]{1,0:T(8,128)(2,1)S(1)}, bf16[192,1536]{1,0:T(8,128)(2,1)S(1)}, u32[]{:S(2)}, u32[]{:S(2)}) collective-permute-start(bf16[192,1536]{1,0:T(8,128)(2,1)S(1)} %bitcast.41), channel_id=1, source_target_pairs={{0,16},{16,0},{1,17},{17,1},{2,18},{18,2},{3,19},{19,3},{4,20},{20... | collective-permute-start | bytes 1769480 | tf_op jit(solution)/shard_map/ppermute | solution.py:177
  32.6 2.0 %fusion.1 = bf16[8,96,384]{2,1,0:T(8,128)(2,1)} fusion(bf16[2,8,96,384]{3,2,1,0:T(8,128)(2,1)} %collective-permute-done.1, bf16[2,8,96,384]{3,2,1,0:T(8,128)(2,1)S(1)} %copy-done.1), kind=kLoop, calls=%fused_computation.5 | loop fusion | flops 1179648 | bytes 1769472 | tf_op jit(solution)/shard_map/convert_element_type | solution.py:170
  34.6 4.6 %collective-permute-start.6 = (bf16[8,96,384]{2,1,0:T(8,128)(2,1)}, bf16[8,96,384]{2,1,0:T(8,128)(2,1)}, u32[]{:S(2)}, u32[]{:S(2)}) collective-permute-start(bf16[8,96,384]{2,1,0:T(8,128)(2,1)} %fusion.1), channel_id=1, source_target_pairs={{0,256},{256,0},{1,257},{257,1},{2,258},{258,2},{3,259},{259,3},{4... | collective-permute-start | bytes 1769480 | tf_op jit(solution)/shard_map/ppermute | solution.py:173
  39.4 2.0 %fusion = bf16[8,96,384]{2,1,0:T(8,128)(2,1)} fusion(bf16[8,96,384]{2,1,0:T(8,128)(2,1)S(1)} %slice_bitcast_fusion.1, bf16[2,8,96,384]{3,2,1,0:T(8,128)(2,1)} %collective-permute-done.1), kind=kLoop, calls=%fused_computation.1 | loop fusion | flops 1179648 | bytes 1769472 | tf_op jit(solution)/shard_map/convert_element_type | solution.py:172
  41.4 9.9 %all-to-all-done.came = bf16[16,120,384]{2,1,0:T(8,128)(2,1)S(1)} async-done(((bf16[16,120,384]{2,1,0:T(8,128)(2,1)}), bf16[16,120,384]{2,1,0:T(8,128)(2,1)S(1)}, u32[]{:S(2)}, u32[]{:S(2)}) %all-to-all-start) | async-done | bytes 1474592 | tf_op jit(solution)/shard_map/all_to_all | solution.py:158
  52.1 4.7 %collective-permute-start.3 = (bf16[784,384]{1,0:T(8,128)(2,1)S(1)}, bf16[784,384]{1,0:T(8,128)(2,1)S(1)}, u32[]{:S(2)}, u32[]{:S(2)}) collective-permute-start(bf16[784,384]{1,0:T(8,128)(2,1)S(1)} %shard_map.113.mine), channel_id=1, source_target_pairs={{0,256},{256,0},{1,257},{257,1},{2,258},{258,2},{3,259},{259,3},{4... | collective-permute-start | bytes 1806344 | tf_op jit(solution)/shard_map/ppermute | solution.py:182
  56.8 2.0 %add_convert_fusion = bf16[8,96,384]{2,1,0:T(8,128)(2,1)} fusion(bf16[8,96,384]{2,1,0:T(8,128)(2,1)} %collective-permute-done.6, bf16[8,96,384]{2,1,0:T(8,128)(2,1)S(1)} %copy-done.4), kind=kLoop, calls=%fused_computation.3 | loop fusion | flops 1179648 | bytes 1769472 | tf_op jit(solution)/shard_map/convert_element_type | solution.py:184
  58.8 4.2 %all-to-all-start.1 = ((bf16[8,96,384]{2,1,0:T(8,128)(2,1)}), bf16[8,96,384]{2,1,0:T(8,128)(2,1)}, u32[]{:S(2)}, u32[]{:S(2)}) async-start(bf16[8,96,384]{2,1,0:T(8,128)(2,1)} %add_convert_fusion), calls=%async_computation.1 | async-start | bytes 1179648 | tf_op jit(solution)/shard_map/all_to_all | solution.py:190
  63.0 2.1 %collective-permute-start.4 = (bf16[784,384]{1,0:T(8,128)(2,1)S(1)}, bf16[784,384]{1,0:T(8,128)(2,1)S(1)}, u32[]{:S(2)}, u32[]{:S(2)}) collective-permute-start(bf16[784,384]{1,0:T(8,128)(2,1)S(1)} %shard_map.113.mine), channel_id=1, source_target_pairs={{0,16},{16,0},{1,17},{17,1},{2,18},{18,2},{3,19},{19,3},{4,20},{20... | collective-permute-start | bytes 1806344 | tf_op jit(solution)/shard_map/ppermute | solution.py:185
  65.1 5.9 %collective-permute-done.3.mine_far = bf16[784,384]{1,0:T(8,128)(2,1)S(1)} collective-permute-done((bf16[784,384]{1,0:T(8,128)(2,1)S(1)}, bf16[784,384]{1,0:T(8,128)(2,1)S(1)}, u32[]{:S(2)}, u32[]{:S(2)}) %collective-permute-start.3) | collective-permute-done | bytes 602144 | tf_op jit(solution)/shard_map/ppermute | solution.py:182
  71.1 2.0 %collective-permute-start.5 = (bf16[784,384]{1,0:T(8,128)(2,1)S(1)}, bf16[784,384]{1,0:T(8,128)(2,1)}, u32[]{:S(2)}, u32[]{:S(2)}) collective-permute-start(bf16[784,384]{1,0:T(8,128)(2,1)S(1)} %collective-permute-done.3.mine_far), channel_id=1, source_target_pairs={{0,16},{16,0},{1,17},{17,1},{2,18},{18,2},{3,19},{19,3},{4,20},{20... | collective-permute-start | bytes 1806344 | tf_op jit(solution)/shard_map/ppermute | solution.py:186
  73.2 1.9 %collective-permute-done.5.far_core = bf16[784,384]{1,0:T(8,128)(2,1)} collective-permute-done((bf16[784,384]{1,0:T(8,128)(2,1)S(1)}, bf16[784,384]{1,0:T(8,128)(2,1)}, u32[]{:S(2)}, u32[]{:S(2)}) %collective-permute-start.5) | collective-permute-done | bytes 602144 | tf_op jit(solution)/shard_map/ppermute | solution.py:186
  75.1 4.5 %shard_map.114 = bf16[16,96,384]{2,1,0:T(8,128)(2,1)} custom-call(s32[4]{0:T(128)S(1)} %pad_add_fusion.place, bf16[784,384]{1,0:T(8,128)(2,1)S(1)} %shard_map.113.mine, bf16[784,384]{1,0:T(8,128)(2,1)S(1)} %collective-permute-done.3.mine_far, bf16[784,384]{1,0:T(8,128)(2,1)S(1)} %collective-permute-done.4.mine_core, ...), custom_call_target="tpu_custom_call" | custom-call | flops 1130000000 | bytes 4800000 | tf_op jit(solution)/shard_map/pallas_call | solution.py:129
  79.6 2.8 %all-to-all-done.1 = bf16[8,96,384]{2,1,0:T(8,128)(2,1)} async-done(((bf16[8,96,384]{2,1,0:T(8,128)(2,1)}), bf16[8,96,384]{2,1,0:T(8,128)(2,1)}, u32[]{:S(2)}, u32[]{:S(2)}) %all-to-all-start.1) | async-done | bytes 589856 | tf_op jit(solution)/shard_map/all_to_all | solution.py:190
  82.5 4.0 %all-to-all-start.2 = ((bf16[16,96,384]{2,1,0:T(8,128)(2,1)}), bf16[16,96,384]{2,1,0:T(8,128)(2,1)S(1)}, u32[]{:S(2)}, u32[]{:S(2)}) async-start(bf16[16,96,384]{2,1,0:T(8,128)(2,1)} %shard_map.114), calls=%async_computation.2 | async-start | bytes 2359296 | tf_op jit(solution)/shard_map/all_to_all | solution.py:198
  86.5 1.2 convert_reduce_fusion
  89.3 27.7 %all-to-all-done.2 = bf16[16,96,384]{2,1,0:T(8,128)(2,1)S(1)} async-done(((bf16[16,96,384]{2,1,0:T(8,128)(2,1)}), bf16[16,96,384]{2,1,0:T(8,128)(2,1)S(1)}, u32[]{:S(2)}, u32[]{:S(2)}) %all-to-all-start.2) | async-done | bytes 1179680 | tf_op jit(solution)/shard_map/all_to_all | solution.py:198
  (44 shorter events, 6.0 us)
Async XLA Ops:
  2.9 12.0 %copy-start.5 = (bf16[3072,96]{0,1:T(8,128)(2,1)S(1)}, bf16[3072,96]{0,1:T(8,128)(2,1)}, u32[]{:S(2)}) copy-start(bf16[3072,96]{0,1:T(8,128)(2,1)} %param.12) | copy-start | bytes 1769476
  2.9 48.4 %all-to-all-start = ((bf16[16,120,384]{2,1,0:T(8,128)(2,1)}), bf16[16,120,384]{2,1,0:T(8,128)(2,1)S(1)}, u32[]{:S(2)}, u32[]{:S(2)}) async-start(bf16[16,120,384]{2,1,0:T(8,128)(2,1)} %bitcast.7), calls=%async_computation | async-start | bytes 2949120 | tf_op jit(solution)/shard_map/all_to_all | solution.py:158
  14.8 5.0 %copy-start.3 = (bf16[512,768]{1,0:T(8,128)(2,1)S(1)}, bf16[512,768]{1,0:T(8,128)(2,1)}, u32[]{:S(2)}) copy-start(bf16[512,768]{1,0:T(8,128)(2,1)} %grad.1) | copy-start | bytes 2359300
  14.9 12.1 %collective-permute-start = (bf16[96,1536]{1,0:T(8,128)(2,1)S(1)}, bf16[96,1536]{1,0:T(8,128)(2,1)S(1)}, u32[]{:S(2)}, u32[]{:S(2)}) collective-permute-start(bf16[96,1536]{1,0:T(8,128)(2,1)S(1)} %get-tuple-element.34), channel_id=1, source_target_pairs={{0,256},{256,0},{1,257},{257,1},{2,258},{258,2},{3,259},{259,3},{4... | collective-permute-start | bytes 884744 | tf_op jit(solution)/shard_map/ppermute | solution.py:164
  19.8 1.9 %copy-start.2 = (bf16[512,3072]{1,0:T(8,128)(2,1)S(1)}, bf16[512,3072]{1,0:T(8,128)(2,1)}, u32[]{:S(2)}) copy-start(bf16[512,3072]{1,0:T(8,128)(2,1)} %act.1) | copy-start | bytes 9437188
  25.2 1.0 copy-start
  27.0 5.6 %collective-permute-start.1 = (bf16[2,8,96,384]{3,2,1,0:T(8,128)(2,1)}, bf16[2,8,96,384]{3,2,1,0:T(8,128)(2,1)}, u32[]{:S(2)}, u32[]{:S(2)}) collective-permute-start(bf16[2,8,96,384]{3,2,1,0:T(8,128)(2,1)} %get-tuple-element.19), channel_id=1, source_target_pairs={{0,16},{16,0},{1,17},{17,1},{2,18},{18,2},{3,19},{19,3},{4,20},{20... | collective-permute-start | bytes 3538952 | tf_op jit(solution)/shard_map/ppermute | solution.py:169
  29.8 2.8 %copy-start.1 = (bf16[2,8,96,384]{3,2,1,0:T(8,128)(2,1)S(1)}, bf16[2,8,96,384]{3,2,1,0:T(8,128)(2,1)}, u32[]{:S(2)}) copy-start(bf16[2,8,96,384]{3,2,1,0:T(8,128)(2,1)} %copy-done) | copy-start | bytes 3538948
  29.9 9.4 %copy-start.9 = (f32[96]{0:T(128)S(1)}, f32[96]{0:T(128)}, u32[]{:S(2)}) copy-start(f32[96]{0:T(128)} %param.13) | copy-start | bytes 1156
  29.9 11.5 %collective-permute-start.2 = (bf16[192,1536]{1,0:T(8,128)(2,1)S(1)}, bf16[192,1536]{1,0:T(8,128)(2,1)S(1)}, u32[]{:S(2)}, u32[]{:S(2)}) collective-permute-start(bf16[192,1536]{1,0:T(8,128)(2,1)S(1)} %bitcast.41), channel_id=1, source_target_pairs={{0,16},{16,0},{1,17},{17,1},{2,18},{18,2},{3,19},{19,3},{4,20},{20... | collective-permute-start | bytes 1769480 | tf_op jit(solution)/shard_map/ppermute | solution.py:177
  34.6 22.1 %collective-permute-start.6 = (bf16[8,96,384]{2,1,0:T(8,128)(2,1)}, bf16[8,96,384]{2,1,0:T(8,128)(2,1)}, u32[]{:S(2)}, u32[]{:S(2)}) collective-permute-start(bf16[8,96,384]{2,1,0:T(8,128)(2,1)} %fusion.1), channel_id=1, source_target_pairs={{0,256},{256,0},{1,257},{257,1},{2,258},{258,2},{3,259},{259,3},{4... | collective-permute-start | bytes 1769480 | tf_op jit(solution)/shard_map/ppermute | solution.py:173
  51.3 5.5 %copy-start.4 = (bf16[8,96,384]{2,1,0:T(8,128)(2,1)S(1)}, bf16[8,96,384]{2,1,0:T(8,128)(2,1)}, u32[]{:S(2)}) copy-start(bf16[8,96,384]{2,1,0:T(8,128)(2,1)} %fusion) | copy-start | bytes 1769476
  52.1 21.0 %copy-start.8 = (f32[1,768]{1,0:T(1,128)S(1)}, f32[1,768]{1,0:T(1,128)}, u32[]{:S(2)}) copy-start(f32[1,768]{1,0:T(1,128)} %param.15) | copy-start | bytes 9220
  52.1 19.0 %collective-permute-start.3 = (bf16[784,384]{1,0:T(8,128)(2,1)S(1)}, bf16[784,384]{1,0:T(8,128)(2,1)S(1)}, u32[]{:S(2)}, u32[]{:S(2)}) collective-permute-start(bf16[784,384]{1,0:T(8,128)(2,1)S(1)} %shard_map.113.mine), channel_id=1, source_target_pairs={{0,256},{256,0},{1,257},{257,1},{2,258},{258,2},{3,259},{259,3},{4... | collective-permute-start | bytes 1806344 | tf_op jit(solution)/shard_map/ppermute | solution.py:182
  58.8 23.6 %all-to-all-start.1 = ((bf16[8,96,384]{2,1,0:T(8,128)(2,1)}), bf16[8,96,384]{2,1,0:T(8,128)(2,1)}, u32[]{:S(2)}, u32[]{:S(2)}) async-start(bf16[8,96,384]{2,1,0:T(8,128)(2,1)} %add_convert_fusion), calls=%async_computation.1 | async-start | bytes 1179648 | tf_op jit(solution)/shard_map/all_to_all | solution.py:190
  63.0 10.1 %collective-permute-start.4 = (bf16[784,384]{1,0:T(8,128)(2,1)S(1)}, bf16[784,384]{1,0:T(8,128)(2,1)S(1)}, u32[]{:S(2)}, u32[]{:S(2)}) collective-permute-start(bf16[784,384]{1,0:T(8,128)(2,1)S(1)} %shard_map.113.mine), channel_id=1, source_target_pairs={{0,16},{16,0},{1,17},{17,1},{2,18},{18,2},{3,19},{19,3},{4,20},{20... | collective-permute-start | bytes 1806344 | tf_op jit(solution)/shard_map/ppermute | solution.py:185
  71.1 4.0 %collective-permute-start.5 = (bf16[784,384]{1,0:T(8,128)(2,1)S(1)}, bf16[784,384]{1,0:T(8,128)(2,1)}, u32[]{:S(2)}, u32[]{:S(2)}) collective-permute-start(bf16[784,384]{1,0:T(8,128)(2,1)S(1)} %collective-permute-done.3.mine_far), channel_id=1, source_target_pairs={{0,16},{16,0},{1,17},{17,1},{2,18},{18,2},{3,19},{19,3},{4,20},{20... | collective-permute-start | bytes 1806344 | tf_op jit(solution)/shard_map/ppermute | solution.py:186
  79.6 6.8 %copy-start.6 = (f32[192,96]{1,0:T(8,128)S(1)}, f32[192,96]{1,0:T(8,128)}, u32[]{:S(2)}) copy-start(f32[192,96]{1,0:T(8,128)} %param.16) | copy-start | bytes 221188
  82.5 34.6 %all-to-all-start.2 = ((bf16[16,96,384]{2,1,0:T(8,128)(2,1)}), bf16[16,96,384]{2,1,0:T(8,128)(2,1)S(1)}, u32[]{:S(2)}, u32[]{:S(2)}) async-start(bf16[16,96,384]{2,1,0:T(8,128)(2,1)} %shard_map.114), calls=%async_computation.2 | async-start | bytes 2359296 | tf_op jit(solution)/shard_map/all_to_all | solution.py:198
  86.4 2.2 %copy-start.7 = (f32[1,24,768]{2,1,0:T(8,128)S(1)}, f32[1,24,768]{2,1,0:T(8,128)}, u32[]{:S(2)}) copy-start(f32[1,24,768]{2,1,0:T(8,128)} %param.17) | copy-start | bytes 221188
